TPU v7x, 128 devices: a whole 4x4x4 slice. The times are simulated.
128 devices in a mesh: seq: 32 (over z, x, core), head: 4 (over y).
Axes of the slice: x: 4, y: 4, z: 4, core: 2. Of those that a mesh axis runs over, the one named last changes fastest.
Arguments:
- tokens: bfloat16 [8192, 2048], P('seq'), may hold values from -6 to 6
- order: int32 [8192], P('seq'), may hold values from 0 to 8191, as said below
- doc_lengths: int32 [8], replicated, may hold values from 1 to 2048, 8192 in all
- w_query: bfloat16 [2048, 2048], P(None, 'head'), may hold values from -0.125 to 0.125
- w_key: bfloat16 [2048, 2048], P(None, 'head'), may hold values from -0.125 to 0.125
- w_value: bfloat16 [2048, 4096], P(None, 'head'), may hold values from -0.125 to 0.125
- w_zgate: bfloat16 [2048, 4096], P(None, 'head'), may hold values from -0.125 to 0.125
- w_beta: bfloat16 [2048, 32], P(None, 'head'), may hold values from -0.125 to 0.125
- w_alpha: bfloat16 [2048, 32], P(None, 'head'), may hold values from -0.125 to 0.125
- conv_query: bfloat16 [4, 2048], P(None, 'head'), may hold values from -3 to 3
- conv_key: bfloat16 [4, 2048], P(None, 'head'), may hold values from -3 to 3
- conv_value: bfloat16 [4, 4096], P(None, 'head'), may hold values from -3 to 3
- decay_log: float32 [32], P('head'), may hold values from -8.5 to -3.2
- decay_bias: float32 [32], P('head'), may hold values from -2 to 1
- norm_gain: float32 [128], replicated, may hold values from 0.5 to 1.5
- w_out: bfloat16 [4096, 2048], P('head'), may hold values from -0.09375 to 0.09375
Outputs:
- mixed: bfloat16 [8192, 2048], P('seq', 'head')
Inputs may be any that keep to these rules, and one draw needn't show every extreme that they name: `order`: a permutation of the positions; each shard of 256 loader rows sends at most 16 rows to any one balanced shard, exactly 16 to some; every shard receives 256; the number sent from shard s to shard d depends only on (d - s) mod the shard count. `doc_lengths`: sum to 8192, one is exactly 2048.
All inputs are finite; a program needn't handle non-finite values.
Results may differ from a plain program's by a relative error of at most 0.017.
Values may be sent and summed in bfloat16 or wider, within the bound.
No kernel may reach another device: no remote copies, remote signals or barrier semaphores. Data moves between devices by JAX's collectives and lax.ppermute only.
A program may use at most 128 MiB of HBM per device.

v0:
```python
import jax
import jax.numpy as jnp
from jax import lax
from jax.sharding import PartitionSpec as P

HEAD_DIMENSION = 128
KERNEL = 4
BLOCK = 64


largest_found = lax.Precision.HIGHEST


def passed_along(value, axis, steps):
    count = lax.axis_size(axis)
    initial, last = (max(0, -steps), min(count, count - steps))
    return lax.ppermute(value, axis, [(source, source + steps) for source in range(initial, last)])


def segment_ids(positions, doc_lengths):
    doc_ends = jnp.cumsum(doc_lengths)
    return jnp.sum((positions[:, None] >= doc_ends[None, :]).astype(jnp.int32), axis=1)


def causal_conv(extended, ext_segment, weights, segment):
    count = segment.shape[0]
    total = jnp.zeros((count, extended.shape[1]), jnp.float32)
    for offset in range(KERNEL):
        rows = extended[offset : offset + count].astype(jnp.float32)
        inside = (ext_segment[offset : offset + count] == segment)[:, None]
        total = total + jnp.where(inside, rows, 0.0) * weights[offset].astype(jnp.float32)
    return jax.nn.silu(total)


def unit_rows(values, heads, factor):
    shaped = values.reshape(values.shape[0], heads, -1)
    return shaped * lax.rsqrt(jnp.sum(shaped * shaped, axis=-1, keepdims=True) + 1e-06) * factor


def local(
    tokens,
    order,
    doc_lengths,
    w_query,
    w_key,
    w_value,
    w_zgate,
    w_beta,
    w_alpha,
    conv_query,
    conv_key,
    conv_value,
    decay_log,
    decay_bias,
    norm_gain,
    w_out,
):
    rows_here, model_width = tokens.shape
    seq_count = lax.axis_size("seq")
    capacity = 2 * rows_here // seq_count
    target = order // rows_here
    landing = order % rows_here
    marks = (target[:, None] == jnp.arange(seq_count, dtype=jnp.int32)[None, :]).astype(jnp.int32)
    earlier = jnp.cumsum(marks, axis=0) - marks
    slot_index = jnp.sum(earlier * marks, axis=1)
    send_spots = (
        jnp.full((seq_count, capacity), rows_here, jnp.int32).at[target, slot_index].set(landing)
    )
    send_rows = (
        jnp.zeros((seq_count, capacity, model_width), tokens.dtype)
        .at[target, slot_index]
        .set(tokens)
    )
    got_rows, got_spots = (
        lax.all_to_all(send_rows, "seq", split_axis=0, concat_axis=0, tiled=True),
        lax.all_to_all(send_spots, "seq", split_axis=0, concat_axis=0, tiled=True),
    )
    balanced = (
        jnp.zeros_like(tokens)
        .at[got_spots.reshape(-1)]
        .set(got_rows.reshape(-1, model_width), mode="drop")
    )
    first = lax.axis_index("seq") * rows_here
    segment = segment_ids(first + jnp.arange(rows_here, dtype=jnp.int32), doc_lengths)
    ext_segment = segment_ids(
        first + jnp.arange(-(KERNEL - 1), rows_here, dtype=jnp.int32), doc_lengths
    )

    def project(weight):
        return jnp.dot(balanced, weight, preferred_element_type=jnp.float32).astype(jnp.bfloat16)

    query_proj = project(w_query)
    key_proj = project(w_key)
    value_proj = project(w_value)
    qk_width = query_proj.shape[1]
    tail_rows = rows_here - (KERNEL - 1)
    tail_block = jnp.concatenate(
        [query_proj[tail_rows:], key_proj[tail_rows:], value_proj[tail_rows:]], axis=1
    )
    tail_got = passed_along(tail_block, "seq", 1)

    def convolve(projected, tail, kernel):
        extended = jnp.concatenate([tail, projected], axis=0)
        return causal_conv(extended, ext_segment, kernel, segment)

    qk_heads = qk_width // HEAD_DIMENSION
    v_heads = value_proj.shape[1] // HEAD_DIMENSION
    repeat = v_heads // qk_heads
    query = unit_rows(
        convolve(query_proj, tail_got[:, :qk_width], conv_query), qk_heads, HEAD_DIMENSION ** (-0.5)
    )
    keys = unit_rows(
        convolve(key_proj, tail_got[:, qk_width : 2 * qk_width], conv_key), qk_heads, 1.0
    )
    values = convolve(value_proj, tail_got[:, 2 * qk_width :], conv_value).reshape(
        rows_here, v_heads, HEAD_DIMENSION
    )
    zgate = project(w_zgate).astype(jnp.float32).reshape(rows_here, v_heads, HEAD_DIMENSION)
    beta = jax.nn.sigmoid(jnp.dot(balanced, w_beta, preferred_element_type=jnp.float32))
    decay = -jnp.exp(decay_log) * jax.nn.softplus(
        jnp.dot(balanced, w_alpha, preferred_element_type=jnp.float32) + decay_bias
    )
    blocks = rows_here // BLOCK

    def by_block(array):
        return array.reshape(blocks, BLOCK, v_heads, -1).transpose(0, 2, 1, 3)

    query_blocks = by_block(jnp.repeat(query, repeat, axis=1))
    key_blocks = by_block(jnp.repeat(keys, repeat, axis=1))
    value_blocks = by_block(values)
    beta_blocks = beta.reshape(blocks, BLOCK, v_heads).transpose(0, 2, 1)
    decay_blocks = decay.reshape(blocks, BLOCK, v_heads).transpose(0, 2, 1)
    segment_blocks = segment.reshape(blocks, BLOCK)
    segment_before = segment_ids(
        first + jnp.arange(blocks, dtype=jnp.int32) * BLOCK - 1, doc_lengths
    )
    identity = jnp.eye(HEAD_DIMENSION, dtype=jnp.float32)
    block_eye = jnp.eye(BLOCK, dtype=jnp.float32)
    lower_incl = jnp.tril(jnp.ones((BLOCK, BLOCK), jnp.bool_))
    lower_strict = jnp.tril(jnp.ones((BLOCK, BLOCK), jnp.float32), -1)

    def step_block(carried_state, inputs):
        (
            query_block,
            key_block,
            value_block,
            beta_block,
            decay_block,
            segment_block,
            segment_prev,
        ) = inputs
        cumulative = jnp.cumsum(decay_block, axis=-1)
        inside = lower_incl & (segment_block[:, None] == segment_block[None, :])
        differences = cumulative[:, :, None] - cumulative[:, None, :]
        weights_incl = jnp.where(inside, jnp.exp(jnp.where(inside, differences, 0.0)), 0.0)
        weights_strict = weights_incl * lower_strict
        carried = jnp.exp(cumulative) * (segment_block == segment_prev).astype(jnp.float32)[None, :]
        key_inner = jnp.einsum("htd,hsd->hts", key_block, key_block, precision=largest_found)
        system = block_eye + beta_block[:, :, None] * weights_strict * key_inner
        right_side = beta_block[:, :, None] * jnp.concatenate(
            [value_block, carried[:, :, None] * key_block], axis=-1
        )
        solved = lax.linalg.triangular_solve(
            system, right_side, left_side=True, lower=True, unit_diagonal=True
        )
        starting_values = solved[..., :HEAD_DIMENSION]
        correction = solved[..., HEAD_DIMENSION:]
        last_weights = weights_incl[:, -1, :]
        scaled_key_rows = last_weights[:, :, None] * key_block
        mixing = weights_incl * jnp.einsum(
            "htd,hsd->hts", query_block, key_block, precision=largest_found
        )
        base_out = jnp.einsum("hts,hsv->htv", mixing, starting_values, precision=largest_found)
        layer_response = carried[:, :, None] * query_block - jnp.einsum(
            "hts,hsd->htd", mixing, correction, precision=largest_found
        )
        transition = carried[:, -1][:, None, None] * identity - jnp.einsum(
            "hsk,hsj->hkj", scaled_key_rows, correction, precision=largest_found
        )
        forwarded_state = jnp.einsum(
            "gin,gif->gnf", scaled_key_rows, starting_values, precision=largest_found
        )
        prior_out = base_out + jnp.einsum(
            "aou,aum->aom",
            layer_response,
            carried_state[..., HEAD_DIMENSION:],
            precision=largest_found,
        )
        state_weight = jnp.einsum(
            "htk,hkj->htj",
            layer_response,
            carried_state[..., :HEAD_DIMENSION],
            precision=largest_found,
        )
        advanced = jnp.einsum("hkj,hjw->hkw", transition, carried_state, precision=largest_found)
        advanced = advanced + jnp.concatenate(
            [jnp.zeros_like(forwarded_state), forwarded_state], axis=-1
        )
        return (advanced, (prior_out, state_weight))

    start = jnp.concatenate(
        [
            jnp.broadcast_to(identity, (v_heads, HEAD_DIMENSION, HEAD_DIMENSION)),
            jnp.zeros((v_heads, HEAD_DIMENSION, HEAD_DIMENSION), jnp.float32),
        ],
        axis=-1,
    )
    carry_end, (prior_blocks, blockwise_weights) = lax.scan(
        step_block,
        start,
        (
            query_blocks,
            key_blocks,
            value_blocks,
            beta_blocks,
            decay_blocks,
            segment_blocks,
            segment_before,
        ),
    )
    every_transition = carry_end[..., :HEAD_DIMENSION]
    every_shift = carry_end[..., HEAD_DIMENSION:]

    def relay(turn, arriving_state):
        departing_state = (
            jnp.einsum("cfm,cmp->cfp", every_transition, arriving_state, precision=largest_found)
            + every_shift
        )
        return passed_along(departing_state.astype(jnp.bfloat16), "seq", 1).astype(
            departing_state.dtype
        )

    entering_state = lax.fori_loop(0, seq_count - 1, relay, jnp.zeros_like(every_shift))
    attended_blocks = prior_blocks + jnp.einsum(
        "yblz,bzd->ybld", blockwise_weights, entering_state, precision=largest_found
    )
    attended = attended_blocks.transpose(0, 2, 1, 3).reshape(rows_here, v_heads, HEAD_DIMENSION)
    normed = (
        attended
        * lax.rsqrt(jnp.mean(attended * attended, axis=-1, keepdims=True) + 1e-06)
        * norm_gain
        * jax.nn.silu(zgate)
    )
    gated = normed.astype(jnp.bfloat16).reshape(rows_here, v_heads * HEAD_DIMENSION)
    term = jnp.dot(gated, w_out, preferred_element_type=jnp.float32)
    return lax.psum_scatter(term.astype(jnp.bfloat16), "head", scatter_dimension=1, tiled=True)


def solution(mesh):
    return jax.shard_map(
        local,
        mesh=mesh,
        in_specs=(
            P("seq", None),
            P("seq"),
            P(),
            P(None, "head"),
            P(None, "head"),
            P(None, "head"),
            P(None, "head"),
            P(None, "head"),
            P(None, "head"),
            P(None, "head"),
            P(None, "head"),
            P(None, "head"),
            P("head"),
            P("head"),
            P(),
            P("head", None),
        ),
        out_specs=P("seq", "head"),
        check_vma=False,
    )
```

profile of v0, /device:TPU:1, one launch (start us, length us, event | category | flops | bytes accessed | tf_op | source)
XLA Modules:
  0.0 806.8 jit_solution(2125791875476773774)
XLA Ops:
  8.4 12.8 %scatter_fusion = s32[32,16]{0,1:T(8,128)S(1)} fusion(s32[32,16]{0,1:T(8,128)S(1)} %broadcast_in_dim.180, s32[256]{0:T(256)S(1)} %bitcast.212, s32[256]{0:T(256)S(1)} %get-tuple-element.251), kind=kCustom, calls=%fused_computation | custom fusion | bytes 5120 | tf_op jit(solution)/shard_map/scatter | solution.py:67
  21.8 9.4 %all-to-all-start = ((s32[32,1,16]{2,1,0:T(1,128)}), s32[32,1,16]{2,1,0:T(1,128)S(1)}, u32[]{:S(2)}, u32[]{:S(2)}) async-start(s32[32,1,16]{2,1,0:T(1,128)} %copy.53), calls=%async_computation | async-start | bytes 32768 | tf_op jit(solution)/shard_map/all_to_all | solution.py:76
  33.1 44.5 %scatter_fusion.1 = bf16[32,16,2048]{2,1,0:T(8,128)(2,1)} fusion(bf16[32,16,2048]{2,1,0:T(8,128)(2,1)} %broadcast_in_dim.182, s32[256]{0:T(256)S(1)} %bitcast.213, bf16[256,2048]{1,0:T(8,128)(2,1)S(1)} %copy-done.6), kind=kCustom, calls=%fused_computation.1 | custom fusion | bytes 3147776 | tf_op jit(solution)/shard_map/scatter | solution.py:72
  77.6 7.4 all-to-all-start.1
  89.4 23.5 %all-to-all-done.1 = bf16[32,16,2048]{2,1,0:T(8,128)(2,1)} async-done(((bf16[32,16,2048]{2,1,0:T(8,128)(2,1)}), bf16[32,16,2048]{2,1,0:T(8,128)(2,1)}, u32[]{:S(2)}, u32[]{:S(2)}) %all-to-all-start.1) | async-done | bytes 2097184 | tf_op jit(solution)/shard_map/all_to_all | solution.py:75
  150.2 218.7 %while.26 = (s32[]{:T(128)}, f32[8,128,256]{2,1,0:T(8,128)S(1)}, f32[4,8,64,128]{3,2,0,1:T(8,128)}, f32[4,8,64,128]{3,2,0,1:T(8,128)}, f32[4,8,64]{2,1,0:T(8,128...) while((s32[]{:T(128)}, f32[8,128,256]{2,1,0:T(8,128)S(1)}, ...), condition=%wide.region_14.15_spmd.clone, body=%wide.region_12.14_spmd.clone.sunk | while | flops 1109106944 | bytes 23711280 | solution.py:208
  152.9 40.0 %custom-call.12 = f32[8,1,64,64]{2,3,1,0:T(8,128)S(1)} custom-call(f32[8,1,64,64]{3,2,1,0:T(8,128)} %fusion.159), custom_call_target="InvertDiagBlocksLowerTriangular" | custom-call | tf_op jit(solution)/shard_map/while/body/eval_jaxpr/triangular_solve | solution.py:163
  207.6 40.0 %custom-call.12 = f32[8,1,64,64]{2,3,1,0:T(8,128)S(1)} custom-call(f32[8,1,64,64]{3,2,1,0:T(8,128)} %fusion.159), custom_call_target="InvertDiagBlocksLowerTriangular" | custom-call | tf_op jit(solution)/shard_map/while/body/eval_jaxpr/triangular_solve | solution.py:163
  262.3 40.0 %custom-call.12 = f32[8,1,64,64]{2,3,1,0:T(8,128)S(1)} custom-call(f32[8,1,64,64]{3,2,1,0:T(8,128)} %fusion.159), custom_call_target="InvertDiagBlocksLowerTriangular" | custom-call | tf_op jit(solution)/shard_map/while/body/eval_jaxpr/triangular_solve | solution.py:163
  317.0 40.0 %custom-call.12 = f32[8,1,64,64]{2,3,1,0:T(8,128)S(1)} custom-call(f32[8,1,64,64]{3,2,1,0:T(8,128)} %fusion.159), custom_call_target="InvertDiagBlocksLowerTriangular" | custom-call | tf_op jit(solution)/shard_map/while/body/eval_jaxpr/triangular_solve | solution.py:163
  370.0 359.5 %while.27 = (s32[]{:T(128)}, f32[8,128,128]{2,1,0:T(8,128)}, f32[8,128,128]{2,1,0:T(8,128)}, f32[8,128,128]{2,1,0:T(8,128)}, s32[]{:T(128)}, /*index=5*/s32[]{:T(128)}) while((s32[]{:T(128)}, f32[8,128,128]{2,1,0:T(8,128)}, f32[8,128,128]{2,1,0:T(8,128)}, f32[8,128,128]{2,1,0:T(8,128)}, s32[]{:T(128)}, ...), condition=%wide.region_16.17_spmd.clone, body=%wide.region_15.16_spmd.clone.sunk | while | flops 201850880 | bytes 3670135 | solution.py:233
  529.0 6.5 collective-permute-start
  554.3 6.5 collective-permute-start
  566.9 6.5 collective-permute-start
  579.6 6.5 collective-permute-start
  604.9 6.5 collective-permute-start
  617.6 6.5 collective-permute-start
  642.9 6.5 collective-permute-start
  655.5 6.5 collective-permute-start
  680.8 6.5 collective-permute-start
  693.5 6.5 collective-permute-start
  718.8 6.5 collective-permute-start
  737.6 7.7 convolution_convert_fusion
  745.3 54.6 %reduce-scatter.2.cloned.1.call-done = bf16[256,512]{1,0:T(8,128)(2,1)} async-done(((bf16[256,2048]{1,0:T(8,128)(2,1)}), bf16[256,512]{1,0:T(8,128)(2,1)}) %reduce-scatter.2.cloned.1.call-update) | async-done | bytes 262160 | tf_op jit(solution)/shard_map/reduce_scatter | solution.py:246
  (360 shorter events, 400.1 us)
Async XLA Ops:
  21.8 55.8 %all-to-all-start = ((s32[32,1,16]{2,1,0:T(1,128)}), s32[32,1,16]{2,1,0:T(1,128)S(1)}, u32[]{:S(2)}, u32[]{:S(2)}) async-start(s32[32,1,16]{2,1,0:T(1,128)} %copy.53), calls=%async_computation | async-start | bytes 32768 | tf_op jit(solution)/shard_map/all_to_all | solution.py:76
  77.6 35.2 %all-to-all-start.1 = ((bf16[32,16,2048]{2,1,0:T(8,128)(2,1)}), bf16[32,16,2048]{2,1,0:T(8,128)(2,1)}, u32[]{:S(2)}, u32[]{:S(2)}) async-start(bf16[32,16,2048]{2,1,0:T(8,128)(2,1)} %scatter_fusion.1), calls=%async_computation.1 | async-start | bytes 4194304 | tf_op jit(solution)/shard_map/all_to_all | solution.py:75
  85.0 714.9 %reduce-scatter.2.cloned.1.call-start = ((), (), s32[]{:S(2)}) async-start(), calls=%async_computation.3 | async-start | bytes 1310720 | tf_op jit(solution)/shard_map/reduce_scatter | solution.py:246
  380.6 7.7 collective-permute-start
  391.1 7.7 collective-permute-start
  443.9 7.7 collective-permute-start
  496.6 7.7 collective-permute-start
  517.7 8.4 %collective-permute-start = (bf16[8,128,128]{2,1,0:T(8,128)(2,1)S(1)}, bf16[8,128,128]{2,1,0:T(8,128)(2,1)S(1)}, u32[]{:S(2)}, u32[]{:S(2)}) collective-permute-start(bf16[8,128,128]{2,1,0:T(8,128)(2,1)S(1)} %fusion.167), channel_id=1, source_target_pairs={{0,4},{4,8},{8,12},{12,16},{16,20},{20,24},{24,28},{28,32},{32,36}... | collective-permute-start | bytes 786440 | tf_op jit(solution)/shard_map/while/body/eval_jaxpr/ppermute | solution.py:17
  529.0 9.8 %collective-permute-start = (bf16[8,128,128]{2,1,0:T(8,128)(2,1)S(1)}, bf16[8,128,128]{2,1,0:T(8,128)(2,1)S(1)}, u32[]{:S(2)}, u32[]{:S(2)}) collective-permute-start(bf16[8,128,128]{2,1,0:T(8,128)(2,1)S(1)} %fusion.167), channel_id=1, source_target_pairs={{0,4},{4,8},{8,12},{12,16},{16,20},{20,24},{24,28},{28,32},{32,36}... | collective-permute-start | bytes 786440 | tf_op jit(solution)/shard_map/while/body/eval_jaxpr/ppermute | solution.py:17
  541.6 9.8 %collective-permute-start = (bf16[8,128,128]{2,1,0:T(8,128)(2,1)S(1)}, bf16[8,128,128]{2,1,0:T(8,128)(2,1)S(1)}, u32[]{:S(2)}, u32[]{:S(2)}) collective-permute-start(bf16[8,128,128]{2,1,0:T(8,128)(2,1)S(1)} %fusion.167), channel_id=1, source_target_pairs={{0,4},{4,8},{8,12},{12,16},{16,20},{20,24},{24,28},{28,32},{32,36}... | collective-permute-start | bytes 786440 | tf_op jit(solution)/shard_map/while/body/eval_jaxpr/ppermute | solution.py:17
  554.3 9.8 %collective-permute-start = (bf16[8,128,128]{2,1,0:T(8,128)(2,1)S(1)}, bf16[8,128,128]{2,1,0:T(8,128)(2,1)S(1)}, u32[]{:S(2)}, u32[]{:S(2)}) collective-permute-start(bf16[8,128,128]{2,1,0:T(8,128)(2,1)S(1)} %fusion.167), channel_id=1, source_target_pairs={{0,4},{4,8},{8,12},{12,16},{16,20},{20,24},{24,28},{28,32},{32,36}... | collective-permute-start | bytes 786440 | tf_op jit(solution)/shard_map/while/body/eval_jaxpr/ppermute | solution.py:17
  566.9 9.8 %collective-permute-start = (bf16[8,128,128]{2,1,0:T(8,128)(2,1)S(1)}, bf16[8,128,128]{2,1,0:T(8,128)(2,1)S(1)}, u32[]{:S(2)}, u32[]{:S(2)}) collective-permute-start(bf16[8,128,128]{2,1,0:T(8,128)(2,1)S(1)} %fusion.167), channel_id=1, source_target_pairs={{0,4},{4,8},{8,12},{12,16},{16,20},{20,24},{24,28},{28,32},{32,36}... | collective-permute-start | bytes 786440 | tf_op jit(solution)/shard_map/while/body/eval_jaxpr/ppermute | solution.py:17
  579.6 9.8 %collective-permute-start = (bf16[8,128,128]{2,1,0:T(8,128)(2,1)S(1)}, bf16[8,128,128]{2,1,0:T(8,128)(2,1)S(1)}, u32[]{:S(2)}, u32[]{:S(2)}) collective-permute-start(bf16[8,128,128]{2,1,0:T(8,128)(2,1)S(1)} %fusion.167), channel_id=1, source_target_pairs={{0,4},{4,8},{8,12},{12,16},{16,20},{20,24},{24,28},{28,32},{32,36}... | collective-permute-start | bytes 786440 | tf_op jit(solution)/shard_map/while/body/eval_jaxpr/ppermute | solution.py:17
  592.2 9.8 %collective-permute-start = (bf16[8,128,128]{2,1,0:T(8,128)(2,1)S(1)}, bf16[8,128,128]{2,1,0:T(8,128)(2,1)S(1)}, u32[]{:S(2)}, u32[]{:S(2)}) collective-permute-start(bf16[8,128,128]{2,1,0:T(8,128)(2,1)S(1)} %fusion.167), channel_id=1, source_target_pairs={{0,4},{4,8},{8,12},{12,16},{16,20},{20,24},{24,28},{28,32},{32,36}... | collective-permute-start | bytes 786440 | tf_op jit(solution)/shard_map/while/body/eval_jaxpr/ppermute | solution.py:17
  604.9 9.8 %collective-permute-start = (bf16[8,128,128]{2,1,0:T(8,128)(2,1)S(1)}, bf16[8,128,128]{2,1,0:T(8,128)(2,1)S(1)}, u32[]{:S(2)}, u32[]{:S(2)}) collective-permute-start(bf16[8,128,128]{2,1,0:T(8,128)(2,1)S(1)} %fusion.167), channel_id=1, source_target_pairs={{0,4},{4,8},{8,12},{12,16},{16,20},{20,24},{24,28},{28,32},{32,36}... | collective-permute-start | bytes 786440 | tf_op jit(solution)/shard_map/while/body/eval_jaxpr/ppermute | solution.py:17
  617.6 9.8 %collective-permute-start = (bf16[8,128,128]{2,1,0:T(8,128)(2,1)S(1)}, bf16[8,128,128]{2,1,0:T(8,128)(2,1)S(1)}, u32[]{:S(2)}, u32[]{:S(2)}) collective-permute-start(bf16[8,128,128]{2,1,0:T(8,128)(2,1)S(1)} %fusion.167), channel_id=1, source_target_pairs={{0,4},{4,8},{8,12},{12,16},{16,20},{20,24},{24,28},{28,32},{32,36}... | collective-permute-start | bytes 786440 | tf_op jit(solution)/shard_map/while/body/eval_jaxpr/ppermute | solution.py:17
  630.2 9.8 %collective-permute-start = (bf16[8,128,128]{2,1,0:T(8,128)(2,1)S(1)}, bf16[8,128,128]{2,1,0:T(8,128)(2,1)S(1)}, u32[]{:S(2)}, u32[]{:S(2)}) collective-permute-start(bf16[8,128,128]{2,1,0:T(8,128)(2,1)S(1)} %fusion.167), channel_id=1, source_target_pairs={{0,4},{4,8},{8,12},{12,16},{16,20},{20,24},{24,28},{28,32},{32,36}... | collective-permute-start | bytes 786440 | tf_op jit(solution)/shard_map/while/body/eval_jaxpr/ppermute | solution.py:17
  642.9 9.8 %collective-permute-start = (bf16[8,128,128]{2,1,0:T(8,128)(2,1)S(1)}, bf16[8,128,128]{2,1,0:T(8,128)(2,1)S(1)}, u32[]{:S(2)}, u32[]{:S(2)}) collective-permute-start(bf16[8,128,128]{2,1,0:T(8,128)(2,1)S(1)} %fusion.167), channel_id=1, source_target_pairs={{0,4},{4,8},{8,12},{12,16},{16,20},{20,24},{24,28},{28,32},{32,36}... | collective-permute-start | bytes 786440 | tf_op jit(solution)/shard_map/while/body/eval_jaxpr/ppermute | solution.py:17
  655.5 9.8 %collective-permute-start = (bf16[8,128,128]{2,1,0:T(8,128)(2,1)S(1)}, bf16[8,128,128]{2,1,0:T(8,128)(2,1)S(1)}, u32[]{:S(2)}, u32[]{:S(2)}) collective-permute-start(bf16[8,128,128]{2,1,0:T(8,128)(2,1)S(1)} %fusion.167), channel_id=1, source_target_pairs={{0,4},{4,8},{8,12},{12,16},{16,20},{20,24},{24,28},{28,32},{32,36}... | collective-permute-start | bytes 786440 | tf_op jit(solution)/shard_map/while/body/eval_jaxpr/ppermute | solution.py:17
  668.2 9.8 %collective-permute-start = (bf16[8,128,128]{2,1,0:T(8,128)(2,1)S(1)}, bf16[8,128,128]{2,1,0:T(8,128)(2,1)S(1)}, u32[]{:S(2)}, u32[]{:S(2)}) collective-permute-start(bf16[8,128,128]{2,1,0:T(8,128)(2,1)S(1)} %fusion.167), channel_id=1, source_target_pairs={{0,4},{4,8},{8,12},{12,16},{16,20},{20,24},{24,28},{28,32},{32,36}... | collective-permute-start | bytes 786440 | tf_op jit(solution)/shard_map/while/body/eval_jaxpr/ppermute | solution.py:17
  680.8 9.8 %collective-permute-start = (bf16[8,128,128]{2,1,0:T(8,128)(2,1)S(1)}, bf16[8,128,128]{2,1,0:T(8,128)(2,1)S(1)}, u32[]{:S(2)}, u32[]{:S(2)}) collective-permute-start(bf16[8,128,128]{2,1,0:T(8,128)(2,1)S(1)} %fusion.167), channel_id=1, source_target_pairs={{0,4},{4,8},{8,12},{12,16},{16,20},{20,24},{24,28},{28,32},{32,36}... | collective-permute-start | bytes 786440 | tf_op jit(solution)/shard_map/while/body/eval_jaxpr/ppermute | solution.py:17
  693.5 9.8 %collective-permute-start = (bf16[8,128,128]{2,1,0:T(8,128)(2,1)S(1)}, bf16[8,128,128]{2,1,0:T(8,128)(2,1)S(1)}, u32[]{:S(2)}, u32[]{:S(2)}) collective-permute-start(bf16[8,128,128]{2,1,0:T(8,128)(2,1)S(1)} %fusion.167), channel_id=1, source_target_pairs={{0,4},{4,8},{8,12},{12,16},{16,20},{20,24},{24,28},{28,32},{32,36}... | collective-permute-start | bytes 786440 | tf_op jit(solution)/shard_map/while/body/eval_jaxpr/ppermute | solution.py:17
  706.1 9.8 %collective-permute-start = (bf16[8,128,128]{2,1,0:T(8,128)(2,1)S(1)}, bf16[8,128,128]{2,1,0:T(8,128)(2,1)S(1)}, u32[]{:S(2)}, u32[]{:S(2)}) collective-permute-start(bf16[8,128,128]{2,1,0:T(8,128)(2,1)S(1)} %fusion.167), channel_id=1, source_target_pairs={{0,4},{4,8},{8,12},{12,16},{16,20},{20,24},{24,28},{28,32},{32,36}... | collective-permute-start | bytes 786440 | tf_op jit(solution)/shard_map/while/body/eval_jaxpr/ppermute | solution.py:17
  718.8 9.8 %collective-permute-start = (bf16[8,128,128]{2,1,0:T(8,128)(2,1)S(1)}, bf16[8,128,128]{2,1,0:T(8,128)(2,1)S(1)}, u32[]{:S(2)}, u32[]{:S(2)}) collective-permute-start(bf16[8,128,128]{2,1,0:T(8,128)(2,1)S(1)} %fusion.167), channel_id=1, source_target_pairs={{0,4},{4,8},{8,12},{12,16},{16,20},{20,24},{24,28},{28,32},{32,36}... | collective-permute-start | bytes 786440 | tf_op jit(solution)/shard_map/while/body/eval_jaxpr/ppermute | solution.py:17
  (41 other events, 336.1 us)
Sparse Core Ops, SparseCore 0:
  745.5 54.4 reduce-scatter.1
where the time goes:
time: 812 us; the launch traced here: 807 us
  other arithmetic  211 us (26%)
  starting transfers between devices  189 us (23%)
  waiting for transfers between devices  180 us (22%)
  matrix products  121 us (15%)
  local copies, waits for them, and re-layouts  89.1 us (11%)
  between operations  14 us (2%)
    ppermute x32, starting transfers between devices, passed_along(): lax.ppermute(value, axis, [(source, source + steps) for source in range(i...  173 us
    another operation x12, other arithmetic, step_block(): lax.linalg.triangular_solve(system, right_side, left_side=True, lower=Tru...  161 us
    ppermute x32, waiting for transfers between devices, passed_along(): lax.ppermute(value, axis, [(source, source + steps) for source in range(i...  102 us
    dot_general x31, matrix products, relay(): jnp.einsum('cfm,cmp->cfp', every_transition, arriving_state, precision=la...  61.8 us
    reduce_scatter x1, waiting for transfers between devices, local(): lax.psum_scatter(term.astype(jnp.bfloat16), 'head', scatter_dimension=1,...  54.6 us
    scatter x1, local copies, waits for them, and re-layouts, local(): send_rows = jnp.zeros((seq_count, capacity, model_width), tokens.dtype).a...  44.5 us
    convert_element_type x31, other arithmetic, relay(): passed_along(departing_state.astype(jnp.bfloat16), 'seq', 1)  26.2 us
    all_to_all x1, waiting for transfers between devices, local(): lax.all_to_all(send_rows, 'seq', split_axis=0, concat_axis=0, tiled=True)  23.5 us
  transfers between devices with their start and end apart: 35, of which 33 were waited for; matrix products, arithmetic and copies ran while one was open for 7% of the time, Pallas kernels for 0%

commit v1 on v0

v1 whole, which is shorter than its diff:
```python
import jax
import jax.numpy as jnp
from jax import lax
from jax.experimental import pallas as pl
from jax.experimental.pallas import tpu as pltpu
from jax.sharding import PartitionSpec as P

HEAD = 128
KERNEL = 4
TAIL = 16
LANES = 128
VMEM = pl.BlockSpec(memory_space=pltpu.VMEM)
SMEM = pl.BlockSpec(memory_space=pltpu.SMEM)
ANY = pl.BlockSpec(memory_space=pl.ANY)
F32 = jnp.float32
BF16 = jnp.bfloat16
HIGHEST = lax.Precision.HIGHEST


def iota(shape, axis):
    return lax.broadcasted_iota(jnp.int32, shape, axis)


def dot(left, right, contract=((1,), (0,)), precision=None):
    return lax.dot_general(
        left, right, (contract, ((), ())), precision=precision, preferred_element_type=F32
    )


def params(mib):
    return pltpu.CompilerParams(vmem_limit_bytes=mib << 20)


def pack_kernel(shards, order_ref, tokens_ref, send_ref):
    rows, width = tokens_ref.shape
    slots = send_ref.shape[0]
    capacity = slots // shards
    order = order_ref[...]
    bits = rows.bit_length() - 1
    target = lax.shift_right_logical(order, jnp.full_like(order, bits))
    landing = lax.bitwise_and(order, jnp.full_like(order, rows - 1))
    marks = (iota((shards, rows), 0) == target).astype(F32)
    before = (iota((rows, rows), 0) < iota((rows, rows), 1)).astype(F32).astype(BF16)
    earlier = dot(marks.astype(BF16), before)
    slot = jnp.sum(earlier * marks, axis=0, keepdims=True).astype(jnp.int32)
    hit = (iota((slots, rows), 0) == target * capacity + slot).astype(F32)
    send_ref[:, :width] = dot(hit.astype(BF16), tokens_ref[...]).astype(BF16)
    spot = jnp.sum(hit * (landing + 1).astype(F32), axis=1, keepdims=True)
    send_ref[:, width:] = jnp.broadcast_to(spot, (slots, LANES)).astype(BF16)


def softplus(x):
    return jnp.maximum(x, 0.0) + jnp.log1p(jnp.exp(-jnp.abs(x)))


def project_kernel(
    got_ref,
    w_query,
    w_key,
    w_value,
    w_zgate,
    w_beta,
    w_alpha,
    decay_log,
    decay_bias,
    query_ref,
    key_ref,
    value_ref,
    zgate_ref,
    tail_ref,
    beta_ref,
    decay_ref,
    balanced_ref,
    query_buf,
    key_buf,
    value_buf,
    zgate_buf,
    sems,
):
    width, rows = balanced_ref.shape[1], balanced_ref.shape[0]
    slots = got_ref.shape[0]
    pairs = ((w_query, query_buf), (w_key, key_buf), (w_value, value_buf), (w_zgate, zgate_buf))
    copies = [pltpu.make_async_copy(w, buf, sems.at[i]) for i, (w, buf) in enumerate(pairs)]
    for copy in copies:
        copy.start()
    spot = got_ref[:, width : width + 1].astype(F32).astype(jnp.int32)
    hit = (spot == iota((slots, rows), 1) + 1).astype(F32)
    balanced_ref[...] = dot(hit.T.astype(BF16), got_ref[:, :width]).astype(BF16)
    balanced = balanced_ref[...]
    beta_ref[...] = jax.nn.sigmoid(dot(balanced, w_beta[...]))
    decay_ref[...] = -jnp.exp(decay_log[...]) * softplus(
        dot(balanced, w_alpha[...]) + decay_bias[...]
    )
    column = 0
    for copy, buf, out in zip(
        copies,
        (query_buf, key_buf, value_buf, zgate_buf),
        (query_ref, key_ref, value_ref, zgate_ref),
    ):
        copy.wait()
        count = out.shape[1]
        for start in range(0, count, 512):
            part = dot(balanced, buf[:, start : start + 512]).astype(BF16)
            out[:, start : start + 512] = part
            if out is not zgate_ref:
                tail_ref[:, column : column + 512] = part[rows - TAIL :]
                column += 512


def silu(x):
    return x / (1.0 + jnp.exp(-x))


def chunk_kernel(
    where_ref,
    lengths_ref,
    query_ref,
    key_ref,
    value_ref,
    tail_ref,
    taps_query,
    taps_key,
    taps_value,
    beta_ref,
    decay_ref,
    mine_ref,
    send_ref,
    base_ref,
    response_ref,
    system_ref,
    inverse_ref,
    queries,
    keys,
    values,
    mixing_ref,
    mask_ref,
):
    rows = query_ref.shape[0]
    first, core = where_ref[0], where_ref[1]
    heads = beta_ref.shape[1]
    key_heads = query_ref.shape[1] // HEAD

    ends, total = [], jnp.int32(0)
    for i in range(lengths_ref.shape[0]):
        total = total + lengths_ref[i]
        ends.append(total)

    def segments(position):
        count = jnp.zeros(position.shape, jnp.int32)
        for end in ends:
            count = count + (position >= end).astype(jnp.int32)
        return count

    position = first + iota((rows, 1), 0)
    segment = segments(position)
    segment_row = segments(first + iota((1, rows), 1))
    segment_before = segments(jnp.full((1, 1), first - 1, jnp.int32))
    same = [(segments(position - lag) == segment).astype(F32) for lag in range(KERNEL)]

    def convolve(projected, tail, taps):
        extended = jnp.concatenate([tail.astype(F32), projected.astype(F32)], axis=0)
        sums = None
        for lag in range(KERNEL):
            shifted = extended if lag == 0 else pltpu.roll(extended, lag, 0)
            tap = taps[KERNEL - 1 - lag : KERNEL - lag, :].astype(F32)
            term = shifted[TAIL:] * tap * same[lag]
            sums = term if sums is None else sums + term
        return silu(sums)

    def unit(x, factor):
        return x * (lax.rsqrt(jnp.sum(x * x, axis=-1, keepdims=True) + 1e-06) * factor)

    width = query_ref.shape[1]
    for h in range(key_heads):
        at = slice(h * HEAD, (h + 1) * HEAD)
        to = slice(width + h * HEAD, width + (h + 1) * HEAD)
        queries[h] = unit(
            convolve(query_ref[:, at], tail_ref[:, at], taps_query[:, at]), HEAD**-0.5
        ).astype(BF16)
        keys[h] = unit(convolve(key_ref[:, at], tail_ref[:, to], taps_key[:, at]), 1.0).astype(
            BF16
        )
    for h in range(heads):
        at = slice(h * HEAD, (h + 1) * HEAD)
        to = slice(2 * width + h * HEAD, 2 * width + (h + 1) * HEAD)
        values[h] = convolve(value_ref[:, at], tail_ref[:, to], taps_value[:, at]).astype(BF16)

    row, column = iota((rows, rows), 0), iota((rows, rows), 1)
    lower = (row >= column).astype(F32)
    cumulative = dot(lower, decay_ref[...], precision=HIGHEST)
    padded = jnp.concatenate([cumulative, jnp.zeros((rows, LANES - heads), F32)], axis=1)
    cumulative_row = padded.T
    inside = (row >= column) & (segment == segment_row)
    strict = (row > column).astype(F32)
    carries = (segment == segment_before).astype(F32)
    levels = []
    size = 1
    while size < rows:
        levels.append(size)
        block = lax.bitwise_and(
            (lax.bitwise_xor(row, column) < 2 * size).astype(jnp.int32),
            lax.bitwise_and(
                (lax.bitwise_and(row, size) != 0).astype(jnp.int32),
                (lax.bitwise_and(column, size) == 0).astype(jnp.int32),
            ),
        )
        mask_ref[len(levels) - 1] = block.astype(F32).astype(BF16)
        size *= 2
    unit_matrix = (row == column).astype(F32)

    for kh in range(key_heads):
        inner = dot(keys[kh], keys[kh], ((1,), (1,)))
        cross = dot(queries[kh], keys[kh], ((1,), (1,)))
        for h in range(kh * heads // key_heads, (kh + 1) * heads // key_heads):
            difference = cumulative[:, h : h + 1] - cumulative_row[h : h + 1, :]
            weights = jnp.where(inside, jnp.exp(jnp.where(inside, difference, 0.0)), 0.0)
            system = beta_ref[:, h : h + 1] * weights * inner * strict
            system_ref[h] = system.astype(BF16)
            mixing_ref[h] = (weights * cross).astype(BF16)
            inverse_ref[h] = (unit_matrix - system * mask_ref[0].astype(F32)).astype(BF16)
    for level in range(1, len(levels)):
        for h in range(heads):
            inverse = inverse_ref[h]
            part = dot(system_ref[h] * mask_ref[level], inverse).astype(BF16)
            inverse_ref[h] = (inverse.astype(F32) - dot(inverse, part)).astype(BF16)

    square = (iota((HEAD, HEAD), 0) == iota((HEAD, HEAD), 1)).astype(F32)
    half = heads // 2
    for h in range(heads):
        kh = h * key_heads // heads
        beta = beta_ref[:, h : h + 1]
        gain = cumulative[:, h : h + 1]
        carried = jnp.exp(gain) * carries
        key = keys[kh].astype(F32)
        right = jnp.concatenate(
            [(beta * values[h].astype(F32)).astype(BF16), (beta * carried * key).astype(BF16)],
            axis=1,
        )
        solved = dot(inverse_ref[h], right).astype(BF16)
        mixed = dot(mixing_ref[h], solved)
        at = slice(h * HEAD, (h + 1) * HEAD)
        base_ref[:, at] = mixed[:, :HEAD]
        response_ref[:, at] = (carried * queries[kh].astype(F32) - mixed[:, HEAD:]).astype(BF16)
        last_same = (segment == segment[rows - 1 : rows, :]).astype(F32)
        last = jnp.exp(gain[rows - 1 : rows, :] - gain) * last_same
        ended = dot((last * key).T.astype(BF16), solved)
        forward = ended[:, :HEAD].astype(BF16)
        transition = (carried[rows - 1 : rows, :] * square - ended[:, HEAD:]).astype(BF16)
        low = h < half
        ours = (core == 0) if low else (core == 1)
        local = h % half

        @pl.when(ours)
        def _():
            mine_ref[0, local] = transition
            mine_ref[1, local] = forward

        @pl.when(jnp.logical_not(ours))
        def _():
            send_ref[0, local] = transition
            send_ref[1, local] = forward


def chip_kernel(where_ref, mine_ref, other_ref, chip_ref):
    core = where_ref[1]

    def compose(early, late):
        for h in range(mine_ref.shape[1]):
            left = late[0, h]
            chip_ref[0, h] = dot(left, early[0, h]).astype(BF16)
            chip_ref[1, h] = (dot(left, early[1, h]) + late[1, h].astype(F32)).astype(BF16)

    @pl.when(core == 0)
    def _():
        compose(mine_ref, other_ref)

    @pl.when(core != 0)
    def _():
        compose(other_ref, mine_ref)


def pair_kernel(chip_ref, before_ref, pair_ref):
    for h in range(chip_ref.shape[1]):
        left = chip_ref[0, h]
        pair_ref[0, h] = dot(left, before_ref[0, h]).astype(BF16)
        pair_ref[1, h] = (dot(left, before_ref[1, h]) + chip_ref[1, h].astype(F32)).astype(BF16)


def enter_kernel(where_ref, near_ref, far_ref, mine_ref, other_ref, keep_ref, send_ref):
    core = where_ref[1]
    for h in range(far_ref.shape[0]):
        entering = dot(near_ref[0, h], far_ref[h]) + near_ref[1, h].astype(F32)
        entering_low = entering.astype(BF16)

        @pl.when(core == 0)
        def _():
            keep_ref[h] = entering_low
            later = dot(mine_ref[0, h], entering_low) + mine_ref[1, h].astype(F32)
            send_ref[h] = later.astype(BF16)

        @pl.when(core != 0)
        def _():
            send_ref[h] = entering_low
            later = dot(other_ref[0, h], entering_low) + other_ref[1, h].astype(F32)
            keep_ref[h] = later.astype(BF16)


def finish_kernel(
    where_ref,
    base_ref,
    response_ref,
    keep_ref,
    other_ref,
    zgate_ref,
    gain_ref,
    w_out,
    term_ref,
    gated_ref,
    state_ref,
):
    core = where_ref[1]
    half = keep_ref.shape[0]

    @pl.when(core == 0)
    def _():
        state_ref[:half] = keep_ref[...]
        state_ref[half:] = other_ref[...]

    @pl.when(core != 0)
    def _():
        state_ref[:half] = other_ref[...]
        state_ref[half:] = keep_ref[...]

    for h in range(2 * half):
        at = slice(h * HEAD, (h + 1) * HEAD)
        attended = base_ref[:, at] + dot(response_ref[:, at], state_ref[h])
        scale = lax.rsqrt(jnp.mean(attended * attended, axis=-1, keepdims=True) + 1e-06)
        gate = silu(zgate_ref[:, at].astype(F32))
        gated_ref[:, at] = (attended * scale * gain_ref[...] * gate).astype(BF16)
    gated = gated_ref[...]
    width = term_ref.shape[2]
    for part in range(term_ref.shape[0]):
        term_ref[part] = dot(gated, w_out[:, part * width : (part + 1) * width]).astype(BF16)


def out(*shape, dtype=BF16):
    return jax.ShapeDtypeStruct(shape, dtype)


def shifted(value, axis, steps):
    count = lax.axis_size(axis)
    return lax.ppermute(value, axis, [(at, at + steps) for at in range(count - steps)])


def turned(value, axis, steps):
    count = lax.axis_size(axis)
    return lax.ppermute(value, axis, [(at, (at + steps) % count) for at in range(count)])


def swapped(value, axis):
    count = lax.axis_size(axis)
    return lax.ppermute(value, axis, [(at, at ^ 1) for at in range(count)])


def local(
    tokens,
    order,
    doc_lengths,
    w_query,
    w_key,
    w_value,
    w_zgate,
    w_beta,
    w_alpha,
    conv_query,
    conv_key,
    conv_value,
    decay_log,
    decay_bias,
    norm_gain,
    w_out,
):
    rows, width = tokens.shape
    shards = lax.axis_size("seq")
    groups = lax.axis_size("head")
    capacity = 2 * rows // shards
    slots = shards * capacity
    qk, vw, heads = w_query.shape[1], w_value.shape[1], w_beta.shape[1]
    half = heads // 2
    index = lax.axis_index("seq")
    where = jnp.stack([index * rows, index % 2]).astype(jnp.int32)

    send = pl.pallas_call(
        lambda *refs: pack_kernel(shards, *refs),
        out_shape=out(slots, width + LANES),
        in_specs=[VMEM] * 2,
        out_specs=VMEM,
        compiler_params=params(24),
        name="pack",
    )(order.reshape(1, rows), tokens)
    got = lax.all_to_all(
        send.reshape(shards, capacity, width + LANES), "seq", split_axis=0, concat_axis=0, tiled=True
    ).reshape(slots, width + LANES)
    query, key, value, zgate, tail, beta, decay = pl.pallas_call(
        project_kernel,
        out_shape=(
            out(rows, qk),
            out(rows, qk),
            out(rows, vw),
            out(rows, vw),
            out(TAIL, 2 * qk + vw),
            out(rows, heads, dtype=F32),
            out(rows, heads, dtype=F32),
        ),
        in_specs=[VMEM] + [ANY] * 4 + [VMEM] * 4,
        out_specs=(VMEM,) * 7,
        scratch_shapes=[
            pltpu.VMEM((rows, width), BF16),
            pltpu.VMEM((width, qk), BF16),
            pltpu.VMEM((width, qk), BF16),
            pltpu.VMEM((width, vw), BF16),
            pltpu.VMEM((width, vw), BF16),
            pltpu.SemaphoreType.DMA((4,)),
        ],
        compiler_params=params(40),
        name="project",
    )(
        got,
        w_query,
        w_key,
        w_value,
        w_zgate,
        w_beta,
        w_alpha,
        decay_log.reshape(1, heads),
        decay_bias.reshape(1, heads),
    )
    tail_got = shifted(tail, "seq", 1)
    states = out(2, half, HEAD, HEAD)
    mine, sent, base, response = pl.pallas_call(
        chunk_kernel,
        out_shape=(states, states, out(rows, vw, dtype=F32), out(rows, vw)),
        in_specs=[SMEM] * 2 + [VMEM] * 9,
        out_specs=(VMEM,) * 4,
        scratch_shapes=[
            pltpu.VMEM((heads, rows, rows), BF16),
            pltpu.VMEM((heads, rows, rows), BF16),
            pltpu.VMEM((qk // HEAD, rows, HEAD), BF16),
            pltpu.VMEM((qk // HEAD, rows, HEAD), BF16),
            pltpu.VMEM((heads, rows, HEAD), BF16),
            pltpu.VMEM((heads, rows, rows), BF16),
            pltpu.VMEM((rows.bit_length() - 1, rows, rows), BF16),
        ],
        compiler_params=params(40),
        name="chunk",
    )(
        where,
        doc_lengths,
        query,
        key,
        value,
        tail_got,
        conv_query,
        conv_key,
        conv_value,
        beta,
        decay,
    )
    other = swapped(sent, "seq")
    chip = pl.pallas_call(
        chip_kernel,
        out_shape=states,
        in_specs=[SMEM, VMEM, VMEM],
        out_specs=VMEM,
        name="chip",
    )(where, mine, other)
    pair = pl.pallas_call(
        pair_kernel, out_shape=states, in_specs=[VMEM] * 2, out_specs=VMEM, name="pair"
    )(chip, shifted(chip, "seq", 2))
    near, far = shifted(pair, "seq", 2), shifted(pair[1], "seq", 6)
    state = out(half, HEAD, HEAD)
    keep, give = pl.pallas_call(
        enter_kernel,
        out_shape=(state, state),
        in_specs=[SMEM] + [VMEM] * 4,
        out_specs=(VMEM,) * 2,
        name="enter",
    )(where, near, far, mine, other)
    term = pl.pallas_call(
        finish_kernel,
        out_shape=out(groups, rows, width // groups),
        in_specs=[SMEM] + [VMEM] * 7,
        out_specs=VMEM,
        scratch_shapes=[pltpu.VMEM((rows, vw), BF16), pltpu.VMEM((heads, HEAD, HEAD), BF16)],
        compiler_params=params(32),
        name="finish",
    )(where, base, response, keep, swapped(give, "seq"), zgate, norm_gain.reshape(1, HEAD), w_out)
    here = lax.axis_index("head")
    mixed = lax.dynamic_index_in_dim(term, here, 0, keepdims=False).astype(F32)
    for steps in range(1, groups):
        leaving = lax.dynamic_index_in_dim(term, (here + steps) % groups, 0, keepdims=False)
        mixed = mixed + turned(leaving, "head", steps).astype(F32)
    return mixed.astype(BF16)


def solution(mesh):
    return jax.shard_map(
        local,
        mesh=mesh,
        in_specs=(
            P("seq", None),
            P("seq"),
            P(),
            P(None, "head"),
            P(None, "head"),
            P(None, "head"),
            P(None, "head"),
            P(None, "head"),
            P(None, "head"),
            P(None, "head"),
            P(None, "head"),
            P(None, "head"),
            P("head"),
            P("head"),
            P(),
            P("head", None),
        ),
        out_specs=P("seq", "head"),
        check_vma=False,
    )
```

time: 812 us -> 137 us (0.17)
  the two profiles are of different devices: /device:TPU:1 before, /device:TPU:64 now
where the time goes in v1:
time: 137 us; the launch traced here: 136 us
  waiting for transfers between devices  64.1 us (47%)
  Pallas kernels  29.8 us (22%)
  starting transfers between devices  25.4 us (19%)
  local copies, waits for them, and re-layouts  15.8 us (12%)
    all_to_all x1, waiting for transfers between devices, local(): lax.all_to_all(send.reshape(shards, capacity, width + LANES), 'seq', spli...  28.4 us
    ppermute x4, waiting for transfers between devices, shifted(): lax.ppermute(value, axis, [(at, at + steps) for at in range(count - steps)])  22.1 us
    unnamed x52, local copies, waits for them, and re-layouts  14.8 us
    pallas_call x1, Pallas kernels, local(): pl.pallas_call(chunk_kernel, out_shape=(states, states, out(rows, vw, dty...  12 us
    ppermute x4, starting transfers between devices, shifted(): lax.ppermute(value, axis, [(at, at + steps) for at in range(count - steps)])  11.8 us
    ppermute x3, waiting for transfers between devices, turned(): lax.ppermute(value, axis, [(at, (at + steps) % count) for at in range(cou...  10.6 us
    all_to_all x1, starting transfers between devices, local(): lax.all_to_all(send.reshape(shards, capacity, width + LANES), 'seq', spli...  7.73 us
    pallas_call x1, Pallas kernels, local(): pl.pallas_call(project_kernel, out_shape=(out(rows, qk), out(rows, qk), o...  5.99 us
  transfers between devices with their start and end apart: 10, of which 9 were waited for; matrix products, arithmetic and copies ran while one was open for 1% of the time, Pallas kernels for 0%

profile of v1, /device:TPU:64, one launch (start us, length us, event | category | flops | bytes accessed | tf_op | source)
XLA Modules:
  0.0 136.3 jit_solution(3917002497799579713)
XLA Ops:
  1.9 2.3 %pack.1 = bf16[512,2176]{1,0:T(8,128)(2,1)} custom-call(s32[1,256]{1,0:T(1,128)S(1)} %bitcast.20, bf16[256,2048]{1,0:T(8,128)(2,1)S(1)} %copy-done.4), custom_call_target="tpu_custom_call" | custom-call | tf_op jit(solution)/shard_map/pack/pallas_call | solution.py:393
  4.2 7.7 %all-to-all-start = ((bf16[32,16,2176]{2,1,0:T(8,128)(2,1)}), bf16[32,16,2176]{2,1,0:T(8,128)(2,1)S(1)}, u32[]{:S(2)}, u32[]{:S(2)}) async-start(bf16[32,16,2176]{2,1,0:T(8,128)(2,1)} %bitcast.3), calls=%async_computation | async-start | bytes 4456448 | tf_op jit(solution)/shard_map/all_to_all | solution.py:401
  12.6 28.4 %all-to-all-done = bf16[32,16,2176]{2,1,0:T(8,128)(2,1)S(1)} async-done(((bf16[32,16,2176]{2,1,0:T(8,128)(2,1)}), bf16[32,16,2176]{2,1,0:T(8,128)(2,1)S(1)}, u32[]{:S(2)}, u32[]{:S(2)}) %all-to-all-start) | async-done | bytes 2228256 | tf_op jit(solution)/shard_map/all_to_all | solution.py:401
  41.0 2.2 %copy-done.1 = bf16[2048,1024]{1,0:T(8,128)(2,1)S(1)} copy-done((bf16[2048,1024]{1,0:T(8,128)(2,1)S(1)}, bf16[2048,1024]{1,0:T(8,128)(2,1)}, u32[]{:S(2)}) %copy-start.1) | copy-done | bytes 4194328
  43.2 1.6 %copy-done.2 = bf16[2048,512]{1,0:T(8,128)(2,1)S(1)} copy-done((bf16[2048,512]{1,0:T(8,128)(2,1)S(1)}, bf16[2048,512]{1,0:T(8,128)(2,1)}, u32[]{:S(2)}) %copy-start.2) | copy-done | bytes 2097176
  44.8 1.6 %copy-done.3 = bf16[2048,512]{1,0:T(8,128)(2,1)S(1)} copy-done((bf16[2048,512]{1,0:T(8,128)(2,1)S(1)}, bf16[2048,512]{1,0:T(8,128)(2,1)}, u32[]{:S(2)}) %copy-start.3) | copy-done | bytes 2097176
  46.4 6.0 %project.1 = (bf16[256,512]{1,0:T(8,128)(2,1)S(1)}, bf16[256,512]{1,0:T(8,128)(2,1)S(1)}, bf16[256,1024]{1,0:T(8,128)(2,1)S(1)}, bf16[256,1024]{1,0:T(8,128)(2,1...) custom-call(bf16[512,2176]{1,0:T(8,128)(2,1)S(1)} %bitcast.19, ...), custom_call_target="tpu_custom_call" | custom-call | tf_op jit(solution)/shard_map/project/pallas_call | solution.py:404
  52.4 2.3 %collective-permute-start = (bf16[16,2048]{1,0:T(8,128)(2,1)S(1)}, bf16[16,2048]{1,0:T(8,128)(2,1)S(1)}, u32[]{:S(2)}, u32[]{:S(2)}) collective-permute-start(bf16[16,2048]{1,0:T(8,128)(2,1)S(1)} %get-tuple-element.21), channel_id=1, source_target_pairs={{0,4},{4,8},{8,12},{12,16},{16,20},{20,24},{24,28},{28,32},{32,36}... | collective-permute-start | bytes 196616 | tf_op jit(solution)/shard_map/ppermute | solution.py:352
  54.8 5.4 %collective-permute-done.tail_ref = bf16[16,2048]{1,0:T(8,128)(2,1)S(1)} collective-permute-done((bf16[16,2048]{1,0:T(8,128)(2,1)S(1)}, bf16[16,2048]{1,0:T(8,128)(2,1)S(1)}, u32[]{:S(2)}, u32[]{:S(2)}) %collective-permute-start) | collective-permute-done | bytes 65568 | tf_op jit(solution)/shard_map/ppermute | solution.py:352
  60.2 12.0 %chunk.1 = (bf16[2,4,128,128]{3,2,1,0:T(8,128)(2,1)S(1)}, bf16[2,4,128,128]{3,2,1,0:T(8,128)(2,1)S(1)}, f32[256,1024]{1,0:T(8,128)S(1)}, bf16[256,1024]{1,0:T(8,128)(2,1)S(1)}) custom-call(s32[2]{0:T(128)S(1)} %pad_add_fusion.where_ref, s32[8]{0:T(128)S(1)} %copy-done.17, bf16[256,512]{1,0:T(8,128)(2,1)S(1)} %get-tuple-element.18.query_ref, ...), custom_call_target="tpu_custom_call" | custom-call | tf_op jit(solution)/shard_map/chunk/pallas_call | solution.py:440
  75.2 1.9 %chip.1.chip_ref = bf16[2,4,128,128]{3,2,1,0:T(8,128)(2,1)} custom-call(s32[2]{0:T(128)} %copy-done.10, bf16[2,4,128,128]{3,2,1,0:T(8,128)(2,1)} %copy-done.5, bf16[2,4,128,128]{3,2,1,0:T(8,128)(2,1)} %copy-done.19), custom_call_target="tpu_custom_call" | custom-call | tf_op jit(solution)/shard_map/chip/pallas_call | solution.py:470
  77.2 1.9 %collective-permute-start.2 = (bf16[2,4,128,128]{3,2,1,0:T(8,128)(2,1)}, bf16[2,4,128,128]{3,2,1,0:T(8,128)(2,1)S(1)}, u32[]{:S(2)}, u32[]{:S(2)}) collective-permute-start(bf16[2,4,128,128]{3,2,1,0:T(8,128)(2,1)} %chip.1.chip_ref), channel_id=1, source_target_pairs={{0,8},{4,12},{8,16},{12,20},{16,24},{20,28},{24,32},{28,36},{32,40... | collective-permute-start | bytes 786440 | tf_op jit(solution)/shard_map/ppermute | solution.py:352
  79.1 10.6 %collective-permute-done.2.before_ref = bf16[2,4,128,128]{3,2,1,0:T(8,128)(2,1)S(1)} collective-permute-done((bf16[2,4,128,128]{3,2,1,0:T(8,128)(2,1)}, bf16[2,4,128,128]{3,2,1,0:T(8,128)(2,1)S(1)}, u32[]{:S(2)}, u32[]{:S(2)}) %collective-permute-start.2) | collective-permute-done | bytes 262176 | tf_op jit(solution)/shard_map/ppermute | solution.py:352
  90.4 1.9 %pair.1 = bf16[2,4,128,128]{3,2,1,0:T(8,128)(2,1)} custom-call(bf16[2,4,128,128]{3,2,1,0:T(8,128)(2,1)} %chip.1.chip_ref, bf16[2,4,128,128]{3,2,1,0:T(8,128)(2,1)} %copy-done.21), custom_call_target="tpu_custom_call" | custom-call | tf_op jit(solution)/shard_map/pair/pallas_call | solution.py:477
  92.4 1.9 %collective-permute-start.3 = (bf16[2,4,128,128]{3,2,1,0:T(8,128)(2,1)}, bf16[2,4,128,128]{3,2,1,0:T(8,128)(2,1)S(1)}, u32[]{:S(2)}, u32[]{:S(2)}) collective-permute-start(bf16[2,4,128,128]{3,2,1,0:T(8,128)(2,1)} %pair.1), channel_id=1, source_target_pairs={{0,8},{4,12},{8,16},{12,20},{16,24},{20,28},{24,32},{28,36},{32,40... | collective-permute-start | bytes 786440 | tf_op jit(solution)/shard_map/ppermute | solution.py:352
  95.2 5.7 %collective-permute-start.4 = (bf16[4,128,128]{2,1,0:T(8,128)(2,1)S(1)}, bf16[4,128,128]{2,1,0:T(8,128)(2,1)S(1)}, u32[]{:S(2)}, u32[]{:S(2)}) collective-permute-start(bf16[4,128,128]{2,1,0:T(8,128)(2,1)S(1)} %slice_bitcast_fusion), channel_id=1, source_target_pairs={{0,24},{4,28},{8,32},{12,36},{16,40},{20,44},{24,48},{28,52},{32,5... | collective-permute-start | bytes 393224 | tf_op jit(solution)/shard_map/ppermute | solution.py:352
  100.9 5.7 %collective-permute-done.4.far_ref = bf16[4,128,128]{2,1,0:T(8,128)(2,1)S(1)} collective-permute-done((bf16[4,128,128]{2,1,0:T(8,128)(2,1)S(1)}, bf16[4,128,128]{2,1,0:T(8,128)(2,1)S(1)}, u32[]{:S(2)}, u32[]{:S(2)}) %collective-permute-start.4) | collective-permute-done | bytes 131104 | tf_op jit(solution)/shard_map/ppermute | solution.py:352
  108.0 3.0 %enter.1 = (bf16[4,128,128]{2,1,0:T(8,128)(2,1)}, bf16[4,128,128]{2,1,0:T(8,128)(2,1)}) custom-call(s32[2]{0:T(128)} %copy-done.10, bf16[2,4,128,128]{3,2,1,0:T(8,128)(2,1)} %copy-done.20, bf16[4,128,128]{2,1,0:T(8,128)(2,1)} %copy-done.22, bf16[2,4,128,128]{3,2,1,0:T(8,128)(2,1)} %copy-done.5, bf16[2,4,128,128]{3,2,1,0:T(8,128)(2,1)} %copy-done.19), custom_call_target="tpu_custom_call" | custom-call | tf_op jit(solution)/shard_map/enter/pallas_call | solution.py:482
  112.5 2.2 %copy-done = bf16[1024,2048]{1,0:T(8,128)(2,1)S(1)} copy-done((bf16[1024,2048]{1,0:T(8,128)(2,1)S(1)}, bf16[1024,2048]{1,0:T(8,128)(2,1)}, u32[]{:S(2)}) %copy-start) | copy-done | bytes 4194328
  116.3 2.6 %finish.1 = bf16[4,256,512]{2,1,0:T(8,128)(2,1)S(1)} custom-call(s32[2]{0:T(128)S(1)} %copy-done.11, f32[256,1024]{1,0:T(8,128)S(1)} %get-tuple-element.24.base_ref, bf16[256,1024]{1,0:T(8,128)(2,1)S(1)} %get-tuple-element.25.response_ref, bf16[4,128,128]{2,1,0:T(8,128)(2,1)S(1)} %copy-done.8, bf16[4,128,128]{2,1,0:T(8,128)(2,1)S(1)} %collective-permute-done.5.other_ref, ...), custom_call_target="tpu_custom_call" | custom-call | tf_op jit(solution)/shard_map/finish/pallas_call | solution.py:489
  119.0 1.6 %collective-permute-start.6 = (bf16[256,512]{1,0:T(8,128)(2,1)S(1)}, bf16[256,512]{1,0:T(8,128)(2,1)S(1)}, u32[]{:S(2)}, u32[]{:S(2)}) collective-permute-start(bf16[256,512]{1,0:T(8,128)(2,1)S(1)} %get-tuple-element.31), channel_id=1, source_target_pairs={{0,1},{1,2},{2,3},{3,0},{4,5},{5,6},{6,7},{7,4},{8,9},{9,10},{10,1... | collective-permute-start | bytes 786440 | tf_op jit(solution)/shard_map/ppermute | solution.py:357
  120.6 2.9 %collective-permute-start.7 = (bf16[256,512]{1,0:T(8,128)(2,1)S(1)}, bf16[256,512]{1,0:T(8,128)(2,1)S(1)}, u32[]{:S(2)}, u32[]{:S(2)}) collective-permute-start(bf16[256,512]{1,0:T(8,128)(2,1)S(1)} %get-tuple-element.33), channel_id=1, source_target_pairs={{0,2},{1,3},{2,0},{3,1},{4,6},{5,7},{6,4},{7,5},{8,10},{9,11},{10,... | collective-permute-start | bytes 786440 | tf_op jit(solution)/shard_map/ppermute | solution.py:357
  124.9 3.8 %collective-permute-done.6 = bf16[256,512]{1,0:T(8,128)(2,1)S(1)} collective-permute-done((bf16[256,512]{1,0:T(8,128)(2,1)S(1)}, bf16[256,512]{1,0:T(8,128)(2,1)S(1)}, u32[]{:S(2)}, u32[]{:S(2)}) %collective-permute-start.6) | collective-permute-done | bytes 262176 | tf_op jit(solution)/shard_map/ppermute | solution.py:357
  128.7 6.8 %collective-permute-done.7 = bf16[256,512]{1,0:T(8,128)(2,1)S(1)} collective-permute-done((bf16[256,512]{1,0:T(8,128)(2,1)S(1)}, bf16[256,512]{1,0:T(8,128)(2,1)S(1)}, u32[]{:S(2)}, u32[]{:S(2)}) %collective-permute-start.7) | collective-permute-done | bytes 262176 | tf_op jit(solution)/shard_map/ppermute | solution.py:357
  (59 shorter events, 13.9 us)
Async XLA Ops:
  4.2 7.8 %copy-start.23 = (bf16[2048,8]{0,1:T(8,128)(2,1)S(1)}, bf16[2048,8]{0,1:T(8,128)(2,1)}, u32[]{:S(2)}) copy-start(bf16[2048,8]{0,1:T(8,128)(2,1)} %param.23) | copy-start | bytes 98308
  4.2 8.1 %copy-start.24 = (bf16[2048,8]{0,1:T(8,128)(2,1)S(1)}, bf16[2048,8]{0,1:T(8,128)(2,1)}, u32[]{:S(2)}) copy-start(bf16[2048,8]{0,1:T(8,128)(2,1)} %param.24) | copy-start | bytes 98308
  4.2 36.8 %copy-start.15 = (f32[8]{0:T(128)S(1)}, f32[8]{0:T(128)}, u32[]{:S(2)}) copy-start(f32[8]{0:T(128)} %param.28) | copy-start | bytes 100
  4.2 36.8 %copy-start.16 = (f32[8]{0:T(128)S(1)}, f32[8]{0:T(128)}, u32[]{:S(2)}) copy-start(f32[8]{0:T(128)} %param.29) | copy-start | bytes 100
  4.2 36.8 %all-to-all-start = ((bf16[32,16,2176]{2,1,0:T(8,128)(2,1)}), bf16[32,16,2176]{2,1,0:T(8,128)(2,1)S(1)}, u32[]{:S(2)}, u32[]{:S(2)}) async-start(bf16[32,16,2176]{2,1,0:T(8,128)(2,1)} %bitcast.3), calls=%async_computation | async-start | bytes 4456448 | tf_op jit(solution)/shard_map/all_to_all | solution.py:401
  41.0 2.2 %copy-start.1 = (bf16[2048,1024]{1,0:T(8,128)(2,1)S(1)}, bf16[2048,1024]{1,0:T(8,128)(2,1)}, u32[]{:S(2)}) copy-start(bf16[2048,1024]{1,0:T(8,128)(2,1)} %w_value.1) | copy-start | bytes 12582916
  46.4 13.9 %copy-start.9 = (bf16[4,1024]{1,0:T(4,128)(2,1)S(1)}, bf16[4,1024]{1,0:T(4,128)(2,1)}, u32[]{:S(2)}) copy-start(bf16[4,1024]{1,0:T(4,128)(2,1)} %taps_value.1) | copy-start | bytes 24580
  46.4 13.9 %copy-start.12 = (bf16[4,512]{1,0:T(4,128)(2,1)S(1)}, bf16[4,512]{1,0:T(4,128)(2,1)}, u32[]{:S(2)}) copy-start(bf16[4,512]{1,0:T(4,128)(2,1)} %taps_query.1) | copy-start | bytes 12292
  46.4 13.9 %copy-start.13 = (bf16[4,512]{1,0:T(4,128)(2,1)S(1)}, bf16[4,512]{1,0:T(4,128)(2,1)}, u32[]{:S(2)}) copy-start(bf16[4,512]{1,0:T(4,128)(2,1)} %taps_key.1) | copy-start | bytes 12292
  46.4 13.9 %copy-start.17 = (s32[8]{0:T(128)S(1)}, s32[8]{0:T(128)}, u32[]{:S(2)}) copy-start(s32[8]{0:T(128)} %lengths_ref.1) | copy-start | bytes 100
  52.4 19.9 %copy-start.6 = (bf16[256,1024]{1,0:T(8,128)(2,1)}, bf16[256,1024]{1,0:T(8,128)(2,1)S(1)}, u32[]{:S(2)}) copy-start(bf16[256,1024]{1,0:T(8,128)(2,1)S(1)} %get-tuple-element.30.zgate_ref) | copy-start | bytes 1572868
  52.4 60.1 %copy-start.18 = (f32[128]{0:T(128)S(1)}, f32[128]{0:T(128)}, u32[]{:S(2)}) copy-start(f32[128]{0:T(128)} %param.30) | copy-start | bytes 1540
  52.4 7.8 %collective-permute-start = (bf16[16,2048]{1,0:T(8,128)(2,1)S(1)}, bf16[16,2048]{1,0:T(8,128)(2,1)S(1)}, u32[]{:S(2)}, u32[]{:S(2)}) collective-permute-start(bf16[16,2048]{1,0:T(8,128)(2,1)S(1)} %get-tuple-element.21), channel_id=1, source_target_pairs={{0,4},{4,8},{8,12},{12,16},{16,20},{20,24},{24,28},{28,32},{32,36}... | collective-permute-start | bytes 196616 | tf_op jit(solution)/shard_map/ppermute | solution.py:352
  54.8 19.7 %copy-start.10 = (s32[2]{0:T(128)}, s32[2]{0:T(128)S(1)}, u32[]{:S(2)}) copy-start(s32[2]{0:T(128)S(1)} %pad_add_fusion.where_ref) | copy-start | bytes 28
  73.0 39.5 %copy-start.7 = (bf16[256,1024]{1,0:T(8,128)(2,1)S(1)}, bf16[256,1024]{1,0:T(8,128)(2,1)}, u32[]{:S(2)}) copy-start(bf16[256,1024]{1,0:T(8,128)(2,1)} %copy-done.6) | copy-start | bytes 1572868
  73.0 1.5 %collective-permute-start.1 = (bf16[2,4,128,128]{3,2,1,0:T(8,128)(2,1)S(1)}, bf16[2,4,128,128]{3,2,1,0:T(8,128)(2,1)S(1)}, u32[]{:S(2)}, u32[]{:S(2)}) collective-permute-start(bf16[2,4,128,128]{3,2,1,0:T(8,128)(2,1)S(1)} %get-tuple-element.27), channel_id=1, source_target_pairs={{0,4},{4,0},{8,12},{12,8},{16,20},{20,16},{24,28},{28,24},{32,36},... | collective-permute-start | bytes 786440 | tf_op jit(solution)/shard_map/ppermute | solution.py:362
  77.2 12.6 %collective-permute-start.2 = (bf16[2,4,128,128]{3,2,1,0:T(8,128)(2,1)}, bf16[2,4,128,128]{3,2,1,0:T(8,128)(2,1)S(1)}, u32[]{:S(2)}, u32[]{:S(2)}) collective-permute-start(bf16[2,4,128,128]{3,2,1,0:T(8,128)(2,1)} %chip.1.chip_ref), channel_id=1, source_target_pairs={{0,8},{4,12},{8,16},{12,20},{16,24},{20,28},{24,32},{28,36},{32,40... | collective-permute-start | bytes 786440 | tf_op jit(solution)/shard_map/ppermute | solution.py:352
  92.4 14.5 %collective-permute-start.3 = (bf16[2,4,128,128]{3,2,1,0:T(8,128)(2,1)}, bf16[2,4,128,128]{3,2,1,0:T(8,128)(2,1)S(1)}, u32[]{:S(2)}, u32[]{:S(2)}) collective-permute-start(bf16[2,4,128,128]{3,2,1,0:T(8,128)(2,1)} %pair.1), channel_id=1, source_target_pairs={{0,8},{4,12},{8,16},{12,20},{16,24},{20,28},{24,32},{28,36},{32,40... | collective-permute-start | bytes 786440 | tf_op jit(solution)/shard_map/ppermute | solution.py:352
  95.2 11.4 %collective-permute-start.4 = (bf16[4,128,128]{2,1,0:T(8,128)(2,1)S(1)}, bf16[4,128,128]{2,1,0:T(8,128)(2,1)S(1)}, u32[]{:S(2)}, u32[]{:S(2)}) collective-permute-start(bf16[4,128,128]{2,1,0:T(8,128)(2,1)S(1)} %slice_bitcast_fusion), channel_id=1, source_target_pairs={{0,24},{4,28},{8,32},{12,36},{16,40},{20,44},{24,48},{28,52},{32,5... | collective-permute-start | bytes 393224 | tf_op jit(solution)/shard_map/ppermute | solution.py:352
  111.0 1.6 %collective-permute-start.5 = (bf16[4,128,128]{2,1,0:T(8,128)(2,1)}, bf16[4,128,128]{2,1,0:T(8,128)(2,1)S(1)}, u32[]{:S(2)}, u32[]{:S(2)}) collective-permute-start(bf16[4,128,128]{2,1,0:T(8,128)(2,1)} %get-tuple-element.29), channel_id=1, source_target_pairs={{0,4},{4,0},{8,12},{12,8},{16,20},{20,16},{24,28},{28,24},{32,36},... | collective-permute-start | bytes 393224 | tf_op jit(solution)/shard_map/ppermute | solution.py:362
  112.5 2.2 %copy-start = (bf16[1024,2048]{1,0:T(8,128)(2,1)S(1)}, bf16[1024,2048]{1,0:T(8,128)(2,1)}, u32[]{:S(2)}) copy-start(bf16[1024,2048]{1,0:T(8,128)(2,1)} %w_out.1) | copy-start | bytes 12582916
  119.0 9.7 %collective-permute-start.6 = (bf16[256,512]{1,0:T(8,128)(2,1)S(1)}, bf16[256,512]{1,0:T(8,128)(2,1)S(1)}, u32[]{:S(2)}, u32[]{:S(2)}) collective-permute-start(bf16[256,512]{1,0:T(8,128)(2,1)S(1)} %get-tuple-element.31), channel_id=1, source_target_pairs={{0,1},{1,2},{2,3},{3,0},{4,5},{5,6},{6,7},{7,4},{8,9},{9,10},{10,1... | collective-permute-start | bytes 786440 | tf_op jit(solution)/shard_map/ppermute | solution.py:357
  120.6 14.9 %collective-permute-start.7 = (bf16[256,512]{1,0:T(8,128)(2,1)S(1)}, bf16[256,512]{1,0:T(8,128)(2,1)S(1)}, u32[]{:S(2)}, u32[]{:S(2)}) collective-permute-start(bf16[256,512]{1,0:T(8,128)(2,1)S(1)} %get-tuple-element.33), channel_id=1, source_target_pairs={{0,2},{1,3},{2,0},{3,1},{4,6},{5,7},{6,4},{7,5},{8,10},{9,11},{10,... | collective-permute-start | bytes 786440 | tf_op jit(solution)/shard_map/ppermute | solution.py:357
  123.5 12.0 %collective-permute-start.8 = (bf16[256,512]{1,0:T(8,128)(2,1)S(1)}, bf16[256,512]{1,0:T(8,128)(2,1)S(1)}, u32[]{:S(2)}, u32[]{:S(2)}) collective-permute-start(bf16[256,512]{1,0:T(8,128)(2,1)S(1)} %get-tuple-element.32), channel_id=1, source_target_pairs={{0,3},{1,0},{2,1},{3,2},{4,7},{5,4},{6,5},{7,6},{8,11},{9,8},{10,9... | collective-permute-start | bytes 786440 | tf_op jit(solution)/shard_map/ppermute | solution.py:357
  (11 other events, 10.1 us)

commit v2 on v1

v2 whole, which is shorter than its diff:
```python
import jax
import jax.numpy as jnp
from jax import lax
from jax.experimental import pallas as pl
from jax.experimental.pallas import tpu as pltpu
from jax.sharding import PartitionSpec as P

HEAD = 128
KERNEL = 4
TAIL = 16
LANES = 128
FETCHES = 4
VMEM = pl.BlockSpec(memory_space=pltpu.VMEM)
SMEM = pl.BlockSpec(memory_space=pltpu.SMEM)
ANY = pl.BlockSpec(memory_space=pl.ANY)
F32 = jnp.float32
BF16 = jnp.bfloat16
HIGHEST = lax.Precision.HIGHEST


def iota(shape, axis):
    return lax.broadcasted_iota(jnp.int32, shape, axis)


def dot(left, right, contract=((1,), (0,)), precision=None):
    return lax.dot_general(
        left, right, (contract, ((), ())), precision=precision, preferred_element_type=F32
    )


def params(mib):
    return pltpu.CompilerParams(vmem_limit_bytes=mib << 20)


def pack_kernel(shards, order_ref, tokens_ref, send_ref):
    rows, width = tokens_ref.shape
    slots = send_ref.shape[0]
    capacity = slots // shards
    order = order_ref[...]
    bits = rows.bit_length() - 1
    target = lax.shift_right_logical(order, jnp.full_like(order, bits))
    landing = lax.bitwise_and(order, jnp.full_like(order, rows - 1))
    marks = (iota((shards, rows), 0) == target).astype(F32)
    before = (iota((rows, rows), 0) < iota((rows, rows), 1)).astype(F32).astype(BF16)
    earlier = dot(marks.astype(BF16), before)
    slot = jnp.sum(earlier * marks, axis=0, keepdims=True).astype(jnp.int32)
    hit = (iota((slots, rows), 0) == target * capacity + slot).astype(F32)
    send_ref[:, :width] = dot(hit.astype(BF16), tokens_ref[...]).astype(BF16)
    spot = jnp.sum(hit * (landing + 1).astype(F32), axis=1, keepdims=True)
    send_ref[:, width:] = jnp.broadcast_to(spot, (slots, LANES)).astype(BF16)


def softplus(x):
    return jnp.maximum(x, 0.0) + jnp.log1p(jnp.exp(-jnp.abs(x)))


def fetch_kernel(*refs):
    count = (len(refs) - 1) // 2
    copies = []
    for i, (source, target) in enumerate(zip(refs[:count], refs[count : 2 * count])):
        part = source.shape[0] // FETCHES
        for j in range(FETCHES):
            at = pl.ds(j * part, part)
            copies.append(
                pltpu.make_async_copy(source.at[at], target.at[at], refs[-1].at[i * FETCHES + j])
            )
    for copy in copies:
        copy.start()
    for copy in copies:
        copy.wait()


def project_kernel(
    got_ref,
    w_key,
    w_value,
    w_beta,
    w_alpha,
    decay_log,
    decay_bias,
    balanced_ref,
    key_ref,
    value_ref,
    tail_ref,
    beta_ref,
    decay_ref,
):
    rows, width = balanced_ref.shape
    slots = got_ref.shape[0]
    spot = got_ref[:, width : width + 1].astype(F32).astype(jnp.int32)
    hit = (spot == iota((slots, rows), 1) + 1).astype(F32).T.astype(BF16)
    for start in range(0, width, 512):
        part = slice(start, start + 512)
        balanced_ref[:, part] = dot(hit, got_ref[:, part]).astype(BF16)
    balanced = balanced_ref[...]
    across = ((1,), (1,))
    column = 0
    for weight, to in ((w_key, key_ref), (w_value, value_ref)):
        for start in range(0, to.shape[1], 512):
            part = dot(balanced, weight[:, start : start + 512]).astype(BF16)
            to[:, start : start + 512] = part
            tail_ref[:, column : column + 512] = part[rows - TAIL :]
            column += 512
    beta_ref[...] = jax.nn.sigmoid(dot(balanced, w_beta[...], across))
    decay_ref[...] = -jnp.exp(decay_log[...]) * softplus(
        dot(balanced, w_alpha[...], across) + decay_bias[...]
    )


def project_more_kernel(balanced_ref, w_query, w_zgate, query_ref, gate_ref, tail_ref):
    rows = balanced_ref.shape[0]
    balanced = balanced_ref[...]
    for weight, to in ((w_query, query_ref), (w_zgate, gate_ref)):
        for start in range(0, to.shape[1], 512):
            part = dot(balanced, weight[:, start : start + 512]).astype(BF16)
            to[:, start : start + 512] = part
            if to is query_ref:
                tail_ref[:, start : start + 512] = part[rows - TAIL :]


def silu(x):
    return x / (1.0 + jnp.exp(-x))


def document_ends(lengths_ref):
    ends, total = [], jnp.int32(0)
    for i in range(lengths_ref.shape[0]):
        total = total + lengths_ref[i]
        ends.append(total)
    return ends


def segments(position, ends):
    count = (position >= 0).astype(jnp.int32) - 1
    for end in ends:
        count = count + (position >= end).astype(jnp.int32)
    return count


def convolve(projected, tail, taps, same):
    extended = jnp.concatenate([tail.astype(F32), projected.astype(F32)], axis=0)
    sums = None
    for lag in range(KERNEL):
        rolled = extended if lag == 0 else pltpu.roll(extended, lag, 0)
        tap = taps[KERNEL - 1 - lag : KERNEL - lag, :].astype(F32)
        term = rolled[TAIL:] * tap
        if lag:
            term = term * same[lag - 1]
        sums = term if sums is None else sums + term
    return silu(sums)


def unit(x, factor):
    return x * (lax.rsqrt(jnp.sum(x * x, axis=-1, keepdims=True) + 1e-06) * factor)


def masks(first, ends, rows):
    position = first + iota((rows, 1), 0)
    segment = segments(position, ends)
    same = [
        (segments(position - lag, ends) == segment).astype(F32) for lag in range(1, KERNEL)
    ]
    inside = segment == segments(first + iota((1, rows), 1), ends)
    before = segments(jnp.full((1, 1), first - 1, jnp.int32), ends)
    carries = (segment == before).astype(F32)
    return segment, same, inside, carries


def cumulated(decay_ref):
    rows, heads = decay_ref.shape
    lower = (iota((rows, rows), 0) >= iota((rows, rows), 1)).astype(F32)
    down = dot(lower, decay_ref[...], precision=HIGHEST)
    padded = jnp.concatenate([down, jnp.zeros((rows, LANES - heads), F32)], axis=1)
    return down, padded.T


def between(down, across, h, inside):
    difference = down[:, h : h + 1] - across[h : h + 1, :]
    return jnp.where(inside, jnp.exp(jnp.where(inside, difference, 0.0)), 0.0)


def column_of(h):
    return slice(h * HEAD, (h + 1) * HEAD)


def chunk_kernel(
    where_ref,
    lengths_ref,
    key_ref,
    value_ref,
    tail_ref,
    taps_key,
    taps_value,
    beta_ref,
    decay_ref,
    mine_ref,
    send_ref,
    keys,
    solved_ref,
    system_ref,
    inverse_ref,
    mask_ref,
):
    rows = key_ref.shape[0]
    first, core = where_ref[0], where_ref[1]
    heads = beta_ref.shape[1]
    key_heads = key_ref.shape[1] // HEAD
    repeat = heads // key_heads
    width = key_ref.shape[1]
    segment, same, inside, carries = masks(first, document_ends(lengths_ref), rows)
    row, column = iota((rows, rows), 0), iota((rows, rows), 1)
    levels = rows.bit_length() - 1
    for level in range(levels):
        size = 1 << level
        apart = (lax.bitwise_xor(row, column) < 2 * size) & (
            lax.bitwise_and(row, size) > lax.bitwise_and(column, size)
        )
        mask_ref[level] = apart.astype(F32).astype(BF16)
    unit_matrix = (row == column).astype(F32)
    strict = inside & (row > column)
    down, across = cumulated(decay_ref)

    for kh in range(key_heads):
        at = column_of(kh)
        keys[kh] = unit(
            convolve(key_ref[:, at], tail_ref[:, at], taps_key[:, at], same), 1.0
        ).astype(BF16)
        inner = dot(keys[kh], keys[kh], ((1,), (1,)))
        for h in range(kh * repeat, (kh + 1) * repeat):
            system = beta_ref[:, h : h + 1] * inner * between(down, across, h, strict)
            system_ref[h] = system.astype(BF16)
            inverse_ref[h] = (unit_matrix - system * mask_ref[0].astype(F32)).astype(BF16)
    for level in range(1, levels):
        for h in range(heads):
            inverse = inverse_ref[h]
            part = dot(system_ref[h] * mask_ref[level], inverse).astype(BF16)
            inverse_ref[h] = (inverse.astype(F32) - dot(inverse, part)).astype(BF16)

    square = (iota((HEAD, HEAD), 0) == iota((HEAD, HEAD), 1)).astype(F32)
    half = heads // 2
    last_same = (segment == segment[rows - 1 : rows, :]).astype(F32)
    for h in range(heads):
        at, to = column_of(h), column_of(key_heads + h)
        beta = beta_ref[:, h : h + 1]
        gain = down[:, h : h + 1]
        carried = jnp.exp(gain) * carries
        key = keys[h // repeat].astype(F32)
        value = convolve(value_ref[:, at], tail_ref[:, to], taps_value[:, at], same)
        right = jnp.concatenate(
            [(beta * value).astype(BF16), (beta * carried * key).astype(BF16)], axis=1
        )
        solved = dot(inverse_ref[h], right).astype(BF16)
        solved_ref[h] = solved
        last = jnp.exp(gain[rows - 1 : rows, :] - gain) * last_same
        ended = dot((last * key).T.astype(BF16), solved)
        forward = ended[:, :HEAD].astype(BF16)
        transition = (carried[rows - 1 : rows, :] * square - ended[:, HEAD:]).astype(BF16)
        ours = (core == 0) if h < half else (core != 0)
        place = h % half

        @pl.when(ours)
        def _():
            mine_ref[0, place] = transition
            mine_ref[1, place] = forward

        @pl.when(jnp.logical_not(ours))
        def _():
            send_ref[0, place] = transition
            send_ref[1, place] = forward


def respond_kernel(
    where_ref,
    lengths_ref,
    query_ref,
    tail_ref,
    taps_query,
    decay_ref,
    keys,
    solved_ref,
    base_ref,
    response_ref,
):
    rows = query_ref.shape[0]
    heads = decay_ref.shape[1]
    key_heads = query_ref.shape[1] // HEAD
    repeat = heads // key_heads
    segment, same, inside, carries = masks(where_ref[0], document_ends(lengths_ref), rows)
    inside = inside & (iota((rows, rows), 0) >= iota((rows, rows), 1))
    down, across = cumulated(decay_ref)
    for kh in range(key_heads):
        at = column_of(kh)
        query = unit(
            convolve(query_ref[:, at], tail_ref[:, at], taps_query[:, at], same), HEAD**-0.5
        )
        cross = dot(query.astype(BF16), keys[kh], ((1,), (1,)))
        for h in range(kh * repeat, (kh + 1) * repeat):
            mixing = (between(down, across, h, inside) * cross).astype(BF16)
            mixed = dot(mixing, solved_ref[h])
            carried = jnp.exp(down[:, h : h + 1]) * carries
            base_ref[:, column_of(h)] = mixed[:, :HEAD]
            response_ref[:, column_of(h)] = (carried * query - mixed[:, HEAD:]).astype(BF16)


def gate_kernel(zgate_ref, gain_ref, gate_ref):
    for start in range(0, zgate_ref.shape[1], HEAD):
        at = slice(start, start + HEAD)
        gate_ref[:, at] = silu(zgate_ref[:, at].astype(F32)) * gain_ref[...]


def chip_kernel(where_ref, mine_ref, other_ref, chip_ref):
    core = where_ref[1]

    def compose(early, late):
        for h in range(mine_ref.shape[1]):
            left = late[0, h]
            chip_ref[0, h] = dot(left, early[0, h]).astype(BF16)
            chip_ref[1, h] = (dot(left, early[1, h]) + late[1, h].astype(F32)).astype(BF16)

    @pl.when(core == 0)
    def _():
        compose(mine_ref, other_ref)

    @pl.when(core != 0)
    def _():
        compose(other_ref, mine_ref)


def pair_kernel(chip_ref, before_ref, pair_ref, forward_ref):
    for h in range(chip_ref.shape[1]):
        left = chip_ref[0, h]
        pair_ref[0, h] = dot(left, before_ref[0, h]).astype(BF16)
        forward = (dot(left, before_ref[1, h]) + chip_ref[1, h].astype(F32)).astype(BF16)
        pair_ref[1, h] = forward
        forward_ref[h] = forward


def enter_kernel(where_ref, near_ref, far_ref, mine_ref, other_ref, keep_ref, send_ref):
    core = where_ref[1]
    for h in range(far_ref.shape[0]):
        entering = dot(near_ref[0, h], far_ref[h]) + near_ref[1, h].astype(F32)
        entering_low = entering.astype(BF16)

        @pl.when(core == 0)
        def _():
            keep_ref[h] = entering_low
            later = dot(mine_ref[0, h], entering_low) + mine_ref[1, h].astype(F32)
            send_ref[h] = later.astype(BF16)

        @pl.when(core != 0)
        def _():
            send_ref[h] = entering_low
            later = dot(other_ref[0, h], entering_low) + other_ref[1, h].astype(F32)
            keep_ref[h] = later.astype(BF16)


def finish_kernel(
    where_ref, base_ref, response_ref, keep_ref, other_ref, gate_ref, w_out, term_ref, gated_ref, state_ref
):
    core = where_ref[1]
    half = keep_ref.shape[0]

    @pl.when(core == 0)
    def _():
        state_ref[:half] = keep_ref[...]
        state_ref[half:] = other_ref[...]

    @pl.when(core != 0)
    def _():
        state_ref[:half] = other_ref[...]
        state_ref[half:] = keep_ref[...]

    for h in range(2 * half):
        at = column_of(h)
        attended = base_ref[:, at] + dot(response_ref[:, at], state_ref[h])
        scale = lax.rsqrt(jnp.mean(attended * attended, axis=-1, keepdims=True) + 1e-06)
        gated_ref[:, at] = (attended * scale * gate_ref[:, at]).astype(BF16)
    gated = gated_ref[...]
    width = term_ref.shape[2]
    for part in range(term_ref.shape[0]):
        term_ref[part] = dot(gated, w_out[:, part * width : (part + 1) * width]).astype(BF16)


def out(*shape, dtype=BF16):
    return jax.ShapeDtypeStruct(shape, dtype)


def turned(value, axis, steps):
    count = lax.axis_size(axis)
    return lax.ppermute(value, axis, [(at, (at + steps) % count) for at in range(count)])


def swapped(value, axis):
    count = lax.axis_size(axis)
    return lax.ppermute(value, axis, [(at, at ^ 1) for at in range(count)])


def after(value, *others):
    return lax.optimization_barrier((value, *others))[0]


def hbm(value):
    return pltpu.with_memory_space_constraint(value, pltpu.HBM)


def vmem(value):
    return pltpu.with_memory_space_constraint(value, pltpu.VMEM)


def call(kernel, name, outs, ins, mib, *, scratch=(), cost=2_000_000, inputs=None):
    single = not isinstance(outs, tuple)
    outs = (outs,) if single else outs
    got = pl.pallas_call(
        kernel,
        out_shape=outs,
        in_specs=[VMEM] * len(ins) if inputs is None else inputs,
        out_specs=(VMEM,) * len(outs),
        scratch_shapes=list(scratch),
        compiler_params=params(mib),
        cost_estimate=pl.CostEstimate(flops=0, bytes_accessed=cost, transcendentals=0),
        name=name,
    )(*ins)
    return got[0] if single else got


def local(
    tokens,
    order,
    doc_lengths,
    w_query,
    w_key,
    w_value,
    w_zgate,
    w_beta,
    w_alpha,
    conv_query,
    conv_key,
    conv_value,
    decay_log,
    decay_bias,
    norm_gain,
    w_out,
):
    rows, width = tokens.shape
    shards = lax.axis_size("seq")
    groups = lax.axis_size("head")
    capacity = 2 * rows // shards
    slots = shards * capacity
    qk, vw, heads = w_query.shape[1], w_value.shape[1], w_beta.shape[1]
    half, key_heads = heads // 2, qk // HEAD
    index = lax.axis_index("seq")
    where = jnp.stack([index * rows, index % 2]).astype(jnp.int32)

    send = call(
        lambda *refs: pack_kernel(shards, *refs),
        "pack",
        out(slots, width + LANES),
        (order.reshape(1, rows), hbm(tokens)),
        16,
    )
    weights = (w_key, w_value, w_query, w_zgate, w_out)
    weights = [hbm(after(weight, send)) for weight in weights]
    w_key, w_value, w_query, w_zgate, w_out = call(
        fetch_kernel,
        "fetch",
        tuple(pltpu.VMEM(weight.shape, weight.dtype) for weight in weights),
        weights,
        2,
        scratch=[pltpu.SemaphoreType.DMA((FETCHES * len(weights),))],
        inputs=[ANY] * len(weights),
        cost=20_000_000,
    )
    got = lax.all_to_all(
        send.reshape(shards, capacity, width + LANES), "seq", split_axis=0, concat_axis=0, tiled=True
    ).reshape(slots, width + LANES)
    balanced, key, value, tail, beta, decay = call(
        project_kernel,
        "project",
        (
            out(rows, width),
            out(rows, qk),
            out(rows, vw),
            out(TAIL, qk + vw),
            out(rows, heads, dtype=F32),
            out(rows, heads, dtype=F32),
        ),
        (
            vmem(got),
            vmem(w_key),
            vmem(w_value),
            w_beta.T,
            w_alpha.T,
            decay_log.reshape(1, heads),
            decay_bias.reshape(1, heads),
        ),
        16,
    )
    tail_got = turned(tail, "seq", 1)
    query, zgate, query_tail = call(
        project_more_kernel,
        "project_more",
        (out(rows, qk), out(rows, vw), out(TAIL, qk)),
        (balanced, vmem(w_query), vmem(w_zgate)),
        12,
    )
    tail_got, query = lax.optimization_barrier((tail_got, query))
    query_tail_got = turned(query_tail, "seq", 1)
    states = out(2, half, HEAD, HEAD)
    mine, sent, keys, solved = call(
        chunk_kernel,
        "chunk",
        (states, states, out(key_heads, rows, HEAD), out(heads, rows, 2 * HEAD)),
        (where, doc_lengths, key, value, tail_got, conv_key, conv_value, beta, decay),
        20,
        scratch=[
            pltpu.VMEM((heads, rows, rows), BF16),
            pltpu.VMEM((heads, rows, rows), BF16),
            pltpu.VMEM((rows.bit_length() - 1, rows, rows), BF16),
        ],
        inputs=[SMEM] * 2 + [VMEM] * 7,
    )
    other = swapped(sent, "seq")
    chip = call(
        chip_kernel, "chip", states, (where, mine, other), 4, inputs=[SMEM, VMEM, VMEM]
    )
    before = turned(chip, "seq", 2)
    base, response = call(
        respond_kernel,
        "respond",
        (out(rows, vw, dtype=F32), out(rows, vw)),
        (where, doc_lengths, after(query, chip), query_tail_got, conv_query, decay, keys, solved),
        16,
        inputs=[SMEM] * 2 + [VMEM] * 6,
        cost=16_000_000,
    )
    base, before = lax.optimization_barrier((base, before))
    pair_out = (states, out(half, HEAD, HEAD))
    pair, pair_forward = call(pair_kernel, "pair", pair_out, (chip, before), 4)
    near, far = turned(pair, "seq", 2), turned(pair_forward, "seq", 6)
    gate = call(
        gate_kernel,
        "gate",
        out(rows, vw, dtype=F32),
        (after(zgate, pair), norm_gain.reshape(1, HEAD)),
        8,
        cost=10_000_000,
    )
    gate, near, far = lax.optimization_barrier((gate, near, far))
    state = out(half, HEAD, HEAD)
    keep, give = call(
        enter_kernel,
        "enter",
        (state, state),
        (where, near, far, mine, other),
        4,
        inputs=[SMEM] + [VMEM] * 4,
    )
    term = call(
        finish_kernel,
        "finish",
        out(groups, rows, width // groups),
        (where, base, response, keep, swapped(give, "seq"), gate, vmem(w_out)),
        16,
        scratch=[pltpu.VMEM((rows, vw), BF16), pltpu.VMEM((heads, HEAD, HEAD), BF16)],
        inputs=[SMEM] + [VMEM] * 6,
    )
    here = lax.axis_index("head")
    mixed = lax.dynamic_index_in_dim(term, here, 0, keepdims=False).astype(F32)
    for steps in (2, 1, 3):
        leaving = lax.dynamic_index_in_dim(term, (here + steps) % groups, 0, keepdims=False)
        mixed = mixed + turned(leaving, "head", steps).astype(F32)
    return mixed.astype(BF16)


def solution(mesh):
    return jax.shard_map(
        local,
        mesh=mesh,
        in_specs=(
            P("seq", None),
            P("seq"),
            P(),
            P(None, "head"),
            P(None, "head"),
            P(None, "head"),
            P(None, "head"),
            P(None, "head"),
            P(None, "head"),
            P(None, "head"),
            P(None, "head"),
            P(None, "head"),
            P("head"),
            P("head"),
            P(),
            P("head", None),
        ),
        out_specs=P("seq", "head"),
        check_vma=False,
    )
```

time: 137 us -> 123 us (0.90)
  the two profiles are of different devices: /device:TPU:64 before, /device:TPU:1 now
where the time goes in v2:
time: 123 us; the launch traced here: 121 us
  waiting for transfers between devices  44.6 us (36%)
  Pallas kernels  31.1 us (25%)
  starting transfers between devices  26.6 us (22%)
  local copies, waits for them, and re-layouts  17.8 us (14%)
    pallas_call x11, Pallas kernels, call(): pl.pallas_call(kernel, out_shape=outs, in_specs=[VMEM] * len(ins) if inpu...  31.1 us
    ppermute x8, waiting for transfers between devices, turned(): lax.ppermute(value, axis, [(at, (at + steps) % count) for at in range(cou...  27.9 us
    unnamed x46, local copies, waits for them, and re-layouts  17.8 us
    all_to_all x1, waiting for transfers between devices, local(): lax.all_to_all(send.reshape(shards, capacity, width + LANES), 'seq', spli...  14.5 us
    ppermute x2, starting transfers between devices, swapped(): return lax.ppermute(value, axis, [(at, at ^ 1) for at in range(count)])  10.6 us
    all_to_all x1, starting transfers between devices, local(): lax.all_to_all(send.reshape(shards, capacity, width + LANES), 'seq', spli...  9.43 us
    ppermute x8, starting transfers between devices, turned(): lax.ppermute(value, axis, [(at, (at + steps) % count) for at in range(cou...  6.58 us
  transfers between devices with their start and end apart: 11, of which 9 were waited for; matrix products, arithmetic and copies ran while one was open for 0% of the time, Pallas kernels for 9%

profile of v2, /device:TPU:1, one launch (start us, length us, event | category | flops | bytes accessed | tf_op | source)
XLA Modules:
  0.0 121.4 jit_solution(782282059656679020)
XLA Ops:
  0.7 2.1 %pack.1 = bf16[512,2176]{1,0:T(8,128)(2,1)S(1)} custom-call(s32[1,256]{1,0:T(1,128)S(1)} %bitcast.23, bf16[256,2048]{1,0:T(8,128)(2,1)} %refs_1_.1), custom_call_target="tpu_custom_call" | custom-call | bytes 2000000 | tf_op jit(solution)/shard_map/pack/pallas_call | solution.py:413
  4.2 9.4 %all-to-all-start = ((bf16[32,16,2176]{2,1,0:T(8,128)(2,1)}), bf16[32,16,2176]{2,1,0:T(8,128)(2,1)S(1)}, u32[]{:S(2)}, u32[]{:S(2)}) async-start(bf16[32,16,2176]{2,1,0:T(8,128)(2,1)} %bitcast.20), calls=%async_computation | async-start | bytes 4456448 | tf_op jit(solution)/shard_map/all_to_all | solution.py:473
  13.7 6.0 %fetch.1 = (bf16[2048,512]{1,0:T(8,128)(2,1)S(1)}, bf16[2048,1024]{1,0:T(8,128)(2,1)S(1)}, bf16[2048,512]{1,0:T(8,128)(2,1)S(1)}, bf16[2048,1024]{1,0:T(8,128)(2,1)S(1)}, bf16[1024,2048]{1,0:T(8,128)(2,1)S(1)}) custom-call(bf16[2048,512]{1,0:T(8,128)(2,1)} %refs_0_, bf16[2048,1024]{1,0:T(8,128)(2,1)} %refs_1_.2, bf16[2048,512]{1,0:T(8,128)(2,1)} %refs_2_, ...), custom_call_target="tpu_custom_call" | custom-call | bytes 20000000 | tf_op jit(solution)/shard_map/fetch/pallas_call | solution.py:413
  19.7 2.0 %copy-done.1 = bf16[2048,1024]{1,0:T(8,128)(2,1)} copy-done((bf16[2048,1024]{1,0:T(8,128)(2,1)}, bf16[2048,1024]{1,0:T(8,128)(2,1)S(1)}, u32[]{:S(2)}) %copy-start.1) | copy-done | bytes 4194328
  21.7 2.0 %copy-done.3 = bf16[1024,2048]{1,0:T(8,128)(2,1)} copy-done((bf16[1024,2048]{1,0:T(8,128)(2,1)}, bf16[1024,2048]{1,0:T(8,128)(2,1)S(1)}, u32[]{:S(2)}) %copy-start.3) | copy-done | bytes 4194328
  23.7 2.0 %copy-done.5 = bf16[2048,1024]{1,0:T(8,128)(2,1)} copy-done((bf16[2048,1024]{1,0:T(8,128)(2,1)}, bf16[2048,1024]{1,0:T(8,128)(2,1)S(1)}, u32[]{:S(2)}) %copy-start.5) | copy-done | bytes 4194328
  28.4 14.5 %all-to-all-done = bf16[32,16,2176]{2,1,0:T(8,128)(2,1)S(1)} async-done(((bf16[32,16,2176]{2,1,0:T(8,128)(2,1)}), bf16[32,16,2176]{2,1,0:T(8,128)(2,1)S(1)}, u32[]{:S(2)}, u32[]{:S(2)}) %all-to-all-start) | async-done | bytes 2228256 | tf_op jit(solution)/shard_map/all_to_all | solution.py:473
  42.9 2.2 %copy-done.6 = bf16[2048,1024]{1,0:T(8,128)(2,1)S(1)} copy-done((bf16[2048,1024]{1,0:T(8,128)(2,1)S(1)}, bf16[2048,1024]{1,0:T(8,128)(2,1)}, u32[]{:S(2)}) %copy-start.6) | copy-done | bytes 4194328
  46.7 3.1 %project.1 = (bf16[256,2048]{1,0:T(8,128)(2,1)S(1)}, bf16[256,512]{1,0:T(8,128)(2,1)S(1)}, bf16[256,1024]{1,0:T(8,128)(2,1)S(1)}, bf16[16,1536]{1,0:T(8,128)(2,1...) custom-call(bf16[512,2176]{1,0:T(8,128)(2,1)S(1)} %bitcast.19, bf16[2048,512]{1,0:T(8,128)(2,1)S(1)} %copy-done.10, ...), custom_call_target="tpu_custom_call" | custom-call | bytes 2000000 | tf_op jit(solution)/shard_map/project/pallas_call | solution.py:413
  49.8 1.8 %collective-permute-start = (bf16[16,1536]{1,0:T(8,128)(2,1)S(1)}, bf16[16,1536]{1,0:T(8,128)(2,1)S(1)}, u32[]{:S(2)}, u32[]{:S(2)}) collective-permute-start(bf16[16,1536]{1,0:T(8,128)(2,1)S(1)} %get-tuple-element.50), channel_id=1, source_target_pairs={{0,4},{4,8},{8,12},{12,16},{16,20},{20,24},{24,28},{28,32},{32,36}... | collective-permute-start | bytes 147464 | tf_op jit(solution)/shard_map/ppermute | solution.py:390
  51.7 1.8 %project_more.1 = (bf16[256,512]{1,0:T(8,128)(2,1)S(1)}, bf16[256,1024]{1,0:T(8,128)(2,1)S(1)}, bf16[16,512]{1,0:T(8,128)(2,1)S(1)}) custom-call(bf16[256,2048]{1,0:T(8,128)(2,1)S(1)} %get-tuple-element.51.balanced_ref, bf16[2048,512]{1,0:T(8,128)(2,1)S(1)} %copy-done.8, bf16[2048,1024]{1,0:T(8,128)(2,1)S(1)} %copy-done.2), custom_call_target="tpu_custom_call" | custom-call | bytes 2000000 | tf_op jit(solution)/shard_map/project_more/pallas_call | solution.py:413
  53.5 10.3 %chunk.1 = (bf16[2,4,128,128]{3,2,1,0:T(8,128)(2,1)S(1)}, bf16[2,4,128,128]{3,2,1,0:T(8,128)(2,1)S(1)}, bf16[4,256,128]{2,1,0:T(8,128)(2,1)S(1)}, bf16[8,256,256]{2,1,0:T(8,128)(2,1)S(1)}) custom-call(s32[2]{0:T(128)S(1)} %pad_add_fusion.where_ref, s32[8]{0:T(128)S(1)} %copy-done.18, bf16[256,512]{1,0:T(8,128)(2,1)S(1)} %get-tuple-element.56.key_ref, ...), custom_call_target="tpu_custom_call" | custom-call | bytes 2000000 | tf_op jit(solution)/shard_map/chunk/pallas_call | solution.py:413
  63.8 5.8 %collective-permute-start.1 = (bf16[2,4,128,128]{3,2,1,0:T(8,128)(2,1)S(1)}, bf16[2,4,128,128]{3,2,1,0:T(8,128)(2,1)S(1)}, u32[]{:S(2)}, u32[]{:S(2)}) collective-permute-start(bf16[2,4,128,128]{3,2,1,0:T(8,128)(2,1)S(1)} %get-tuple-element.62), channel_id=1, source_target_pairs={{0,4},{4,0},{8,12},{12,8},{16,20},{20,16},{24,28},{28,24},{32,36},... | collective-permute-start | bytes 786440 | tf_op jit(solution)/shard_map/ppermute | solution.py:395
  71.7 5.9 %collective-permute-done.2.tail_ref = bf16[16,512]{1,0:T(8,128)(2,1)S(1)} collective-permute-done((bf16[16,512]{1,0:T(8,128)(2,1)S(1)}, bf16[16,512]{1,0:T(8,128)(2,1)S(1)}, u32[]{:S(2)}, u32[]{:S(2)}) %collective-permute-start.2) | collective-permute-done | bytes 16416 | tf_op jit(solution)/shard_map/ppermute | solution.py:390
  77.6 2.8 %respond.1 = (f32[256,1024]{1,0:T(8,128)S(1)}, bf16[256,1024]{1,0:T(8,128)(2,1)S(1)}) custom-call(s32[2]{0:T(128)S(1)} %pad_add_fusion.where_ref, s32[8]{0:T(128)S(1)} %copy-done.18, bf16[256,512]{1,0:T(8,128)(2,1)S(1)} %get-tuple-element.63.query_ref, bf16[16,512]{1,0:T(8,128)(2,1)S(1)} %collective-permute-done.2.tail_ref, bf16[4,512]{1,0:T(4,128)(2,1)S(1)} %copy-done.17, ...), custom_call_target="tpu_custom_call" | custom-call | bytes 16000000 | tf_op jit(solution)/shard_map/respond/pallas_call | solution.py:413
  80.4 2.0 %collective-permute-done.3.before_ref = bf16[2,4,128,128]{3,2,1,0:T(8,128)(2,1)S(1)} collective-permute-done((bf16[2,4,128,128]{3,2,1,0:T(8,128)(2,1)S(1)}, bf16[2,4,128,128]{3,2,1,0:T(8,128)(2,1)S(1)}, u32[]{:S(2)}, u32[]{:S(2)}) %collective-permute-start.3) | collective-permute-done | bytes 262176 | tf_op jit(solution)/shard_map/ppermute | solution.py:390
  83.1 5.9 %collective-permute-done.5.far_ref = bf16[4,128,128]{2,1,0:T(8,128)(2,1)S(1)} collective-permute-done((bf16[4,128,128]{2,1,0:T(8,128)(2,1)S(1)}, bf16[4,128,128]{2,1,0:T(8,128)(2,1)S(1)}, u32[]{:S(2)}, u32[]{:S(2)}) %collective-permute-start.5) | collective-permute-done | bytes 131104 | tf_op jit(solution)/shard_map/ppermute | solution.py:390
  89.0 2.7 %collective-permute-done.4.near_ref = bf16[2,4,128,128]{3,2,1,0:T(8,128)(2,1)S(1)} collective-permute-done((bf16[2,4,128,128]{3,2,1,0:T(8,128)(2,1)S(1)}, bf16[2,4,128,128]{3,2,1,0:T(8,128)(2,1)S(1)}, u32[]{:S(2)}, u32[]{:S(2)}) %collective-permute-start.4) | collective-permute-done | bytes 262176 | tf_op jit(solution)/shard_map/ppermute | solution.py:390
  93.3 4.8 %collective-permute-start.6 = (bf16[4,128,128]{2,1,0:T(8,128)(2,1)S(1)}, bf16[4,128,128]{2,1,0:T(8,128)(2,1)S(1)}, u32[]{:S(2)}, u32[]{:S(2)}) collective-permute-start(bf16[4,128,128]{2,1,0:T(8,128)(2,1)S(1)} %get-tuple-element.78), channel_id=1, source_target_pairs={{0,4},{4,0},{8,12},{12,8},{16,20},{20,16},{24,28},{28,24},{32,36},... | collective-permute-start | bytes 393224 | tf_op jit(solution)/shard_map/ppermute | solution.py:395
  99.2 2.2 %copy-done.4 = bf16[1024,2048]{1,0:T(8,128)(2,1)S(1)} copy-done((bf16[1024,2048]{1,0:T(8,128)(2,1)S(1)}, bf16[1024,2048]{1,0:T(8,128)(2,1)}, u32[]{:S(2)}) %copy-start.4) | copy-done | bytes 4194328
  102.4 2.2 %finish.1 = bf16[4,256,512]{2,1,0:T(8,128)(2,1)S(1)} custom-call(s32[2]{0:T(128)S(1)} %pad_add_fusion.where_ref, f32[256,1024]{1,0:T(8,128)S(1)} %get-tuple-element.68.base_ref, bf16[256,1024]{1,0:T(8,128)(2,1)S(1)} %copy-done.12, bf16[4,128,128]{2,1,0:T(8,128)(2,1)S(1)} %get-tuple-element.77.keep_ref, ...), custom_call_target="tpu_custom_call" | custom-call | bytes 2000000 | tf_op jit(solution)/shard_map/finish/pallas_call | solution.py:413
  104.6 2.8 %collective-permute-start.9 = (bf16[256,512]{1,0:T(8,128)(2,1)S(1)}, bf16[256,512]{1,0:T(8,128)(2,1)S(1)}, u32[]{:S(2)}, u32[]{:S(2)}) collective-permute-start(bf16[256,512]{1,0:T(8,128)(2,1)S(1)} %get-tuple-element.82), channel_id=1, source_target_pairs={{0,3},{1,0},{2,1},{3,2},{4,7},{5,4},{6,5},{7,6},{8,11},{9,8},{10,9... | collective-permute-start | bytes 786440 | tf_op jit(solution)/shard_map/ppermute | solution.py:390
  109.1 9.2 %collective-permute-done.9 = bf16[256,512]{1,0:T(8,128)(2,1)S(1)} collective-permute-done((bf16[256,512]{1,0:T(8,128)(2,1)S(1)}, bf16[256,512]{1,0:T(8,128)(2,1)S(1)}, u32[]{:S(2)}, u32[]{:S(2)}) %collective-permute-start.9) | collective-permute-done | bytes 262176 | tf_op jit(solution)/shard_map/ppermute | solution.py:390
  118.3 2.2 %collective-permute-done.7 = bf16[256,512]{1,0:T(8,128)(2,1)S(1)} collective-permute-done((bf16[256,512]{1,0:T(8,128)(2,1)S(1)}, bf16[256,512]{1,0:T(8,128)(2,1)S(1)}, u32[]{:S(2)}, u32[]{:S(2)}) %collective-permute-start.7) | collective-permute-done | bytes 262176 | tf_op jit(solution)/shard_map/ppermute | solution.py:390
  (58 shorter events, 15.3 us)
Async XLA Ops:
  4.2 38.7 %all-to-all-start = ((bf16[32,16,2176]{2,1,0:T(8,128)(2,1)}), bf16[32,16,2176]{2,1,0:T(8,128)(2,1)S(1)}, u32[]{:S(2)}, u32[]{:S(2)}) async-start(bf16[32,16,2176]{2,1,0:T(8,128)(2,1)} %bitcast.20), calls=%async_computation | async-start | bytes 4456448 | tf_op jit(solution)/shard_map/all_to_all | solution.py:473
  13.6 29.3 %copy-start.13 = (bf16[2048,8]{0,1:T(8,128)(2,1)S(1)}, bf16[2048,8]{0,1:T(8,128)(2,1)}, u32[]{:S(2)}) copy-start(bf16[2048,8]{0,1:T(8,128)(2,1)} %param.23) | copy-start | bytes 98308
  13.6 29.2 %copy-start.14 = (bf16[2048,8]{0,1:T(8,128)(2,1)S(1)}, bf16[2048,8]{0,1:T(8,128)(2,1)}, u32[]{:S(2)}) copy-start(bf16[2048,8]{0,1:T(8,128)(2,1)} %param.24) | copy-start | bytes 98308
  13.6 29.2 %copy-start.20 = (f32[8]{0:T(128)S(1)}, f32[8]{0:T(128)}, u32[]{:S(2)}) copy-start(f32[8]{0:T(128)} %param.28) | copy-start | bytes 100
  13.6 29.2 %copy-start.21 = (f32[8]{0:T(128)S(1)}, f32[8]{0:T(128)}, u32[]{:S(2)}) copy-start(f32[8]{0:T(128)} %param.29) | copy-start | bytes 100
  42.9 2.2 %copy-start.6 = (bf16[2048,1024]{1,0:T(8,128)(2,1)S(1)}, bf16[2048,1024]{1,0:T(8,128)(2,1)}, u32[]{:S(2)}) copy-start(bf16[2048,1024]{1,0:T(8,128)(2,1)} %copy-done.5) | copy-start | bytes 12582916
  46.7 5.0 %copy-start.2 = (bf16[2048,1024]{1,0:T(8,128)(2,1)S(1)}, bf16[2048,1024]{1,0:T(8,128)(2,1)}, u32[]{:S(2)}) copy-start(bf16[2048,1024]{1,0:T(8,128)(2,1)} %copy-done.1) | copy-start | bytes 12582916
  46.7 5.0 %copy-start.8 = (bf16[2048,512]{1,0:T(8,128)(2,1)S(1)}, bf16[2048,512]{1,0:T(8,128)(2,1)}, u32[]{:S(2)}) copy-start(bf16[2048,512]{1,0:T(8,128)(2,1)} %copy-done.7) | copy-start | bytes 6291460
  49.8 3.8 %copy-start.15 = (bf16[4,1024]{1,0:T(4,128)(2,1)S(1)}, bf16[4,1024]{1,0:T(4,128)(2,1)}, u32[]{:S(2)}) copy-start(bf16[4,1024]{1,0:T(4,128)(2,1)} %taps_value.1) | copy-start | bytes 24580
  49.8 3.8 %copy-start.16 = (bf16[4,512]{1,0:T(4,128)(2,1)S(1)}, bf16[4,512]{1,0:T(4,128)(2,1)}, u32[]{:S(2)}) copy-start(bf16[4,512]{1,0:T(4,128)(2,1)} %taps_key.1) | copy-start | bytes 12292
  49.8 3.8 %copy-start.18 = (s32[8]{0:T(128)S(1)}, s32[8]{0:T(128)}, u32[]{:S(2)}) copy-start(s32[8]{0:T(128)} %lengths_ref.3) | copy-start | bytes 100
  49.8 3.7 %collective-permute-start = (bf16[16,1536]{1,0:T(8,128)(2,1)S(1)}, bf16[16,1536]{1,0:T(8,128)(2,1)S(1)}, u32[]{:S(2)}, u32[]{:S(2)}) collective-permute-start(bf16[16,1536]{1,0:T(8,128)(2,1)S(1)} %get-tuple-element.50), channel_id=1, source_target_pairs={{0,4},{4,8},{8,12},{12,16},{16,20},{20,24},{24,28},{28,32},{32,36}... | collective-permute-start | bytes 147464 | tf_op jit(solution)/shard_map/ppermute | solution.py:390
  51.7 25.9 %copy-start.17 = (bf16[4,512]{1,0:T(4,128)(2,1)S(1)}, bf16[4,512]{1,0:T(4,128)(2,1)}, u32[]{:S(2)}) copy-start(bf16[4,512]{1,0:T(4,128)(2,1)} %taps_query.1) | copy-start | bytes 12292
  51.7 31.1 %copy-start.22 = (f32[128]{0:T(128)S(1)}, f32[128]{0:T(128)}, u32[]{:S(2)}) copy-start(f32[128]{0:T(128)} %param.30) | copy-start | bytes 1540
  63.8 6.9 %collective-permute-start.1 = (bf16[2,4,128,128]{3,2,1,0:T(8,128)(2,1)S(1)}, bf16[2,4,128,128]{3,2,1,0:T(8,128)(2,1)S(1)}, u32[]{:S(2)}, u32[]{:S(2)}) collective-permute-start(bf16[2,4,128,128]{3,2,1,0:T(8,128)(2,1)S(1)} %get-tuple-element.62), channel_id=1, source_target_pairs={{0,4},{4,0},{8,12},{12,8},{16,20},{20,16},{24,28},{28,24},{32,36},... | collective-permute-start | bytes 786440 | tf_op jit(solution)/shard_map/ppermute | solution.py:395
  71.5 10.9 %collective-permute-start.3 = (bf16[2,4,128,128]{3,2,1,0:T(8,128)(2,1)S(1)}, bf16[2,4,128,128]{3,2,1,0:T(8,128)(2,1)S(1)}, u32[]{:S(2)}, u32[]{:S(2)}) collective-permute-start(bf16[2,4,128,128]{3,2,1,0:T(8,128)(2,1)S(1)} %chip.1.chip_ref), channel_id=1, source_target_pairs={{0,8},{4,12},{8,16},{12,20},{16,24},{20,28},{24,32},{28,36},{32,40... | collective-permute-start | bytes 786440 | tf_op jit(solution)/shard_map/ppermute | solution.py:390
  71.6 6.0 %collective-permute-start.2 = (bf16[16,512]{1,0:T(8,128)(2,1)S(1)}, bf16[16,512]{1,0:T(8,128)(2,1)S(1)}, u32[]{:S(2)}, u32[]{:S(2)}) collective-permute-start(bf16[16,512]{1,0:T(8,128)(2,1)S(1)} %get-tuple-element.64), channel_id=1, source_target_pairs={{0,4},{4,8},{8,12},{12,16},{16,20},{20,24},{24,28},{28,32},{32,36}... | collective-permute-start | bytes 49160 | tf_op jit(solution)/shard_map/ppermute | solution.py:390
  80.4 12.9 %copy-start.11 = (bf16[256,1024]{1,0:T(8,128)(2,1)}, bf16[256,1024]{1,0:T(8,128)(2,1)S(1)}, u32[]{:S(2)}) copy-start(bf16[256,1024]{1,0:T(8,128)(2,1)S(1)} %get-tuple-element.69.response_ref) | copy-start | bytes 1572868
  82.7 9.0 %collective-permute-start.4 = (bf16[2,4,128,128]{3,2,1,0:T(8,128)(2,1)S(1)}, bf16[2,4,128,128]{3,2,1,0:T(8,128)(2,1)S(1)}, u32[]{:S(2)}, u32[]{:S(2)}) collective-permute-start(bf16[2,4,128,128]{3,2,1,0:T(8,128)(2,1)S(1)} %get-tuple-element.72), channel_id=1, source_target_pairs={{0,8},{4,12},{8,16},{12,20},{16,24},{20,28},{24,32},{28,36},{32,40... | collective-permute-start | bytes 786440 | tf_op jit(solution)/shard_map/ppermute | solution.py:390
  82.7 6.3 %collective-permute-start.5 = (bf16[4,128,128]{2,1,0:T(8,128)(2,1)S(1)}, bf16[4,128,128]{2,1,0:T(8,128)(2,1)S(1)}, u32[]{:S(2)}, u32[]{:S(2)}) collective-permute-start(bf16[4,128,128]{2,1,0:T(8,128)(2,1)S(1)} %get-tuple-element.74), channel_id=1, source_target_pairs={{0,24},{4,28},{8,32},{12,36},{16,40},{20,44},{24,48},{28,52},{32,5... | collective-permute-start | bytes 393224 | tf_op jit(solution)/shard_map/ppermute | solution.py:390
  93.3 5.8 %collective-permute-start.6 = (bf16[4,128,128]{2,1,0:T(8,128)(2,1)S(1)}, bf16[4,128,128]{2,1,0:T(8,128)(2,1)S(1)}, u32[]{:S(2)}, u32[]{:S(2)}) collective-permute-start(bf16[4,128,128]{2,1,0:T(8,128)(2,1)S(1)} %get-tuple-element.78), channel_id=1, source_target_pairs={{0,4},{4,0},{8,12},{12,8},{16,20},{20,16},{24,28},{28,24},{32,36},... | collective-permute-start | bytes 393224 | tf_op jit(solution)/shard_map/ppermute | solution.py:395
  104.6 13.6 %collective-permute-start.9 = (bf16[256,512]{1,0:T(8,128)(2,1)S(1)}, bf16[256,512]{1,0:T(8,128)(2,1)S(1)}, u32[]{:S(2)}, u32[]{:S(2)}) collective-permute-start(bf16[256,512]{1,0:T(8,128)(2,1)S(1)} %get-tuple-element.82), channel_id=1, source_target_pairs={{0,3},{1,0},{2,1},{3,2},{4,7},{5,4},{6,5},{7,6},{8,11},{9,8},{10,9... | collective-permute-start | bytes 786440 | tf_op jit(solution)/shard_map/ppermute | solution.py:390
  107.5 10.8 %collective-permute-start.8 = (bf16[256,512]{1,0:T(8,128)(2,1)S(1)}, bf16[256,512]{1,0:T(8,128)(2,1)S(1)}, u32[]{:S(2)}, u32[]{:S(2)}) collective-permute-start(bf16[256,512]{1,0:T(8,128)(2,1)S(1)} %get-tuple-element.83), channel_id=1, source_target_pairs={{0,1},{1,2},{2,3},{3,0},{4,5},{5,6},{6,7},{7,4},{8,9},{9,10},{10,1... | collective-permute-start | bytes 786440 | tf_op jit(solution)/shard_map/ppermute | solution.py:390
  107.5 13.1 %collective-permute-start.7 = (bf16[256,512]{1,0:T(8,128)(2,1)S(1)}, bf16[256,512]{1,0:T(8,128)(2,1)S(1)}, u32[]{:S(2)}, u32[]{:S(2)}) collective-permute-start(bf16[256,512]{1,0:T(8,128)(2,1)S(1)} %get-tuple-element.81), channel_id=1, source_target_pairs={{0,2},{1,3},{2,0},{3,1},{4,6},{5,7},{6,4},{7,5},{8,10},{9,11},{10,... | collective-permute-start | bytes 786440 | tf_op jit(solution)/shard_map/ppermute | solution.py:390
  (10 other events, 15.5 us)

commit v3 on v2

v3 whole, which is shorter than its diff:
```python
import jax
import jax.numpy as jnp
from jax import lax
from jax.experimental import pallas as pl
from jax.experimental.pallas import tpu as pltpu
from jax.sharding import PartitionSpec as P

HEAD = 128
KERNEL = 4
TAIL = 16
LANES = 128
FETCHES = 4
VMEM = pl.BlockSpec(memory_space=pltpu.VMEM)
SMEM = pl.BlockSpec(memory_space=pltpu.SMEM)
ANY = pl.BlockSpec(memory_space=pl.ANY)
F32 = jnp.float32
BF16 = jnp.bfloat16
HIGHEST = lax.Precision.HIGHEST


def iota(shape, axis):
    return lax.broadcasted_iota(jnp.int32, shape, axis)


def dot(left, right, contract=((1,), (0,)), precision=None):
    return lax.dot_general(
        left, right, (contract, ((), ())), precision=precision, preferred_element_type=F32
    )


def params(mib):
    return pltpu.CompilerParams(vmem_limit_bytes=mib << 20)


def pack_kernel(shards, order_ref, tokens_ref, send_ref, part_ref, sem):
    rows, width = part_ref.shape
    slots = send_ref.shape[0]
    capacity = slots // shards
    here = pl.multiple_of(lax.axis_index("head") * width, width)
    copy = pltpu.make_async_copy(tokens_ref.at[:, pl.ds(here, width)], part_ref, sem)
    copy.start()
    order = order_ref[...]
    bits = rows.bit_length() - 1
    target = lax.shift_right_logical(order, jnp.full_like(order, bits))
    landing = lax.bitwise_and(order, jnp.full_like(order, rows - 1))
    marks = (iota((shards, rows), 0) == target).astype(F32)
    before = (iota((rows, rows), 0) < iota((rows, rows), 1)).astype(F32).astype(BF16)
    earlier = dot(marks.astype(BF16), before)
    slot = jnp.sum(earlier * marks, axis=0, keepdims=True).astype(jnp.int32)
    hit = (iota((slots, rows), 0) == target * capacity + slot).astype(F32)
    spot = jnp.sum(hit * (landing + 1).astype(F32), axis=1, keepdims=True)
    send_ref[:, width:] = jnp.broadcast_to(spot, (slots, LANES)).astype(BF16)
    copy.wait()
    send_ref[:, :width] = dot(hit.astype(BF16), part_ref[...]).astype(BF16)


def place_kernel(got_ref, part_ref):
    rows, width = part_ref.shape
    slots = got_ref.shape[0]
    spot = got_ref[:, width : width + 1].astype(F32).astype(jnp.int32)
    hit = (spot == iota((slots, rows), 1) + 1).astype(F32).T.astype(BF16)
    part_ref[...] = dot(hit, got_ref[:, :width]).astype(BF16)


def softplus(x):
    return jnp.maximum(x, 0.0) + jnp.log1p(jnp.exp(-jnp.abs(x)))


def in_parts(source, target, sems, first):
    part = source.shape[0] // FETCHES
    return [
        pltpu.make_async_copy(
            source.at[pl.ds(j * part, part)], target.at[pl.ds(j * part, part)], sems.at[first + j]
        )
        for j in range(FETCHES)
    ]


def fetch_kernel(*refs):
    count = (len(refs) - 1) // 2
    copies = []
    for i, (source, target) in enumerate(zip(refs[:count], refs[count : 2 * count])):
        copies += in_parts(source, target, refs[-1], i * FETCHES)
    for copy in copies:
        copy.start()
    for copy in copies:
        copy.wait()


def project_kernel(
    part0_ref,
    part1_ref,
    part2_ref,
    part3_ref,
    w_query,
    w_key,
    w_value,
    w_beta,
    w_alpha,
    decay_log,
    decay_bias,
    balanced_ref,
    query_ref,
    key_ref,
    value_ref,
    tail_ref,
    beta_ref,
    decay_ref,
):
    rows = balanced_ref.shape[0]
    parts = (part0_ref, part1_ref, part2_ref, part3_ref)
    width = part0_ref.shape[1]
    here = lax.axis_index("head")
    for steps, part in enumerate(parts):
        at = lax.rem(here + len(parts) - steps, len(parts)) * width
        balanced_ref[:, pl.ds(pl.multiple_of(at, width), width)] = part[...]
    balanced = balanced_ref[...]
    across = ((1,), (1,))
    column = 0
    for weight, to in ((w_query, query_ref), (w_key, key_ref), (w_value, value_ref)):
        for start in range(0, to.shape[1], 512):
            part = dot(balanced, weight[:, start : start + 512]).astype(BF16)
            to[:, start : start + 512] = part
            tail_ref[:, column : column + 512] = part[rows - TAIL :]
            column += 512
    beta_ref[...] = jax.nn.sigmoid(dot(balanced, w_beta[...], across))
    decay_ref[...] = -jnp.exp(decay_log[...]) * softplus(
        dot(balanced, w_alpha[...], across) + decay_bias[...]
    )


def project_gate_kernel(balanced_ref, w_zgate, zgate_ref):
    balanced = balanced_ref[...]
    for start in range(0, zgate_ref.shape[1], 512):
        part = dot(balanced, w_zgate[:, start : start + 512])
        zgate_ref[:, start : start + 512] = part.astype(BF16)


def silu(x):
    return x / (1.0 + jnp.exp(-x))


def document_ends(lengths_ref):
    ends, total = [], jnp.int32(0)
    for i in range(lengths_ref.shape[0]):
        total = total + lengths_ref[i]
        ends.append(total)
    return ends


def segments(position, ends):
    count = (position >= 0).astype(jnp.int32) - 1
    for end in ends:
        count = count + (position >= end).astype(jnp.int32)
    return count


def convolve(projected, tail, taps, same):
    extended = jnp.concatenate([tail.astype(F32), projected.astype(F32)], axis=0)
    sums = None
    for lag in range(KERNEL):
        rolled = extended if lag == 0 else pltpu.roll(extended, lag, 0)
        tap = taps[KERNEL - 1 - lag : KERNEL - lag, :].astype(F32)
        term = rolled[TAIL:] * tap
        if lag:
            term = term * same[lag - 1]
        sums = term if sums is None else sums + term
    return silu(sums)


def unit(x, factor):
    return x * (lax.rsqrt(jnp.sum(x * x, axis=-1, keepdims=True) + 1e-06) * factor)


def masks(first, ends, rows):
    position = first + iota((rows, 1), 0)
    segment = segments(position, ends)
    same = [
        (segments(position - lag, ends) == segment).astype(F32) for lag in range(1, KERNEL)
    ]
    inside = segment == segments(first + iota((1, rows), 1), ends)
    before = segments(jnp.full((1, 1), first - 1, jnp.int32), ends)
    carries = (segment == before).astype(F32)
    return segment, same, inside, carries


def cumulated(decay_ref):
    rows, heads = decay_ref.shape
    lower = (iota((rows, rows), 0) >= iota((rows, rows), 1)).astype(F32)
    down = dot(lower, decay_ref[...], precision=HIGHEST)
    padded = jnp.concatenate([down, jnp.zeros((rows, LANES - heads), F32)], axis=1)
    return down, padded.T


def between(down, across, h, inside):
    difference = down[:, h : h + 1] - across[h : h + 1, :]
    return jnp.where(inside, jnp.exp(jnp.where(inside, difference, 0.0)), 0.0)


def my_core():
    return lax.rem(lax.axis_index("seq"), 2)


def column_of(h):
    return slice(h * HEAD, (h + 1) * HEAD)


def chunk_kernel(
    lengths_ref,
    key_ref,
    value_ref,
    tail_ref,
    taps_key,
    taps_value,
    beta_ref,
    decay_ref,
    mine_ref,
    send_ref,
    keys,
    solved_ref,
    system_ref,
    inverse_ref,
    mask_ref,
    states_ref,
    right_ref,
):
    rows = key_ref.shape[0]
    first, core = lax.axis_index("seq") * rows, my_core()
    heads = beta_ref.shape[1]
    key_heads = key_ref.shape[1] // HEAD
    repeat = heads // key_heads
    width = key_ref.shape[1]
    segment, same, inside, carries = masks(first, document_ends(lengths_ref), rows)
    row, column = iota((rows, rows), 0), iota((rows, rows), 1)
    levels = rows.bit_length() - 1
    for level in range(levels):
        size = 1 << level
        apart = (lax.bitwise_xor(row, column) < 2 * size) & (
            lax.bitwise_and(row, size) > lax.bitwise_and(column, size)
        )
        mask_ref[level] = apart.astype(F32).astype(BF16)
    unit_matrix = (row == column).astype(F32)
    strict = inside & (row > column)
    down, across = cumulated(decay_ref)

    for kh in range(key_heads):
        at = column_of(kh)
        keys[kh] = unit(
            convolve(key_ref[:, at], tail_ref[:, column_of(key_heads + kh)], taps_key[:, at], same), 1.0
        ).astype(BF16)
        inner = dot(keys[kh], keys[kh], ((1,), (1,)))
        for h in range(kh * repeat, (kh + 1) * repeat):
            system = beta_ref[:, h : h + 1] * inner * between(down, across, h, strict)
            system_ref[h] = system.astype(BF16)
            inverse_ref[h] = (unit_matrix - system * mask_ref[0].astype(F32)).astype(BF16)
    for h in range(heads):
        at, to = column_of(h), column_of(2 * key_heads + h)
        beta = beta_ref[:, h : h + 1]
        carried = jnp.exp(down[:, h : h + 1]) * carries
        value = convolve(value_ref[:, at], tail_ref[:, to], taps_value[:, at], same)
        right_ref[h, :, :HEAD] = (beta * value).astype(BF16)
        right_ref[h, :, HEAD:] = (beta * carried * keys[h // repeat].astype(F32)).astype(BF16)
    for level in range(1, levels):
        for h in range(heads):
            inverse = inverse_ref[h]
            part = dot(system_ref[h] * mask_ref[level], inverse).astype(BF16)
            inverse_ref[h] = (inverse.astype(F32) - dot(inverse, part)).astype(BF16)

    square = (iota((HEAD, HEAD), 0) == iota((HEAD, HEAD), 1)).astype(F32)
    half = heads // 2
    last_same = (segment == segment[rows - 1 : rows, :]).astype(F32)
    for h in range(heads):
        solved_ref[h] = dot(inverse_ref[h], right_ref[h]).astype(BF16)
    for h in range(heads):
        gain = down[:, h : h + 1]
        last = jnp.exp(gain[rows - 1 : rows, :] - gain) * last_same
        ended = dot((last * keys[h // repeat].astype(F32)).astype(BF16), solved_ref[h], ((0,), (0,)))
        carried = (jnp.exp(gain) * carries)[rows - 1 : rows, :]
        states_ref[0, h] = (carried * square - ended[:, HEAD:]).astype(BF16)
        states_ref[1, h] = ended[:, :HEAD].astype(BF16)

    @pl.when(core == 0)
    def _():
        mine_ref[...] = states_ref[:, :half]
        send_ref[...] = states_ref[:, half:]

    @pl.when(core != 0)
    def _():
        mine_ref[...] = states_ref[:, half:]
        send_ref[...] = states_ref[:, :half]


def chunk_scratch(heads, rows):
    return [
        pltpu.VMEM((heads, rows, rows), BF16),
        pltpu.VMEM((heads, rows, rows), BF16),
        pltpu.VMEM((rows.bit_length() - 1, rows, rows), BF16),
        pltpu.VMEM((2, heads, HEAD, HEAD), BF16),
        pltpu.VMEM((heads, rows, 2 * HEAD), BF16),
    ]


def respond_kernel(
    lengths_ref,
    query_ref,
    tail_ref,
    taps_query,
    decay_ref,
    keys,
    solved_ref,
    base_ref,
    response_ref,
):
    rows = query_ref.shape[0]
    heads = decay_ref.shape[1]
    key_heads = query_ref.shape[1] // HEAD
    repeat = heads // key_heads
    segment, same, inside, carries = masks(
        lax.axis_index("seq") * rows, document_ends(lengths_ref), rows
    )
    inside = inside & (iota((rows, rows), 0) >= iota((rows, rows), 1))
    down, across = cumulated(decay_ref)
    for kh in range(key_heads):
        at = column_of(kh)
        query = unit(
            convolve(query_ref[:, at], tail_ref[:, at], taps_query[:, at], same), HEAD**-0.5
        )
        cross = dot(query.astype(BF16), keys[kh], ((1,), (1,)))
        for h in range(kh * repeat, (kh + 1) * repeat):
            mixing = (between(down, across, h, inside) * cross).astype(BF16)
            mixed = dot(mixing, solved_ref[h])
            carried = jnp.exp(down[:, h : h + 1]) * carries
            base_ref[:, column_of(h)] = mixed[:, :HEAD]
            response_ref[:, column_of(h)] = (carried * query - mixed[:, HEAD:]).astype(BF16)


def gate_kernel(zgate_ref, gain_ref, w_out, gate_ref, out_ref, sems):
    copies = in_parts(w_out, out_ref, sems, 0)
    for copy in copies:
        copy.start()
    for start in range(0, zgate_ref.shape[1], HEAD):
        at = slice(start, start + HEAD)
        gate_ref[:, at] = silu(zgate_ref[:, at].astype(F32)) * gain_ref[...]
    for copy in copies:
        copy.wait()


def chip_kernel(mine_ref, other_ref, chip_ref):
    core = my_core()

    def compose(early, late):
        for h in range(mine_ref.shape[1]):
            left = late[0, h]
            chip_ref[0, h] = dot(left, early[0, h]).astype(BF16)
            chip_ref[1, h] = (dot(left, early[1, h]) + late[1, h].astype(F32)).astype(BF16)

    @pl.when(core == 0)
    def _():
        compose(mine_ref, other_ref)

    @pl.when(core != 0)
    def _():
        compose(other_ref, mine_ref)


def pair_kernel(chip_ref, before_ref, pair_ref, forward_ref):
    for h in range(chip_ref.shape[1]):
        left = chip_ref[0, h]
        pair_ref[0, h] = dot(left, before_ref[0, h]).astype(BF16)
        forward = (dot(left, before_ref[1, h]) + chip_ref[1, h].astype(F32)).astype(BF16)
        pair_ref[1, h] = forward
        forward_ref[h] = forward


def enter_kernel(near_ref, far_ref, mine_ref, other_ref, keep_ref, send_ref):
    core = my_core()

    def step(first_ref, early_ref, late_ref):
        heads = range(far_ref.shape[0])
        for h in heads:
            entering = dot(near_ref[0, h], far_ref[h]) + near_ref[1, h].astype(F32)
            early_ref[h] = entering.astype(BF16)
        for h in heads:
            later = dot(first_ref[0, h], early_ref[h]) + first_ref[1, h].astype(F32)
            late_ref[h] = later.astype(BF16)

    @pl.when(core == 0)
    def _():
        step(mine_ref, keep_ref, send_ref)

    @pl.when(core != 0)
    def _():
        step(other_ref, send_ref, keep_ref)


def finish_kernel(
    base_ref,
    response_ref,
    keep_ref,
    other_ref,
    gate_ref,
    w_out,
    term0_ref,
    term1_ref,
    term2_ref,
    term3_ref,
    gated_ref,
    state_ref,
):
    core = my_core()
    half = keep_ref.shape[0]

    @pl.when(core == 0)
    def _():
        state_ref[:half] = keep_ref[...]
        state_ref[half:] = other_ref[...]

    @pl.when(core != 0)
    def _():
        state_ref[:half] = other_ref[...]
        state_ref[half:] = keep_ref[...]

    for h in range(2 * half):
        at = column_of(h)
        attended = base_ref[:, at] + dot(response_ref[:, at], state_ref[h])
        scale = lax.rsqrt(jnp.mean(attended * attended, axis=-1, keepdims=True) + 1e-06)
        gated_ref[:, at] = (attended * scale * gate_ref[:, at]).astype(BF16)
    gated = gated_ref[...]
    terms = (term0_ref, term1_ref, term2_ref, term3_ref)
    width = term0_ref.shape[1]
    here = lax.axis_index("head")
    for steps, term in enumerate(terms):
        at = pl.multiple_of(lax.rem(here + steps, len(terms)) * width, width)
        term[...] = dot(gated, w_out[:, pl.ds(at, width)]).astype(BF16)


def out(*shape, dtype=BF16):
    return pltpu.VMEM(shape, dtype)


def turned(value, axis, steps):
    count = lax.axis_size(axis)
    return lax.ppermute(value, axis, [(at, (at + steps) % count) for at in range(count)])


def swapped(value, axis):
    count = lax.axis_size(axis)
    return lax.ppermute(value, axis, [(at, at ^ 1) for at in range(count)])


def after(value, *others):
    return lax.optimization_barrier((value, *others))[0]


def hbm(value):
    return pltpu.with_memory_space_constraint(value, pltpu.HBM)


def vmem(value):
    return pltpu.with_memory_space_constraint(value, pltpu.VMEM)


def call(kernel, name, outs, ins, mib, *, scratch=(), cost=2_000_000, inputs=None, specs=None):
    single = not isinstance(outs, tuple)
    outs = (outs,) if single else outs
    got = pl.pallas_call(
        kernel,
        out_shape=outs,
        in_specs=[VMEM] * len(ins) if inputs is None else inputs,
        out_specs=(VMEM,) * len(outs) if specs is None else specs,
        scratch_shapes=list(scratch),
        compiler_params=params(mib),
        cost_estimate=pl.CostEstimate(flops=0, bytes_accessed=cost, transcendentals=0),
        name=name,
    )(*ins)
    return got[0] if single else got


def local(
    tokens,
    order,
    doc_lengths,
    w_query,
    w_key,
    w_value,
    w_zgate,
    w_beta,
    w_alpha,
    conv_query,
    conv_key,
    conv_value,
    decay_log,
    decay_bias,
    norm_gain,
    w_out,
):
    rows, width = tokens.shape
    shards = lax.axis_size("seq")
    groups = lax.axis_size("head")
    capacity = 2 * rows // shards
    slots = shards * capacity
    qk, vw, heads = w_query.shape[1], w_value.shape[1], w_beta.shape[1]
    half, key_heads = heads // 2, qk // HEAD
    part = width // groups

    send = call(
        lambda *refs: pack_kernel(shards, *refs),
        "pack",
        pltpu.HBM((slots, part + LANES), BF16),
        (hbm(order.reshape(1, rows)), hbm(tokens)),
        8,
        scratch=[pltpu.VMEM((rows, part), BF16), pltpu.SemaphoreType.DMA],
        inputs=[VMEM, ANY],
    )
    got = lax.all_to_all(
        send.reshape(shards, capacity, part + LANES), "seq", split_axis=0, concat_axis=0, tiled=True
    ).reshape(slots, part + LANES)
    parts = [call(place_kernel, "place", out(rows, part), (got,), 4)]
    for steps in range(1, groups):
        parts.append(turned(parts[0], "head", steps))
    weights = [hbm(after(weight, parts[0])) for weight in (w_query, w_key, w_value, w_zgate)]
    fetched = call(
        fetch_kernel,
        "fetch",
        tuple(pltpu.VMEM(weight.shape, weight.dtype) for weight in weights),
        tuple(weights),
        2,
        scratch=[pltpu.SemaphoreType.DMA((FETCHES * len(weights),))],
        inputs=[ANY] * len(weights),
        specs=(ANY,) * len(weights),
        cost=20_000_000,
    )
    balanced, query, key, value, tail, beta, decay = call(
        project_kernel,
        "project",
        (
            out(rows, width),
            out(rows, qk),
            out(rows, qk),
            out(rows, vw),
            out(TAIL, 2 * qk + vw),
            out(rows, heads, dtype=F32),
            out(rows, heads, dtype=F32),
        ),
        (
            *parts,
            *[vmem(weight) for weight in fetched[:3]],
            w_beta.T,
            w_alpha.T,
            decay_log.reshape(1, heads),
            decay_bias.reshape(1, heads),
        ),
        8,
    )
    tail_got = turned(tail, "seq", 1)
    zgate = call(
        project_gate_kernel, "project_gate", out(rows, vw), (balanced, vmem(fetched[3])), 8
    )
    tail_got, zgate = lax.optimization_barrier((tail_got, zgate))
    states = out(2, half, HEAD, HEAD)
    mine, sent, keys, solved = call(
        chunk_kernel,
        "chunk",
        (states, states, out(key_heads, rows, HEAD), out(heads, rows, 2 * HEAD)),
        (doc_lengths, key, value, tail_got, conv_key, conv_value, beta, decay),
        16,
        scratch=chunk_scratch(heads, rows),
        inputs=[SMEM] + [VMEM] * 7,
    )
    other = swapped(sent, "seq")
    chip = call(chip_kernel, "chip", states, (mine, other), 4)
    before = turned(chip, "seq", 2)
    base, response = call(
        respond_kernel,
        "respond",
        (out(rows, vw, dtype=F32), out(rows, vw)),
        (doc_lengths, after(query, chip), tail_got, conv_query, decay, keys, solved),
        8,
        inputs=[SMEM] + [VMEM] * 6,
        cost=16_000_000,
    )
    base, before = lax.optimization_barrier((base, before))
    pair, pair_forward = call(
        pair_kernel, "pair", (states, out(half, HEAD, HEAD)), (chip, before), 4
    )
    near, far = turned(pair, "seq", 2), turned(pair_forward, "seq", 6)
    gate, w_out = call(
        gate_kernel,
        "gate",
        (out(rows, vw, dtype=F32), pltpu.VMEM(w_out.shape, w_out.dtype)),
        (after(zgate, pair), norm_gain.reshape(1, HEAD), hbm(w_out)),
        4,
        scratch=[pltpu.SemaphoreType.DMA((FETCHES,))],
        inputs=[VMEM, VMEM, ANY],
        specs=(VMEM, ANY),
        cost=10_000_000,
    )
    gate, near, far = lax.optimization_barrier((gate, near, far))
    state = out(half, HEAD, HEAD)
    keep, give = call(enter_kernel, "enter", (state, state), (near, far, mine, other), 4)
    terms = call(
        finish_kernel,
        "finish",
        (out(rows, part),) * groups,
        (base, response, keep, swapped(give, "seq"), gate, vmem(w_out)),
        8,
        scratch=[pltpu.VMEM((rows, vw), BF16), pltpu.VMEM((heads, HEAD, HEAD), BF16)],
    )
    mixed = terms[0].astype(F32)
    for steps in (2, 1, 3):
        mixed = mixed + turned(terms[steps], "head", steps).astype(F32)
    return mixed.astype(BF16)


def solution(mesh):
    return jax.shard_map(
        local,
        mesh=mesh,
        in_specs=(
            P("seq", None),
            P("seq"),
            P(),
            P(None, "head"),
            P(None, "head"),
            P(None, "head"),
            P(None, "head"),
            P(None, "head"),
            P(None, "head"),
            P(None, "head"),
            P(None, "head"),
            P(None, "head"),
            P("head"),
            P("head"),
            P(),
            P("head", None),
        ),
        out_specs=P("seq", "head"),
        check_vma=False,
    )
```

time: 123 us -> 109 us (0.89); the launches traced: 121 us -> 109 us
  blocking collectives: 0 us -> 22.4 us
  local copies, waits for them, and re-layouts: 17.8 us -> 0.05 us
  starting transfers between devices: 26.6 us -> 16.4 us
  waiting for transfers between devices: 44.6 us -> 41.1 us
  Pallas kernels: 31.1 us -> 27.9 us
    all_to_all x0 -> x1, blocking collectives: none -> 22.4 us  [local(): lax.all_to_all(send.reshape(shards, capacity, part + LANES), 'seq', split...]
    unnamed x46 -> x18, local copies, waits for them, and re-layouts: 17.8 us -> 0.05 us
    all_to_all x1 -> x0, waiting for transfers between devices: 14.5 us -> none  [local(): lax.all_to_all(send.reshape(shards, capacity, width + LANES), 'seq', spli...]
    ppermute x8 -> x10, waiting for transfers between devices: 27.9 us -> 38.9 us  [turned(): lax.ppermute(value, axis, [(at, (at + steps) % count) for at in range(cou...]
    all_to_all x1 -> x0, starting transfers between devices: 9.43 us -> none  [local(): lax.all_to_all(send.reshape(shards, capacity, width + LANES), 'seq', spli...]
    pallas_call x11 -> x12, Pallas kernels: 31.1 us -> 27.9 us  [call(): pl.pallas_call(kernel, out_shape=outs, in_specs=[VMEM] * len(ins) if inpu...]
    ppermute x2, starting transfers between devices: 10.6 us -> 7.83 us  [swapped(): return lax.ppermute(value, axis, [(at, at ^ 1) for at in range(count)])]
    ppermute x8 -> x10, starting transfers between devices: 6.58 us -> 8.57 us  [turned(): lax.ppermute(value, axis, [(at, (at + steps) % count) for at in range(cou...]
  transfers between devices with their start and end apart: 11 -> 12, of which waited for: 9 -> 10; matrix products, arithmetic and copies ran while one was open for 0% -> 0% of each run, Pallas kernels for 9% -> 10%
where the time goes in v3:
time: 109 us
  waiting for transfers between devices  41.1 us (38%)
  Pallas kernels  27.9 us (26%)
  blocking collectives  22.4 us (21%)
  starting transfers between devices  16.4 us (15%)
    ppermute x10, waiting for transfers between devices, turned(): lax.ppermute(value, axis, [(at, (at + steps) % count) for at in range(cou...  38.9 us
    pallas_call x12, Pallas kernels, call(): pl.pallas_call(kernel, out_shape=outs, in_specs=[VMEM] * len(ins) if inpu...  27.9 us
    all_to_all x1, blocking collectives, local(): lax.all_to_all(send.reshape(shards, capacity, part + LANES), 'seq', split...  22.4 us
    ppermute x10, starting transfers between devices, turned(): lax.ppermute(value, axis, [(at, (at + steps) % count) for at in range(cou...  8.57 us
    ppermute x2, starting transfers between devices, swapped(): return lax.ppermute(value, axis, [(at, at ^ 1) for at in range(count)])  7.83 us
  transfers between devices with their start and end apart: 12, of which 10 were waited for; matrix products, arithmetic and copies ran while one was open for 0% of the time, Pallas kernels for 10%

profile of v3, /device:TPU:1, one launch (start us, length us, event | category | flops | bytes accessed | tf_op | source)
XLA Modules:
  0.0 108.8 jit_solution(10598463914775206330)
XLA Ops:
  0.0 2.8 %pack.1 = bf16[512,640]{1,0:T(8,128)(2,1)} custom-call(s32[1,256]{1,0:T(1,128)} %bitcast.15, bf16[256,2048]{1,0:T(8,128)(2,1)} %refs_1_.1), custom_call_target="tpu_custom_call" | custom-call | bytes 2000000 | tf_op jit(solution)/shard_map/pack/pallas_call | solution.py:466
  2.8 22.4 %all_to_all.5 = bf16[32,16,640]{2,1,0:T(8,128)(2,1)S(1)} all-to-all(bf16[32,16,640]{2,1,0:T(8,128)(2,1)} %bitcast.14), channel_id=1, replica_groups=mesh['seq'=32,'head'=4] {'seq'}, dimensions={0} | all-to-all | bytes 1310720 | tf_op jit(solution)/shard_map/all_to_all | solution.py:515
  25.7 2.8 %collective-permute-start.2 = (bf16[256,512]{1,0:T(8,128)(2,1)S(1)}, bf16[256,512]{1,0:T(8,128)(2,1)S(1)}, u32[]{:S(2)}, u32[]{:S(2)}) collective-permute-start(bf16[256,512]{1,0:T(8,128)(2,1)S(1)} %place.1.part0_ref), channel_id=1, source_target_pairs={{0,3},{1,0},{2,1},{3,2},{4,7},{5,4},{6,5},{7,6},{8,11},{9,8},{10,9... | collective-permute-start | bytes 786440 | tf_op jit(solution)/shard_map/ppermute | solution.py:443
  29.5 4.7 %fetch.1 = (bf16[2048,512]{1,0:T(8,128)(2,1)S(1)}, bf16[2048,512]{1,0:T(8,128)(2,1)S(1)}, bf16[2048,1024]{1,0:T(8,128)(2,1)S(1)}, bf16[2048,1024]{1,0:T(8,128)(2,1)S(1)}) custom-call(bf16[2048,512]{1,0:T(8,128)(2,1)} %refs_0_, bf16[2048,512]{1,0:T(8,128)(2,1)} %refs_1_.2, bf16[2048,1024]{1,0:T(8,128)(2,1)} %refs_2_, bf16[2048,1024]{1,0:T(8,128)(2,1)} %refs_3_), custom_call_target="tpu_custom_call" | custom-call | bytes 20000000 | tf_op jit(solution)/shard_map/fetch/pallas_call | solution.py:466
  34.3 4.8 %collective-permute-done.2.part3_ref = bf16[256,512]{1,0:T(8,128)(2,1)S(1)} collective-permute-done((bf16[256,512]{1,0:T(8,128)(2,1)S(1)}, bf16[256,512]{1,0:T(8,128)(2,1)S(1)}, u32[]{:S(2)}, u32[]{:S(2)}) %collective-permute-start.2) | collective-permute-done | bytes 262176 | tf_op jit(solution)/shard_map/ppermute | solution.py:443
  39.1 4.7 %collective-permute-done.part1_ref = bf16[256,512]{1,0:T(8,128)(2,1)S(1)} collective-permute-done((bf16[256,512]{1,0:T(8,128)(2,1)S(1)}, bf16[256,512]{1,0:T(8,128)(2,1)S(1)}, u32[]{:S(2)}, u32[]{:S(2)}) %collective-permute-start) | collective-permute-done | bytes 262176 | tf_op jit(solution)/shard_map/ppermute | solution.py:443
  43.9 3.0 %project.1 = (bf16[256,2048]{1,0:T(8,128)(2,1)S(1)}, bf16[256,512]{1,0:T(8,128)(2,1)S(1)}, bf16[256,512]{1,0:T(8,128)(2,1)S(1)}, bf16[256,1024]{1,0:T(8,128)(2,1...) custom-call(bf16[256,512]{1,0:T(8,128)(2,1)S(1)} %place.1.part0_ref, ...), custom_call_target="tpu_custom_call" | custom-call | bytes 2000000 | tf_op jit(solution)/shard_map/project/pallas_call | solution.py:466
  46.9 1.2 %collective-permute-start.3 = (bf16[16,2048]{1,0:T(8,128)(2,1)S(1)}, bf16[16,2048]{1,0:T(8,128)(2,1)S(1)}, u32[]{:S(2)}, u32[]{:S(2)}) collective-permute-start(bf16[16,2048]{1,0:T(8,128)(2,1)S(1)} %get-tuple-element.55), channel_id=1, source_target_pairs={{0,4},{4,8},{8,12},{12,16},{16,20},{20,24},{24,28},{28,32},{32,36}... | collective-permute-start | bytes 196616 | tf_op jit(solution)/shard_map/ppermute | solution.py:443
  48.1 1.3 %project_gate.1.zgate_ref = bf16[256,1024]{1,0:T(8,128)(2,1)S(1)} custom-call(bf16[256,2048]{1,0:T(8,128)(2,1)S(1)} %get-tuple-element.56.balanced_ref, bf16[2048,1024]{1,0:T(8,128)(2,1)S(1)} %get-tuple-element.57.w_zgate), custom_call_target="tpu_custom_call" | custom-call | bytes 2000000 | tf_op jit(solution)/shard_map/project_gate/pallas_call | solution.py:466
  49.4 8.2 %chunk.1 = (bf16[2,4,128,128]{3,2,1,0:T(8,128)(2,1)S(1)}, bf16[2,4,128,128]{3,2,1,0:T(8,128)(2,1)S(1)}, bf16[4,256,128]{2,1,0:T(8,128)(2,1)S(1)}, bf16[8,256,256]{2,1,0:T(8,128)(2,1)S(1)}) custom-call(s32[8]{0:T(128)S(1)} %copy-done.5, bf16[256,512]{1,0:T(8,128)(2,1)S(1)} %get-tuple-element.53.key_ref, bf16[256,1024]{1,0:T(8,128)(2,1)S(1)} %get-tuple-element.54.value_ref, ...), custom_call_target="tpu_custom_call" | custom-call | bytes 2000000 | tf_op jit(solution)/shard_map/chunk/pallas_call | solution.py:466
  57.6 5.3 %collective-permute-start.4 = (bf16[2,4,128,128]{3,2,1,0:T(8,128)(2,1)S(1)}, bf16[2,4,128,128]{3,2,1,0:T(8,128)(2,1)S(1)}, u32[]{:S(2)}, u32[]{:S(2)}) collective-permute-start(bf16[2,4,128,128]{3,2,1,0:T(8,128)(2,1)S(1)} %get-tuple-element.62), channel_id=1, source_target_pairs={{0,4},{4,0},{8,12},{12,8},{16,20},{20,16},{24,28},{28,24},{32,36},... | collective-permute-start | bytes 786440 | tf_op jit(solution)/shard_map/ppermute | solution.py:448
  63.0 1.2 %collective-permute-done.4.other_ref = bf16[2,4,128,128]{3,2,1,0:T(8,128)(2,1)S(1)} collective-permute-done((bf16[2,4,128,128]{3,2,1,0:T(8,128)(2,1)S(1)}, bf16[2,4,128,128]{3,2,1,0:T(8,128)(2,1)S(1)}, u32[]{:S(2)}, u32[]{:S(2)}) %collective-permute-start.4) | collective-permute-done | bytes 262176 | tf_op jit(solution)/shard_map/ppermute | solution.py:448
  64.4 2.8 %respond.1 = (f32[256,1024]{1,0:T(8,128)S(1)}, bf16[256,1024]{1,0:T(8,128)(2,1)S(1)}) custom-call(s32[8]{0:T(128)S(1)} %copy-done.5, bf16[256,512]{1,0:T(8,128)(2,1)S(1)} %get-tuple-element.63.query_ref, bf16[16,2048]{1,0:T(8,128)(2,1)S(1)} %collective-permute-done.3.tail_ref, bf16[4,512]{1,0:T(4,128)(2,1)S(1)} %copy-done.4, ...), custom_call_target="tpu_custom_call" | custom-call | bytes 16000000 | tf_op jit(solution)/shard_map/respond/pallas_call | solution.py:466
  67.2 8.0 %collective-permute-done.5.before_ref = bf16[2,4,128,128]{3,2,1,0:T(8,128)(2,1)S(1)} collective-permute-done((bf16[2,4,128,128]{3,2,1,0:T(8,128)(2,1)S(1)}, bf16[2,4,128,128]{3,2,1,0:T(8,128)(2,1)S(1)}, u32[]{:S(2)}, u32[]{:S(2)}) %collective-permute-start.5) | collective-permute-done | bytes 262176 | tf_op jit(solution)/shard_map/ppermute | solution.py:443
  75.9 2.2 %gate.1 = (f32[256,1024]{1,0:T(8,128)S(1)}, bf16[1024,2048]{1,0:T(8,128)(2,1)S(1)}) custom-call(bf16[256,1024]{1,0:T(8,128)(2,1)S(1)} %project_gate.1.zgate_ref, f32[1,128]{1,0:T(1,128)S(1)} %bitcast.13, bf16[1024,2048]{1,0:T(8,128)(2,1)} %w_out.1), custom_call_target="tpu_custom_call" | custom-call | bytes 10000000 | tf_op jit(solution)/shard_map/gate/pallas_call | solution.py:466
  78.1 4.0 %collective-permute-done.7.far_ref = bf16[4,128,128]{2,1,0:T(8,128)(2,1)S(1)} collective-permute-done((bf16[4,128,128]{2,1,0:T(8,128)(2,1)S(1)}, bf16[4,128,128]{2,1,0:T(8,128)(2,1)S(1)}, u32[]{:S(2)}, u32[]{:S(2)}) %collective-permute-start.7) | collective-permute-done | bytes 131104 | tf_op jit(solution)/shard_map/ppermute | solution.py:443
  82.0 5.0 %collective-permute-done.6.near_ref = bf16[2,4,128,128]{3,2,1,0:T(8,128)(2,1)S(1)} collective-permute-done((bf16[2,4,128,128]{3,2,1,0:T(8,128)(2,1)S(1)}, bf16[2,4,128,128]{3,2,1,0:T(8,128)(2,1)S(1)}, u32[]{:S(2)}, u32[]{:S(2)}) %collective-permute-start.6) | collective-permute-done | bytes 262176 | tf_op jit(solution)/shard_map/ppermute | solution.py:443
  87.4 2.5 %collective-permute-start.8 = (bf16[4,128,128]{2,1,0:T(8,128)(2,1)S(1)}, bf16[4,128,128]{2,1,0:T(8,128)(2,1)S(1)}, u32[]{:S(2)}, u32[]{:S(2)}) collective-permute-start(bf16[4,128,128]{2,1,0:T(8,128)(2,1)S(1)} %get-tuple-element.78), channel_id=1, source_target_pairs={{0,4},{4,0},{8,12},{12,8},{16,20},{20,16},{24,28},{28,24},{32,36},... | collective-permute-start | bytes 393224 | tf_op jit(solution)/shard_map/ppermute | solution.py:448
  89.9 1.0 collective-permute-done.8.other_ref
  90.9 1.6 %finish.1 = (bf16[256,512]{1,0:T(8,128)(2,1)S(1)}, bf16[256,512]{1,0:T(8,128)(2,1)S(1)}, bf16[256,512]{1,0:T(8,128)(2,1)S(1)}, bf16[256,512]{1,0:T(8,128)(2,1)S(1)}) custom-call(f32[256,1024]{1,0:T(8,128)S(1)} %get-tuple-element.67.base_ref, bf16[256,1024]{1,0:T(8,128)(2,1)S(1)} %get-tuple-element.68.response_ref, ...), custom_call_target="tpu_custom_call" | custom-call | bytes 2000000 | tf_op jit(solution)/shard_map/finish/pallas_call | solution.py:466
  93.5 2.1 %collective-permute-start.11 = (bf16[256,512]{1,0:T(8,128)(2,1)S(1)}, bf16[256,512]{1,0:T(8,128)(2,1)S(1)}, u32[]{:S(2)}, u32[]{:S(2)}) collective-permute-start(bf16[256,512]{1,0:T(8,128)(2,1)S(1)} %get-tuple-element.84), channel_id=1, source_target_pairs={{0,3},{1,0},{2,1},{3,2},{4,7},{5,4},{6,5},{7,6},{8,11},{9,8},{10,9... | collective-permute-start | bytes 786440 | tf_op jit(solution)/shard_map/ppermute | solution.py:443
  95.6 6.1 %collective-permute-done.9 = bf16[256,512]{1,0:T(8,128)(2,1)S(1)} collective-permute-done((bf16[256,512]{1,0:T(8,128)(2,1)S(1)}, bf16[256,512]{1,0:T(8,128)(2,1)S(1)}, u32[]{:S(2)}, u32[]{:S(2)}) %collective-permute-start.9) | collective-permute-done | bytes 262176 | tf_op jit(solution)/shard_map/ppermute | solution.py:443
  101.7 6.3 %collective-permute-done.10 = bf16[256,512]{1,0:T(8,128)(2,1)S(1)} collective-permute-done((bf16[256,512]{1,0:T(8,128)(2,1)S(1)}, bf16[256,512]{1,0:T(8,128)(2,1)S(1)}, u32[]{:S(2)}, u32[]{:S(2)}) %collective-permute-start.10) | collective-permute-done | bytes 262176 | tf_op jit(solution)/shard_map/ppermute | solution.py:443
  108.0 0.8 add_convert_fusion
  (32 shorter events, 3.8 us)
Async XLA Ops:
  25.6 18.2 %copy-start = (bf16[2048,8]{0,1:T(8,128)(2,1)S(1)}, bf16[2048,8]{0,1:T(8,128)(2,1)}, u32[]{:S(2)}) copy-start(bf16[2048,8]{0,1:T(8,128)(2,1)} %param.23) | copy-start | bytes 98308
  25.7 18.2 %copy-start.1 = (bf16[2048,8]{0,1:T(8,128)(2,1)S(1)}, bf16[2048,8]{0,1:T(8,128)(2,1)}, u32[]{:S(2)}) copy-start(bf16[2048,8]{0,1:T(8,128)(2,1)} %param.24) | copy-start | bytes 98308
  25.7 18.2 %copy-start.6 = (f32[8]{0:T(128)S(1)}, f32[8]{0:T(128)}, u32[]{:S(2)}) copy-start(f32[8]{0:T(128)} %param.28) | copy-start | bytes 100
  25.7 18.2 %copy-start.7 = (f32[8]{0:T(128)S(1)}, f32[8]{0:T(128)}, u32[]{:S(2)}) copy-start(f32[8]{0:T(128)} %param.29) | copy-start | bytes 100
  25.7 13.4 %collective-permute-start.2 = (bf16[256,512]{1,0:T(8,128)(2,1)S(1)}, bf16[256,512]{1,0:T(8,128)(2,1)S(1)}, u32[]{:S(2)}, u32[]{:S(2)}) collective-permute-start(bf16[256,512]{1,0:T(8,128)(2,1)S(1)} %place.1.part0_ref), channel_id=1, source_target_pairs={{0,3},{1,0},{2,1},{3,2},{4,7},{5,4},{6,5},{7,6},{8,11},{9,8},{10,9... | collective-permute-start | bytes 786440 | tf_op jit(solution)/shard_map/ppermute | solution.py:443
  28.5 10.6 %collective-permute-start.1 = (bf16[256,512]{1,0:T(8,128)(2,1)S(1)}, bf16[256,512]{1,0:T(8,128)(2,1)S(1)}, u32[]{:S(2)}, u32[]{:S(2)}) collective-permute-start(bf16[256,512]{1,0:T(8,128)(2,1)S(1)} %place.1.part0_ref), channel_id=1, source_target_pairs={{0,2},{1,3},{2,0},{3,1},{4,6},{5,7},{6,4},{7,5},{8,10},{9,11},{10,... | collective-permute-start | bytes 786440 | tf_op jit(solution)/shard_map/ppermute | solution.py:443
  28.8 15.0 %collective-permute-start = (bf16[256,512]{1,0:T(8,128)(2,1)S(1)}, bf16[256,512]{1,0:T(8,128)(2,1)S(1)}, u32[]{:S(2)}, u32[]{:S(2)}) collective-permute-start(bf16[256,512]{1,0:T(8,128)(2,1)S(1)} %place.1.part0_ref), channel_id=1, source_target_pairs={{0,1},{1,2},{2,3},{3,0},{4,5},{5,6},{6,7},{7,4},{8,9},{9,10},{10,1... | collective-permute-start | bytes 786440 | tf_op jit(solution)/shard_map/ppermute | solution.py:443
  46.9 2.6 %copy-start.2 = (bf16[4,1024]{1,0:T(4,128)(2,1)S(1)}, bf16[4,1024]{1,0:T(4,128)(2,1)}, u32[]{:S(2)}) copy-start(bf16[4,1024]{1,0:T(4,128)(2,1)} %taps_value.1) | copy-start | bytes 24580
  46.9 2.5 %copy-start.3 = (bf16[4,512]{1,0:T(4,128)(2,1)S(1)}, bf16[4,512]{1,0:T(4,128)(2,1)}, u32[]{:S(2)}) copy-start(bf16[4,512]{1,0:T(4,128)(2,1)} %taps_key.1) | copy-start | bytes 12292
  46.9 2.5 %copy-start.5 = (s32[8]{0:T(128)S(1)}, s32[8]{0:T(128)}, u32[]{:S(2)}) copy-start(s32[8]{0:T(128)} %lengths_ref.3) | copy-start | bytes 100
  46.9 17.5 %copy-start.4 = (bf16[4,512]{1,0:T(4,128)(2,1)S(1)}, bf16[4,512]{1,0:T(4,128)(2,1)}, u32[]{:S(2)}) copy-start(bf16[4,512]{1,0:T(4,128)(2,1)} %taps_query.1) | copy-start | bytes 12292
  46.9 2.5 %collective-permute-start.3 = (bf16[16,2048]{1,0:T(8,128)(2,1)S(1)}, bf16[16,2048]{1,0:T(8,128)(2,1)S(1)}, u32[]{:S(2)}, u32[]{:S(2)}) collective-permute-start(bf16[16,2048]{1,0:T(8,128)(2,1)S(1)} %get-tuple-element.55), channel_id=1, source_target_pairs={{0,4},{4,8},{8,12},{12,16},{16,20},{20,24},{24,28},{28,32},{32,36}... | collective-permute-start | bytes 196616 | tf_op jit(solution)/shard_map/ppermute | solution.py:443
  48.1 27.8 %copy-start.8 = (f32[128]{0:T(128)S(1)}, f32[128]{0:T(128)}, u32[]{:S(2)}) copy-start(f32[128]{0:T(128)} %param.30) | copy-start | bytes 1540
  57.6 6.5 %collective-permute-start.4 = (bf16[2,4,128,128]{3,2,1,0:T(8,128)(2,1)S(1)}, bf16[2,4,128,128]{3,2,1,0:T(8,128)(2,1)S(1)}, u32[]{:S(2)}, u32[]{:S(2)}) collective-permute-start(bf16[2,4,128,128]{3,2,1,0:T(8,128)(2,1)S(1)} %get-tuple-element.62), channel_id=1, source_target_pairs={{0,4},{4,0},{8,12},{12,8},{16,20},{20,16},{24,28},{28,24},{32,36},... | collective-permute-start | bytes 786440 | tf_op jit(solution)/shard_map/ppermute | solution.py:448
  64.3 10.9 %collective-permute-start.5 = (bf16[2,4,128,128]{3,2,1,0:T(8,128)(2,1)S(1)}, bf16[2,4,128,128]{3,2,1,0:T(8,128)(2,1)S(1)}, u32[]{:S(2)}, u32[]{:S(2)}) collective-permute-start(bf16[2,4,128,128]{3,2,1,0:T(8,128)(2,1)S(1)} %chip.1.chip_ref), channel_id=1, source_target_pairs={{0,8},{4,12},{8,16},{12,20},{16,24},{20,28},{24,32},{28,36},{32,40... | collective-permute-start | bytes 786440 | tf_op jit(solution)/shard_map/ppermute | solution.py:443
  75.5 11.6 %collective-permute-start.6 = (bf16[2,4,128,128]{3,2,1,0:T(8,128)(2,1)S(1)}, bf16[2,4,128,128]{3,2,1,0:T(8,128)(2,1)S(1)}, u32[]{:S(2)}, u32[]{:S(2)}) collective-permute-start(bf16[2,4,128,128]{3,2,1,0:T(8,128)(2,1)S(1)} %get-tuple-element.71), channel_id=1, source_target_pairs={{0,8},{4,12},{8,16},{12,20},{16,24},{20,28},{24,32},{28,36},{32,40... | collective-permute-start | bytes 786440 | tf_op jit(solution)/shard_map/ppermute | solution.py:443
  75.8 6.3 %collective-permute-start.7 = (bf16[4,128,128]{2,1,0:T(8,128)(2,1)S(1)}, bf16[4,128,128]{2,1,0:T(8,128)(2,1)S(1)}, u32[]{:S(2)}, u32[]{:S(2)}) collective-permute-start(bf16[4,128,128]{2,1,0:T(8,128)(2,1)S(1)} %get-tuple-element.74), channel_id=1, source_target_pairs={{0,24},{4,28},{8,32},{12,36},{16,40},{20,44},{24,48},{28,52},{32,5... | collective-permute-start | bytes 393224 | tf_op jit(solution)/shard_map/ppermute | solution.py:443
  87.4 3.5 %collective-permute-start.8 = (bf16[4,128,128]{2,1,0:T(8,128)(2,1)S(1)}, bf16[4,128,128]{2,1,0:T(8,128)(2,1)S(1)}, u32[]{:S(2)}, u32[]{:S(2)}) collective-permute-start(bf16[4,128,128]{2,1,0:T(8,128)(2,1)S(1)} %get-tuple-element.78), channel_id=1, source_target_pairs={{0,4},{4,0},{8,12},{12,8},{16,20},{20,16},{24,28},{28,24},{32,36},... | collective-permute-start | bytes 393224 | tf_op jit(solution)/shard_map/ppermute | solution.py:448
  92.5 9.2 %collective-permute-start.9 = (bf16[256,512]{1,0:T(8,128)(2,1)S(1)}, bf16[256,512]{1,0:T(8,128)(2,1)S(1)}, u32[]{:S(2)}, u32[]{:S(2)}) collective-permute-start(bf16[256,512]{1,0:T(8,128)(2,1)S(1)} %get-tuple-element.82), channel_id=1, source_target_pairs={{0,2},{1,3},{2,0},{3,1},{4,6},{5,7},{6,4},{7,5},{8,10},{9,11},{10,... | collective-permute-start | bytes 786440 | tf_op jit(solution)/shard_map/ppermute | solution.py:443
  93.0 15.0 %collective-permute-start.10 = (bf16[256,512]{1,0:T(8,128)(2,1)S(1)}, bf16[256,512]{1,0:T(8,128)(2,1)S(1)}, u32[]{:S(2)}, u32[]{:S(2)}) collective-permute-start(bf16[256,512]{1,0:T(8,128)(2,1)S(1)} %get-tuple-element.83), channel_id=1, source_target_pairs={{0,1},{1,2},{2,3},{3,0},{4,5},{5,6},{6,7},{7,4},{8,9},{9,10},{10,1... | collective-permute-start | bytes 786440 | tf_op jit(solution)/shard_map/ppermute | solution.py:443
  93.5 14.4 %collective-permute-start.11 = (bf16[256,512]{1,0:T(8,128)(2,1)S(1)}, bf16[256,512]{1,0:T(8,128)(2,1)S(1)}, u32[]{:S(2)}, u32[]{:S(2)}) collective-permute-start(bf16[256,512]{1,0:T(8,128)(2,1)S(1)} %get-tuple-element.84), channel_id=1, source_target_pairs={{0,3},{1,0},{2,1},{3,2},{4,7},{5,4},{6,5},{7,6},{8,11},{9,8},{10,9... | collective-permute-start | bytes 786440 | tf_op jit(solution)/shard_map/ppermute | solution.py:443

commit v4 on v3

--- a/solution.py
+++ b/solution.py
@@ -10,6 +10,8 @@
 TAIL = 16
 LANES = 128
 FETCHES = 4
+PACKED = 4
+SPOTS = 12
 VMEM = pl.BlockSpec(memory_space=pltpu.VMEM)
 SMEM = pl.BlockSpec(memory_space=pltpu.SMEM)
 ANY = pl.BlockSpec(memory_space=pl.ANY)
@@ -36,6 +38,7 @@
     rows, width = part_ref.shape
     slots = send_ref.shape[0]
     capacity = slots // shards
+    pieces = width // LANES
     here = pl.multiple_of(lax.axis_index("head") * width, width)
     copy = pltpu.make_async_copy(tokens_ref.at[:, pl.ds(here, width)], part_ref, sem)
     copy.start()
@@ -47,19 +50,48 @@
     before = (iota((rows, rows), 0) < iota((rows, rows), 1)).astype(F32).astype(BF16)
     earlier = dot(marks.astype(BF16), before)
     slot = jnp.sum(earlier * marks, axis=0, keepdims=True).astype(jnp.int32)
-    hit = (iota((slots, rows), 0) == target * capacity + slot).astype(F32)
-    spot = jnp.sum(hit * (landing + 1).astype(F32), axis=1, keepdims=True)
-    send_ref[:, width:] = jnp.broadcast_to(spot, (slots, LANES)).astype(BF16)
+    spots = jnp.where(iota((LANES, rows), 0) == slot, (landing + 1).astype(F32), 0.0)
+    at = iota((slots, rows), 0)
+
+    def chosen(index):
+        return (at == index).astype(F32).astype(BF16)
+
+    extra = dot(chosen(target * capacity + SPOTS), spots.astype(BF16), ((1,), (1,)))
+    hit = chosen(target * capacity + slot)
+    later = jnp.where(target == shards - 1, 0, target + 1) * capacity
+    halo = landing - (rows - KERNEL + 1)
+    halo = jnp.where(halo >= 0, later + halo * pieces, -pieces)
+    halos = [chosen(halo + piece) for piece in range(pieces)]
     copy.wait()
-    send_ref[:, :width] = dot(hit.astype(BF16), part_ref[...]).astype(BF16)
-
-
-def place_kernel(got_ref, part_ref):
-    rows, width = part_ref.shape
+    send_ref[:, :width] = dot(hit, part_ref[...]).astype(BF16)
+    for piece in range(pieces):
+        extra = extra + dot(halos[piece], part_ref[:, piece * LANES : (piece + 1) * LANES])
+    send_ref[:, width:] = extra.astype(BF16)
+
+
+def place_kernel(shards, got_ref, part_ref):
     slots = got_ref.shape[0]
-    spot = got_ref[:, width : width + 1].astype(F32).astype(jnp.int32)
-    hit = (spot == iota((slots, rows), 1) + 1).astype(F32).T.astype(BF16)
-    part_ref[...] = dot(hit, got_ref[:, :width]).astype(BF16)
+    width = part_ref.shape[1]
+    rows = part_ref.shape[0] - TAIL
+    capacity = slots // shards
+    pieces = width // LANES
+    extra = got_ref[:, width:]
+    named = (iota((shards, slots), 1) == iota((shards, slots), 0) * capacity + SPOTS)
+    spots = dot(named.astype(F32).astype(BF16), extra).astype(BF16)
+    inner = lax.bitwise_and(iota((LANES, slots), 1), capacity - 1)
+    turn = (inner == iota((LANES, slots), 0)).astype(F32).astype(BF16)
+    outer = iota((shards, slots), 1) - iota((shards, slots), 0) * capacity
+    spot = jnp.where((outer >= 0) & (outer < capacity), dot(spots, turn), 0.0)
+    spot = jnp.sum(spot, axis=0, keepdims=True).astype(jnp.int32)
+    hit = (spot == iota((rows, slots), 0) + 1).astype(F32).astype(BF16)
+    part_ref[TAIL:] = dot(hit, got_ref[:, :width]).astype(BF16)
+    inner = lax.bitwise_and(iota((TAIL, slots), 1), capacity - 1)
+    halo = iota((TAIL, slots), 0) - (TAIL - KERNEL + 1)
+    for piece in range(pieces):
+        from_slot = (halo >= 0) & (inner == halo * pieces + piece)
+        part_ref[:TAIL, piece * LANES : (piece + 1) * LANES] = dot(
+            from_slot.astype(F32).astype(BF16), extra
+        ).astype(BF16)
 
 
 def softplus(x):
@@ -103,11 +135,9 @@
     query_ref,
     key_ref,
     value_ref,
-    tail_ref,
     beta_ref,
     decay_ref,
 ):
-    rows = balanced_ref.shape[0]
     parts = (part0_ref, part1_ref, part2_ref, part3_ref)
     width = part0_ref.shape[1]
     here = lax.axis_index("head")
@@ -116,13 +146,11 @@
         balanced_ref[:, pl.ds(pl.multiple_of(at, width), width)] = part[...]
     balanced = balanced_ref[...]
     across = ((1,), (1,))
-    column = 0
     for weight, to in ((w_query, query_ref), (w_key, key_ref), (w_value, value_ref)):
         for start in range(0, to.shape[1], 512):
-            part = dot(balanced, weight[:, start : start + 512]).astype(BF16)
-            to[:, start : start + 512] = part
-            tail_ref[:, column : column + 512] = part[rows - TAIL :]
-            column += 512
+            part = dot(balanced, weight[:, start : start + 512])
+            to[:, start : start + 512] = part.astype(BF16)
+    balanced = balanced_ref[TAIL:]
     beta_ref[...] = jax.nn.sigmoid(dot(balanced, w_beta[...], across))
     decay_ref[...] = -jnp.exp(decay_log[...]) * softplus(
         dot(balanced, w_alpha[...], across) + decay_bias[...]
@@ -130,7 +158,7 @@
 
 
 def project_gate_kernel(balanced_ref, w_zgate, zgate_ref):
-    balanced = balanced_ref[...]
+    balanced = balanced_ref[TAIL:]
     for start in range(0, zgate_ref.shape[1], 512):
         part = dot(balanced, w_zgate[:, start : start + 512])
         zgate_ref[:, start : start + 512] = part.astype(BF16)
@@ -155,8 +183,8 @@
     return count
 
 
-def convolve(projected, tail, taps, same):
-    extended = jnp.concatenate([tail.astype(F32), projected.astype(F32)], axis=0)
+def convolve(projected, taps, same):
+    extended = projected.astype(F32)
     sums = None
     for lag in range(KERNEL):
         rolled = extended if lag == 0 else pltpu.roll(extended, lag, 0)
@@ -209,7 +237,6 @@
     lengths_ref,
     key_ref,
     value_ref,
-    tail_ref,
     taps_key,
     taps_value,
     beta_ref,
@@ -219,12 +246,14 @@
     keys,
     solved_ref,
     system_ref,
+    packed_ref,
     inverse_ref,
+    whole_ref,
     mask_ref,
     states_ref,
     right_ref,
 ):
-    rows = key_ref.shape[0]
+    rows = beta_ref.shape[0]
     first, core = lax.axis_index("seq") * rows, my_core()
     heads = beta_ref.shape[1]
     key_heads = key_ref.shape[1] // HEAD
@@ -232,45 +261,83 @@
     width = key_ref.shape[1]
     segment, same, inside, carries = masks(first, document_ends(lengths_ref), rows)
     row, column = iota((rows, rows), 0), iota((rows, rows), 1)
-    levels = rows.bit_length() - 1
+    small = rows // PACKED
+    levels = small.bit_length() - 1
+    down_row, lane = iota((small, rows), 0), iota((small, rows), 1)
+    lane_in = lax.bitwise_and(lane, small - 1)
     for level in range(levels):
         size = 1 << level
-        apart = (lax.bitwise_xor(row, column) < 2 * size) & (
-            lax.bitwise_and(row, size) > lax.bitwise_and(column, size)
+        apart = (lax.bitwise_xor(down_row, lane_in) < 2 * size) & (
+            lax.bitwise_and(down_row, size) > lax.bitwise_and(lane_in, size)
         )
         mask_ref[level] = apart.astype(F32).astype(BF16)
-    unit_matrix = (row == column).astype(F32)
+    diagonal = (down_row == lane_in).astype(F32).astype(BF16)
+    blocks = [
+        ((lane >= i * small) & (lane < (i + 1) * small)).astype(F32).astype(BF16)
+        for i in range(PACKED)
+    ]
+
+    def spread(packed):
+        return jnp.concatenate([packed * block for block in blocks], axis=0)
     strict = inside & (row > column)
     down, across = cumulated(decay_ref)
 
     for kh in range(key_heads):
         at = column_of(kh)
         keys[kh] = unit(
-            convolve(key_ref[:, at], tail_ref[:, column_of(key_heads + kh)], taps_key[:, at], same), 1.0
+            convolve(key_ref[:, at], taps_key[:, at], same), 1.0
         ).astype(BF16)
         inner = dot(keys[kh], keys[kh], ((1,), (1,)))
         for h in range(kh * repeat, (kh + 1) * repeat):
             system = beta_ref[:, h : h + 1] * inner * between(down, across, h, strict)
             system_ref[h] = system.astype(BF16)
-            inverse_ref[h] = (unit_matrix - system * mask_ref[0].astype(F32)).astype(BF16)
     for h in range(heads):
-        at, to = column_of(h), column_of(2 * key_heads + h)
+        at = column_of(h)
         beta = beta_ref[:, h : h + 1]
         carried = jnp.exp(down[:, h : h + 1]) * carries
-        value = convolve(value_ref[:, at], tail_ref[:, to], taps_value[:, at], same)
+        value = convolve(value_ref[:, at], taps_value[:, at], same)
         right_ref[h, :, :HEAD] = (beta * value).astype(BF16)
         right_ref[h, :, HEAD:] = (beta * carried * keys[h // repeat].astype(F32)).astype(BF16)
+    for h in range(heads):
+        packed = None
+        for i in range(PACKED):
+            term = system_ref[h, i * small : (i + 1) * small] * blocks[i]
+            packed = term if packed is None else packed + term
+        packed_ref[h] = packed
+        inverse_ref[h] = diagonal - packed * mask_ref[0]
     for level in range(1, levels):
         for h in range(heads):
             inverse = inverse_ref[h]
-            part = dot(system_ref[h] * mask_ref[level], inverse).astype(BF16)
-            inverse_ref[h] = (inverse.astype(F32) - dot(inverse, part)).astype(BF16)
+            part = dot(packed_ref[h] * mask_ref[level], spread(inverse)).astype(BF16)
+            inverse_ref[h] = inverse - dot(inverse, spread(part)).astype(BF16)
+    zero = jnp.zeros((small, rows), BF16)
+    for h in range(heads):
+        inverse = inverse_ref[h]
+        spread_inverse = spread(inverse)
+        below = (
+            system_ref[h, small : 2 * small] * blocks[0]
+            + system_ref[h, 3 * small : 4 * small] * blocks[2]
+        )
+        part = dot(below, spread_inverse).astype(BF16)
+        part = jnp.concatenate([zero, part * blocks[0], zero, part * blocks[2]], axis=0)
+        part = dot(inverse, part).astype(BF16)
+        part = jnp.concatenate([zero, part * blocks[0], zero, part * blocks[2]], axis=0)
+        whole_ref[h] = spread_inverse - part
 
     square = (iota((HEAD, HEAD), 0) == iota((HEAD, HEAD), 1)).astype(F32)
-    half = heads // 2
+    half, middle = heads // 2, rows // 2
     last_same = (segment == segment[rows - 1 : rows, :]).astype(F32)
     for h in range(heads):
-        solved_ref[h] = dot(inverse_ref[h], right_ref[h]).astype(BF16)
+        solved_ref[h, :middle] = dot(
+            whole_ref[h, :middle, :middle], right_ref[h, :middle]
+        ).astype(BF16)
+    for h in range(heads):
+        rest = right_ref[h, middle:].astype(F32) - dot(
+            system_ref[h, middle:, :middle], solved_ref[h, :middle]
+        )
+        solved_ref[h, middle:] = dot(whole_ref[h, middle:, middle:], rest.astype(BF16)).astype(
+            BF16
+        )
     for h in range(heads):
         gain = down[:, h : h + 1]
         last = jnp.exp(gain[rows - 1 : rows, :] - gain) * last_same
@@ -291,10 +358,13 @@
 
 
 def chunk_scratch(heads, rows):
+    small = rows // PACKED
     return [
         pltpu.VMEM((heads, rows, rows), BF16),
+        pltpu.VMEM((heads, small, rows), BF16),
+        pltpu.VMEM((heads, small, rows), BF16),
         pltpu.VMEM((heads, rows, rows), BF16),
-        pltpu.VMEM((rows.bit_length() - 1, rows, rows), BF16),
+        pltpu.VMEM((small.bit_length() - 1, small, rows), BF16),
         pltpu.VMEM((2, heads, HEAD, HEAD), BF16),
         pltpu.VMEM((heads, rows, 2 * HEAD), BF16),
     ]
@@ -303,7 +373,6 @@
 def respond_kernel(
     lengths_ref,
     query_ref,
-    tail_ref,
     taps_query,
     decay_ref,
     keys,
@@ -311,8 +380,7 @@
     base_ref,
     response_ref,
 ):
-    rows = query_ref.shape[0]
-    heads = decay_ref.shape[1]
+    rows, heads = decay_ref.shape
     key_heads = query_ref.shape[1] // HEAD
     repeat = heads // key_heads
     segment, same, inside, carries = masks(
@@ -323,7 +391,7 @@
     for kh in range(key_heads):
         at = column_of(kh)
         query = unit(
-            convolve(query_ref[:, at], tail_ref[:, at], taps_query[:, at], same), HEAD**-0.5
+            convolve(query_ref[:, at], taps_query[:, at], same), HEAD**-0.5
         )
         cross = dot(query.astype(BF16), keys[kh], ((1,), (1,)))
         for h in range(kh * repeat, (kh + 1) * repeat):
@@ -515,9 +583,10 @@
     got = lax.all_to_all(
         send.reshape(shards, capacity, part + LANES), "seq", split_axis=0, concat_axis=0, tiled=True
     ).reshape(slots, part + LANES)
-    parts = [call(place_kernel, "place", out(rows, part), (got,), 4)]
-    for steps in range(1, groups):
-        parts.append(turned(parts[0], "head", steps))
+    own = call(
+        lambda *refs: place_kernel(shards, *refs), "place", out(TAIL + rows, part), (got,), 4
+    )
+    parts = [own] + [turned(own, "head", steps) for steps in range(1, groups)]
     weights = [hbm(after(weight, parts[0])) for weight in (w_query, w_key, w_value, w_zgate)]
     fetched = call(
         fetch_kernel,
@@ -530,15 +599,14 @@
         specs=(ANY,) * len(weights),
         cost=20_000_000,
     )
-    balanced, query, key, value, tail, beta, decay = call(
+    balanced, query, key, value, beta, decay = call(
         project_kernel,
         "project",
         (
-            out(rows, width),
-            out(rows, qk),
-            out(rows, qk),
-            out(rows, vw),
-            out(TAIL, 2 * qk + vw),
+            out(TAIL + rows, width),
+            out(TAIL + rows, qk),
+            out(TAIL + rows, qk),
+            out(TAIL + rows, vw),
             out(rows, heads, dtype=F32),
             out(rows, heads, dtype=F32),
         ),
@@ -552,20 +620,15 @@
         ),
         8,
     )
-    tail_got = turned(tail, "seq", 1)
-    zgate = call(
-        project_gate_kernel, "project_gate", out(rows, vw), (balanced, vmem(fetched[3])), 8
-    )
-    tail_got, zgate = lax.optimization_barrier((tail_got, zgate))
     states = out(2, half, HEAD, HEAD)
     mine, sent, keys, solved = call(
         chunk_kernel,
         "chunk",
         (states, states, out(key_heads, rows, HEAD), out(heads, rows, 2 * HEAD)),
-        (doc_lengths, key, value, tail_got, conv_key, conv_value, beta, decay),
+        (doc_lengths, key, value, conv_key, conv_value, beta, decay),
         16,
         scratch=chunk_scratch(heads, rows),
-        inputs=[SMEM] + [VMEM] * 7,
+        inputs=[SMEM] + [VMEM] * 6,
     )
     other = swapped(sent, "seq")
     chip = call(chip_kernel, "chip", states, (mine, other), 4)
@@ -574,12 +637,20 @@
         respond_kernel,
         "respond",
         (out(rows, vw, dtype=F32), out(rows, vw)),
-        (doc_lengths, after(query, chip), tail_got, conv_query, decay, keys, solved),
+        (doc_lengths, after(query, chip), conv_query, decay, keys, solved),
         8,
-        inputs=[SMEM] + [VMEM] * 6,
+        inputs=[SMEM] + [VMEM] * 5,
         cost=16_000_000,
     )
-    base, before = lax.optimization_barrier((base, before))
+    zgate = call(
+        project_gate_kernel,
+        "project_gate",
+        out(rows, vw),
+        (after(balanced, base), vmem(fetched[3])),
+        8,
+        cost=6_000_000,
+    )
+    zgate, base, before = lax.optimization_barrier((zgate, base, before))
     pair, pair_forward = call(
         pair_kernel, "pair", (states, out(half, HEAD, HEAD)), (chip, before), 4
     )

time: 109 us -> 101 us (0.927)
  starting transfers between devices: 16.4 us -> 12.1 us
  waiting for transfers between devices: 41.1 us -> 38.8 us
  Pallas kernels: 27.9 us -> 26.7 us
    ppermute x2, starting transfers between devices: 7.83 us -> 3.07 us  [swapped(): return lax.ppermute(value, axis, [(at, at ^ 1) for at in range(count)])]
    ppermute x10 -> x9, waiting for transfers between devices: 38.9 us -> 36.7 us  [turned(): lax.ppermute(value, axis, [(at, (at + steps) % count) for at in range(cou...]
    pallas_call x12, Pallas kernels: 27.9 us -> 26.7 us  [call(): pl.pallas_call(kernel, out_shape=outs, in_specs=[VMEM] * len(ins) if inpu...]
    ppermute x10 -> x9, starting transfers between devices: 8.57 us -> 9.04 us  [turned(): lax.ppermute(value, axis, [(at, (at + steps) % count) for at in range(cou...]
  transfers between devices with their start and end apart: 12 -> 11, of which waited for: 10 -> 9; matrix products, arithmetic and copies ran while one was open for 0% -> 0% of each run, Pallas kernels for 10% -> 11%
where the time goes in v4:
time: 101 us
  waiting for transfers between devices  38.8 us (38%)
  Pallas kernels  26.7 us (26%)
  blocking collectives  22.4 us (22%)
  starting transfers between devices  12.1 us (12%)
    ppermute x9, waiting for transfers between devices, turned(): lax.ppermute(value, axis, [(at, (at + steps) % count) for at in range(cou...  36.7 us
    pallas_call x12, Pallas kernels, call(): pl.pallas_call(kernel, out_shape=outs, in_specs=[VMEM] * len(ins) if inpu...  26.7 us
    all_to_all x1, blocking collectives, local(): lax.all_to_all(send.reshape(shards, capacity, part + LANES), 'seq', split...  22.4 us
    ppermute x9, starting transfers between devices, turned(): lax.ppermute(value, axis, [(at, (at + steps) % count) for at in range(cou...  9.04 us
    ppermute x2, starting transfers between devices, swapped(): return lax.ppermute(value, axis, [(at, at ^ 1) for at in range(count)])  3.07 us
    ppermute x2, waiting for transfers between devices, swapped(): return lax.ppermute(value, axis, [(at, at ^ 1) for at in range(count)])  2.15 us
  transfers between devices with their start and end apart: 11, of which 9 were waited for; matrix products, arithmetic and copies ran while one was open for 0% of the time, Pallas kernels for 11%

profile of v4, /device:TPU:1, one launch (start us, length us, event | category | flops | bytes accessed | tf_op | source)
XLA Modules:
  0.0 101.1 jit_solution(1571902685026536023)
XLA Ops:
  0.0 3.2 %pack.1 = bf16[512,640]{1,0:T(8,128)(2,1)} custom-call(s32[1,256]{1,0:T(1,128)} %bitcast.15, bf16[256,2048]{1,0:T(8,128)(2,1)} %refs_1_.1), custom_call_target="tpu_custom_call" | custom-call | bytes 2000000 | tf_op jit(solution)/shard_map/pack/pallas_call | solution.py:534
  3.2 22.4 %all_to_all.5 = bf16[32,16,640]{2,1,0:T(8,128)(2,1)S(1)} all-to-all(bf16[32,16,640]{2,1,0:T(8,128)(2,1)} %bitcast.14), channel_id=1, replica_groups=mesh['seq'=32,'head'=4] {'seq'}, dimensions={0} | all-to-all | bytes 1310720 | tf_op jit(solution)/shard_map/all_to_all | solution.py:583
  26.2 2.8 %collective-permute-start.2 = (bf16[272,512]{1,0:T(8,128)(2,1)S(1)}, bf16[272,512]{1,0:T(8,128)(2,1)S(1)}, u32[]{:S(2)}, u32[]{:S(2)}) collective-permute-start(bf16[272,512]{1,0:T(8,128)(2,1)S(1)} %place.1.part0_ref), channel_id=1, source_target_pairs={{0,3},{1,0},{2,1},{3,2},{4,7},{5,4},{6,5},{7,6},{8,11},{9,8},{10,9... | collective-permute-start | bytes 835592 | tf_op jit(solution)/shard_map/ppermute | solution.py:511
  30.0 4.7 %fetch.1 = (bf16[2048,512]{1,0:T(8,128)(2,1)S(1)}, bf16[2048,512]{1,0:T(8,128)(2,1)S(1)}, bf16[2048,1024]{1,0:T(8,128)(2,1)S(1)}, bf16[2048,1024]{1,0:T(8,128)(2,1)S(1)}) custom-call(bf16[2048,512]{1,0:T(8,128)(2,1)} %refs_0_, bf16[2048,512]{1,0:T(8,128)(2,1)} %refs_1_.2, bf16[2048,1024]{1,0:T(8,128)(2,1)} %refs_2_, bf16[2048,1024]{1,0:T(8,128)(2,1)} %refs_3_), custom_call_target="tpu_custom_call" | custom-call | bytes 20000000 | tf_op jit(solution)/shard_map/fetch/pallas_call | solution.py:534
  34.7 5.5 %collective-permute-done.2.part3_ref = bf16[272,512]{1,0:T(8,128)(2,1)S(1)} collective-permute-done((bf16[272,512]{1,0:T(8,128)(2,1)S(1)}, bf16[272,512]{1,0:T(8,128)(2,1)S(1)}, u32[]{:S(2)}, u32[]{:S(2)}) %collective-permute-start.2) | collective-permute-done | bytes 278560 | tf_op jit(solution)/shard_map/ppermute | solution.py:511
  40.2 4.8 %collective-permute-done.part1_ref = bf16[272,512]{1,0:T(8,128)(2,1)S(1)} collective-permute-done((bf16[272,512]{1,0:T(8,128)(2,1)S(1)}, bf16[272,512]{1,0:T(8,128)(2,1)S(1)}, u32[]{:S(2)}, u32[]{:S(2)}) %collective-permute-start) | collective-permute-done | bytes 278560 | tf_op jit(solution)/shard_map/ppermute | solution.py:511
  45.1 3.1 %project.1 = (bf16[272,2048]{1,0:T(8,128)(2,1)S(1)}, bf16[272,512]{1,0:T(8,128)(2,1)S(1)}, bf16[272,512]{1,0:T(8,128)(2,1)S(1)}, bf16[272,1024]{1,0:T(8,128)(2,1...) custom-call(bf16[272,512]{1,0:T(8,128)(2,1)S(1)} %place.1.part0_ref, ...), custom_call_target="tpu_custom_call" | custom-call | bytes 2000000 | tf_op jit(solution)/shard_map/project/pallas_call | solution.py:534
  48.2 6.5 %chunk.1 = (bf16[2,4,128,128]{3,2,1,0:T(8,128)(2,1)S(1)}, bf16[2,4,128,128]{3,2,1,0:T(8,128)(2,1)S(1)}, bf16[4,256,128]{2,1,0:T(8,128)(2,1)S(1)}, bf16[8,256,256]{2,1,0:T(8,128)(2,1)S(1)}) custom-call(s32[8]{0:T(128)S(1)} %copy-done.5, bf16[272,512]{1,0:T(8,128)(2,1)S(1)} %get-tuple-element.53.key_ref, bf16[272,1024]{1,0:T(8,128)(2,1)S(1)} %get-tuple-element.54.value_ref, ...), custom_call_target="tpu_custom_call" | custom-call | bytes 2000000 | tf_op jit(solution)/shard_map/chunk/pallas_call | solution.py:534
  55.3 1.2 %collective-permute-done.3.other_ref = bf16[2,4,128,128]{3,2,1,0:T(8,128)(2,1)S(1)} collective-permute-done((bf16[2,4,128,128]{3,2,1,0:T(8,128)(2,1)S(1)}, bf16[2,4,128,128]{3,2,1,0:T(8,128)(2,1)S(1)}, u32[]{:S(2)}, u32[]{:S(2)}) %collective-permute-start.3) | collective-permute-done | bytes 262176 | tf_op jit(solution)/shard_map/ppermute | solution.py:516
  56.7 0.8 collective-permute-start.4
  57.5 2.8 %respond.1 = (f32[256,1024]{1,0:T(8,128)S(1)}, bf16[256,1024]{1,0:T(8,128)(2,1)S(1)}) custom-call(s32[8]{0:T(128)S(1)} %copy-done.5, bf16[272,512]{1,0:T(8,128)(2,1)S(1)} %get-tuple-element.59.query_ref, bf16[4,512]{1,0:T(4,128)(2,1)S(1)} %copy-done.4, f32[256,8]{1,0:T(8,128)S(1)} %get-tuple-element.56.decay_ref, ...), custom_call_target="tpu_custom_call" | custom-call | bytes 16000000 | tf_op jit(solution)/shard_map/respond/pallas_call | solution.py:534
  60.3 1.3 %project_gate.1.zgate_ref = bf16[256,1024]{1,0:T(8,128)(2,1)S(1)} custom-call(bf16[272,2048]{1,0:T(8,128)(2,1)S(1)} %get-tuple-element.63.balanced_ref, bf16[2048,1024]{1,0:T(8,128)(2,1)S(1)} %get-tuple-element.64.w_zgate), custom_call_target="tpu_custom_call" | custom-call | bytes 6000000 | tf_op jit(solution)/shard_map/project_gate/pallas_call | solution.py:534
  61.5 6.2 %collective-permute-done.4.before_ref = bf16[2,4,128,128]{3,2,1,0:T(8,128)(2,1)S(1)} collective-permute-done((bf16[2,4,128,128]{3,2,1,0:T(8,128)(2,1)S(1)}, bf16[2,4,128,128]{3,2,1,0:T(8,128)(2,1)S(1)}, u32[]{:S(2)}, u32[]{:S(2)}) %collective-permute-start.4) | collective-permute-done | bytes 262176 | tf_op jit(solution)/shard_map/ppermute | solution.py:511
  68.1 1.2 %collective-permute-start.6 = (bf16[4,128,128]{2,1,0:T(8,128)(2,1)S(1)}, bf16[4,128,128]{2,1,0:T(8,128)(2,1)S(1)}, u32[]{:S(2)}, u32[]{:S(2)}) collective-permute-start(bf16[4,128,128]{2,1,0:T(8,128)(2,1)S(1)} %get-tuple-element.72), channel_id=1, source_target_pairs={{0,24},{4,28},{8,32},{12,36},{16,40},{20,44},{24,48},{28,52},{32,5... | collective-permute-start | bytes 393224 | tf_op jit(solution)/shard_map/ppermute | solution.py:511
  69.3 2.2 %gate.1 = (f32[256,1024]{1,0:T(8,128)S(1)}, bf16[1024,2048]{1,0:T(8,128)(2,1)S(1)}) custom-call(bf16[256,1024]{1,0:T(8,128)(2,1)S(1)} %project_gate.1.zgate_ref, f32[1,128]{1,0:T(1,128)S(1)} %bitcast.13, bf16[1024,2048]{1,0:T(8,128)(2,1)} %w_out.1), custom_call_target="tpu_custom_call" | custom-call | bytes 10000000 | tf_op jit(solution)/shard_map/gate/pallas_call | solution.py:534
  71.5 2.8 %collective-permute-done.6.far_ref = bf16[4,128,128]{2,1,0:T(8,128)(2,1)S(1)} collective-permute-done((bf16[4,128,128]{2,1,0:T(8,128)(2,1)S(1)}, bf16[4,128,128]{2,1,0:T(8,128)(2,1)S(1)}, u32[]{:S(2)}, u32[]{:S(2)}) %collective-permute-start.6) | collective-permute-done | bytes 131104 | tf_op jit(solution)/shard_map/ppermute | solution.py:511
  74.3 5.0 %collective-permute-done.5.near_ref = bf16[2,4,128,128]{3,2,1,0:T(8,128)(2,1)S(1)} collective-permute-done((bf16[2,4,128,128]{3,2,1,0:T(8,128)(2,1)S(1)}, bf16[2,4,128,128]{3,2,1,0:T(8,128)(2,1)S(1)}, u32[]{:S(2)}, u32[]{:S(2)}) %collective-permute-start.5) | collective-permute-done | bytes 262176 | tf_op jit(solution)/shard_map/ppermute | solution.py:511
  79.7 2.5 %collective-permute-start.7 = (bf16[4,128,128]{2,1,0:T(8,128)(2,1)S(1)}, bf16[4,128,128]{2,1,0:T(8,128)(2,1)S(1)}, u32[]{:S(2)}, u32[]{:S(2)}) collective-permute-start(bf16[4,128,128]{2,1,0:T(8,128)(2,1)S(1)} %get-tuple-element.76), channel_id=1, source_target_pairs={{0,4},{4,0},{8,12},{12,8},{16,20},{20,16},{24,28},{28,24},{32,36},... | collective-permute-start | bytes 393224 | tf_op jit(solution)/shard_map/ppermute | solution.py:516
  82.2 1.0 collective-permute-done.7.other_ref
  83.2 1.6 %finish.1 = (bf16[256,512]{1,0:T(8,128)(2,1)S(1)}, bf16[256,512]{1,0:T(8,128)(2,1)S(1)}, bf16[256,512]{1,0:T(8,128)(2,1)S(1)}, bf16[256,512]{1,0:T(8,128)(2,1)S(1)}) custom-call(f32[256,1024]{1,0:T(8,128)S(1)} %get-tuple-element.65.base_ref, bf16[256,1024]{1,0:T(8,128)(2,1)S(1)} %get-tuple-element.66.response_ref, ...), custom_call_target="tpu_custom_call" | custom-call | bytes 2000000 | tf_op jit(solution)/shard_map/finish/pallas_call | solution.py:534
  85.8 2.1 %collective-permute-start.10 = (bf16[256,512]{1,0:T(8,128)(2,1)S(1)}, bf16[256,512]{1,0:T(8,128)(2,1)S(1)}, u32[]{:S(2)}, u32[]{:S(2)}) collective-permute-start(bf16[256,512]{1,0:T(8,128)(2,1)S(1)} %get-tuple-element.82), channel_id=1, source_target_pairs={{0,3},{1,0},{2,1},{3,2},{4,7},{5,4},{6,5},{7,6},{8,11},{9,8},{10,9... | collective-permute-start | bytes 786440 | tf_op jit(solution)/shard_map/ppermute | solution.py:511
  87.9 6.0 %collective-permute-done.8 = bf16[256,512]{1,0:T(8,128)(2,1)S(1)} collective-permute-done((bf16[256,512]{1,0:T(8,128)(2,1)S(1)}, bf16[256,512]{1,0:T(8,128)(2,1)S(1)}, u32[]{:S(2)}, u32[]{:S(2)}) %collective-permute-start.8) | collective-permute-done | bytes 262176 | tf_op jit(solution)/shard_map/ppermute | solution.py:511
  94.0 6.3 %collective-permute-done.9 = bf16[256,512]{1,0:T(8,128)(2,1)S(1)} collective-permute-done((bf16[256,512]{1,0:T(8,128)(2,1)S(1)}, bf16[256,512]{1,0:T(8,128)(2,1)S(1)}, u32[]{:S(2)}, u32[]{:S(2)}) %collective-permute-start.9) | collective-permute-done | bytes 262176 | tf_op jit(solution)/shard_map/ppermute | solution.py:511
  100.3 0.8 add_convert_fusion
  (30 shorter events, 4.1 us)
Async XLA Ops:
  26.1 18.9 %copy-start = (bf16[2048,8]{0,1:T(8,128)(2,1)S(1)}, bf16[2048,8]{0,1:T(8,128)(2,1)}, u32[]{:S(2)}) copy-start(bf16[2048,8]{0,1:T(8,128)(2,1)} %param.23) | copy-start | bytes 98308
  26.1 18.9 %copy-start.1 = (bf16[2048,8]{0,1:T(8,128)(2,1)S(1)}, bf16[2048,8]{0,1:T(8,128)(2,1)}, u32[]{:S(2)}) copy-start(bf16[2048,8]{0,1:T(8,128)(2,1)} %param.24) | copy-start | bytes 98308
  26.1 18.9 %copy-start.6 = (f32[8]{0:T(128)S(1)}, f32[8]{0:T(128)}, u32[]{:S(2)}) copy-start(f32[8]{0:T(128)} %param.28) | copy-start | bytes 100
  26.1 18.9 %copy-start.7 = (f32[8]{0:T(128)S(1)}, f32[8]{0:T(128)}, u32[]{:S(2)}) copy-start(f32[8]{0:T(128)} %param.29) | copy-start | bytes 100
  26.2 14.1 %collective-permute-start.2 = (bf16[272,512]{1,0:T(8,128)(2,1)S(1)}, bf16[272,512]{1,0:T(8,128)(2,1)S(1)}, u32[]{:S(2)}, u32[]{:S(2)}) collective-permute-start(bf16[272,512]{1,0:T(8,128)(2,1)S(1)} %place.1.part0_ref), channel_id=1, source_target_pairs={{0,3},{1,0},{2,1},{3,2},{4,7},{5,4},{6,5},{7,6},{8,11},{9,8},{10,9... | collective-permute-start | bytes 835592 | tf_op jit(solution)/shard_map/ppermute | solution.py:511
  29.0 11.3 %collective-permute-start.1 = (bf16[272,512]{1,0:T(8,128)(2,1)S(1)}, bf16[272,512]{1,0:T(8,128)(2,1)S(1)}, u32[]{:S(2)}, u32[]{:S(2)}) collective-permute-start(bf16[272,512]{1,0:T(8,128)(2,1)S(1)} %place.1.part0_ref), channel_id=1, source_target_pairs={{0,2},{1,3},{2,0},{3,1},{4,6},{5,7},{6,4},{7,5},{8,10},{9,11},{10,... | collective-permute-start | bytes 835592 | tf_op jit(solution)/shard_map/ppermute | solution.py:511
  29.3 15.7 %collective-permute-start = (bf16[272,512]{1,0:T(8,128)(2,1)S(1)}, bf16[272,512]{1,0:T(8,128)(2,1)S(1)}, u32[]{:S(2)}, u32[]{:S(2)}) collective-permute-start(bf16[272,512]{1,0:T(8,128)(2,1)S(1)} %place.1.part0_ref), channel_id=1, source_target_pairs={{0,1},{1,2},{2,3},{3,0},{4,5},{5,6},{6,7},{7,4},{8,9},{9,10},{10,1... | collective-permute-start | bytes 835592 | tf_op jit(solution)/shard_map/ppermute | solution.py:511
  45.0 3.2 %copy-start.2 = (bf16[4,1024]{1,0:T(4,128)(2,1)S(1)}, bf16[4,1024]{1,0:T(4,128)(2,1)}, u32[]{:S(2)}) copy-start(bf16[4,1024]{1,0:T(4,128)(2,1)} %taps_value.1) | copy-start | bytes 24580
  45.0 3.2 %copy-start.3 = (bf16[4,512]{1,0:T(4,128)(2,1)S(1)}, bf16[4,512]{1,0:T(4,128)(2,1)}, u32[]{:S(2)}) copy-start(bf16[4,512]{1,0:T(4,128)(2,1)} %taps_key.1) | copy-start | bytes 12292
  45.0 3.2 %copy-start.5 = (s32[8]{0:T(128)S(1)}, s32[8]{0:T(128)}, u32[]{:S(2)}) copy-start(s32[8]{0:T(128)} %lengths_ref.3) | copy-start | bytes 100
  45.1 12.4 %copy-start.4 = (bf16[4,512]{1,0:T(4,128)(2,1)S(1)}, bf16[4,512]{1,0:T(4,128)(2,1)}, u32[]{:S(2)}) copy-start(bf16[4,512]{1,0:T(4,128)(2,1)} %taps_query.1) | copy-start | bytes 12292
  54.7 1.7 %collective-permute-start.3 = (bf16[2,4,128,128]{3,2,1,0:T(8,128)(2,1)S(1)}, bf16[2,4,128,128]{3,2,1,0:T(8,128)(2,1)S(1)}, u32[]{:S(2)}, u32[]{:S(2)}) collective-permute-start(bf16[2,4,128,128]{3,2,1,0:T(8,128)(2,1)S(1)} %get-tuple-element.58), channel_id=1, source_target_pairs={{0,4},{4,0},{8,12},{12,8},{16,20},{20,16},{24,28},{28,24},{32,36},... | collective-permute-start | bytes 786440 | tf_op jit(solution)/shard_map/ppermute | solution.py:516
  56.7 12.6 %copy-start.8 = (f32[128]{0:T(128)S(1)}, f32[128]{0:T(128)}, u32[]{:S(2)}) copy-start(f32[128]{0:T(128)} %param.30) | copy-start | bytes 1540
  56.7 11.1 %collective-permute-start.4 = (bf16[2,4,128,128]{3,2,1,0:T(8,128)(2,1)S(1)}, bf16[2,4,128,128]{3,2,1,0:T(8,128)(2,1)S(1)}, u32[]{:S(2)}, u32[]{:S(2)}) collective-permute-start(bf16[2,4,128,128]{3,2,1,0:T(8,128)(2,1)S(1)} %chip.1.chip_ref), channel_id=1, source_target_pairs={{0,8},{4,12},{8,16},{12,20},{16,24},{20,28},{24,32},{28,36},{32,40... | collective-permute-start | bytes 786440 | tf_op jit(solution)/shard_map/ppermute | solution.py:511
  68.0 11.4 %collective-permute-start.5 = (bf16[2,4,128,128]{3,2,1,0:T(8,128)(2,1)S(1)}, bf16[2,4,128,128]{3,2,1,0:T(8,128)(2,1)S(1)}, u32[]{:S(2)}, u32[]{:S(2)}) collective-permute-start(bf16[2,4,128,128]{3,2,1,0:T(8,128)(2,1)S(1)} %get-tuple-element.69), channel_id=1, source_target_pairs={{0,8},{4,12},{8,16},{12,20},{16,24},{20,28},{24,32},{28,36},{32,40... | collective-permute-start | bytes 786440 | tf_op jit(solution)/shard_map/ppermute | solution.py:511
  68.1 6.3 %collective-permute-start.6 = (bf16[4,128,128]{2,1,0:T(8,128)(2,1)S(1)}, bf16[4,128,128]{2,1,0:T(8,128)(2,1)S(1)}, u32[]{:S(2)}, u32[]{:S(2)}) collective-permute-start(bf16[4,128,128]{2,1,0:T(8,128)(2,1)S(1)} %get-tuple-element.72), channel_id=1, source_target_pairs={{0,24},{4,28},{8,32},{12,36},{16,40},{20,44},{24,48},{28,52},{32,5... | collective-permute-start | bytes 393224 | tf_op jit(solution)/shard_map/ppermute | solution.py:511
  79.7 3.5 %collective-permute-start.7 = (bf16[4,128,128]{2,1,0:T(8,128)(2,1)S(1)}, bf16[4,128,128]{2,1,0:T(8,128)(2,1)S(1)}, u32[]{:S(2)}, u32[]{:S(2)}) collective-permute-start(bf16[4,128,128]{2,1,0:T(8,128)(2,1)S(1)} %get-tuple-element.76), channel_id=1, source_target_pairs={{0,4},{4,0},{8,12},{12,8},{16,20},{20,16},{24,28},{28,24},{32,36},... | collective-permute-start | bytes 393224 | tf_op jit(solution)/shard_map/ppermute | solution.py:516
  84.8 9.2 %collective-permute-start.8 = (bf16[256,512]{1,0:T(8,128)(2,1)S(1)}, bf16[256,512]{1,0:T(8,128)(2,1)S(1)}, u32[]{:S(2)}, u32[]{:S(2)}) collective-permute-start(bf16[256,512]{1,0:T(8,128)(2,1)S(1)} %get-tuple-element.80), channel_id=1, source_target_pairs={{0,2},{1,3},{2,0},{3,1},{4,6},{5,7},{6,4},{7,5},{8,10},{9,11},{10,... | collective-permute-start | bytes 786440 | tf_op jit(solution)/shard_map/ppermute | solution.py:511
  85.3 15.0 %collective-permute-start.9 = (bf16[256,512]{1,0:T(8,128)(2,1)S(1)}, bf16[256,512]{1,0:T(8,128)(2,1)S(1)}, u32[]{:S(2)}, u32[]{:S(2)}) collective-permute-start(bf16[256,512]{1,0:T(8,128)(2,1)S(1)} %get-tuple-element.81), channel_id=1, source_target_pairs={{0,1},{1,2},{2,3},{3,0},{4,5},{5,6},{6,7},{7,4},{8,9},{9,10},{10,1... | collective-permute-start | bytes 786440 | tf_op jit(solution)/shard_map/ppermute | solution.py:511
  85.8 14.4 %collective-permute-start.10 = (bf16[256,512]{1,0:T(8,128)(2,1)S(1)}, bf16[256,512]{1,0:T(8,128)(2,1)S(1)}, u32[]{:S(2)}, u32[]{:S(2)}) collective-permute-start(bf16[256,512]{1,0:T(8,128)(2,1)S(1)} %get-tuple-element.82), channel_id=1, source_target_pairs={{0,3},{1,0},{2,1},{3,2},{4,7},{5,4},{6,5},{7,6},{8,11},{9,8},{10,9... | collective-permute-start | bytes 786440 | tf_op jit(solution)/shard_map/ppermute | solution.py:511

commit v5 on v4

--- a/solution.py
+++ b/solution.py
@@ -119,49 +119,49 @@
         copy.wait()
 
 
+def rows_of(steps, width):
+    groups = lax.axis_size("head")
+    at = lax.rem(lax.axis_index("head") + groups - steps, groups) * width
+    return pl.ds(pl.multiple_of(at, width), width)
+
+
+ACROSS = ((1,), (1,))
+
+
 def project_kernel(
     part0_ref,
-    part1_ref,
     part2_ref,
-    part3_ref,
     w_query,
     w_key,
     w_value,
     w_beta,
     w_alpha,
-    decay_log,
-    decay_bias,
-    balanced_ref,
     query_ref,
     key_ref,
     value_ref,
     beta_ref,
-    decay_ref,
+    alpha_ref,
 ):
-    parts = (part0_ref, part1_ref, part2_ref, part3_ref)
     width = part0_ref.shape[1]
-    here = lax.axis_index("head")
-    for steps, part in enumerate(parts):
-        at = lax.rem(here + len(parts) - steps, len(parts)) * width
-        balanced_ref[:, pl.ds(pl.multiple_of(at, width), width)] = part[...]
-    balanced = balanced_ref[...]
-    across = ((1,), (1,))
-    for weight, to in ((w_query, query_ref), (w_key, key_ref), (w_value, value_ref)):
+    parts = [(rows_of(0, width), part0_ref), (rows_of(2, width), part2_ref)]
+    for weight, to in ((w_key, key_ref), (w_value, value_ref), (w_query, query_ref)):
         for start in range(0, to.shape[1], 512):
-            part = dot(balanced, weight[:, start : start + 512])
-            to[:, start : start + 512] = part.astype(BF16)
-    balanced = balanced_ref[TAIL:]
-    beta_ref[...] = jax.nn.sigmoid(dot(balanced, w_beta[...], across))
-    decay_ref[...] = -jnp.exp(decay_log[...]) * softplus(
-        dot(balanced, w_alpha[...], across) + decay_bias[...]
-    )
-
-
-def project_gate_kernel(balanced_ref, w_zgate, zgate_ref):
-    balanced = balanced_ref[TAIL:]
+            column = slice(start, start + 512)
+            to[:, column] = sum(dot(part[...], weight[at, column]) for at, part in parts)
+    for weight, to in ((w_beta, beta_ref), (w_alpha, alpha_ref)):
+        to[...] = sum(dot(part[TAIL:], weight[:, at], ACROSS) for at, part in parts)
+
+
+def project_gate_kernel(part0_ref, part1_ref, part2_ref, part3_ref, w_zgate, zgate_ref):
+    width = part0_ref.shape[1]
+    parts = [
+        (rows_of(n, width), part)
+        for n, part in enumerate((part0_ref, part1_ref, part2_ref, part3_ref))
+    ]
     for start in range(0, zgate_ref.shape[1], 512):
-        part = dot(balanced, w_zgate[:, start : start + 512])
-        zgate_ref[:, start : start + 512] = part.astype(BF16)
+        column = slice(start, start + 512)
+        total = sum(dot(part[TAIL:], w_zgate[at, column]) for at, part in parts)
+        zgate_ref[:, column] = total.astype(BF16)
 
 
 def silu(x):
@@ -212,10 +212,10 @@
     return segment, same, inside, carries
 
 
-def cumulated(decay_ref):
-    rows, heads = decay_ref.shape
+def cumulated(decay):
+    rows, heads = decay.shape
     lower = (iota((rows, rows), 0) >= iota((rows, rows), 1)).astype(F32)
-    down = dot(lower, decay_ref[...], precision=HIGHEST)
+    down = dot(lower, decay, precision=HIGHEST)
     padded = jnp.concatenate([down, jnp.zeros((rows, LANES - heads), F32)], axis=1)
     return down, padded.T
 
@@ -235,16 +235,30 @@
 
 def chunk_kernel(
     lengths_ref,
-    key_ref,
-    value_ref,
+    part1_ref,
+    part3_ref,
+    query_sum,
+    key_sum,
+    value_sum,
+    beta_sum,
+    alpha_sum,
+    w_query,
+    w_key,
+    w_value,
+    w_beta,
+    w_alpha,
+    decay_log,
+    decay_bias,
     taps_key,
     taps_value,
-    beta_ref,
-    decay_ref,
     mine_ref,
     send_ref,
     keys,
     solved_ref,
+    query_ref,
+    decay_ref,
+    key_ref,
+    value_ref,
     system_ref,
     packed_ref,
     inverse_ref,
@@ -253,12 +267,28 @@
     states_ref,
     right_ref,
 ):
-    rows = beta_ref.shape[0]
+    rows, heads = beta_sum.shape
+    width = part1_ref.shape[1]
+    parts = [(rows_of(1, width), part1_ref), (rows_of(3, width), part3_ref)]
+
+    def project(weight, before, to, start):
+        at = slice(start, start + 512)
+        total = sum(dot(part[...], weight[own, at]) for own, part in parts)
+        to[:, at] = (before[:, at] + total).astype(BF16)
+
+    def small_project(weight, before):
+        return before[...] + sum(dot(part[TAIL:], weight[:, own], ACROSS) for own, part in parts)
+
+    beta_all = jax.nn.sigmoid(small_project(w_beta, beta_sum))
+    alpha = small_project(w_alpha, alpha_sum)
+    decay = -jnp.exp(decay_log[...]) * softplus(alpha + decay_bias[...])
+    decay_ref[...] = decay
+    project(w_key, key_sum, key_ref, 0)
+    fillers = [(w_value, value_sum, value_ref, at) for at in range(0, value_ref.shape[1], 512)]
+    fillers += [(w_query, query_sum, query_ref, at) for at in range(0, query_ref.shape[1], 512)]
     first, core = lax.axis_index("seq") * rows, my_core()
-    heads = beta_ref.shape[1]
     key_heads = key_ref.shape[1] // HEAD
     repeat = heads // key_heads
-    width = key_ref.shape[1]
     segment, same, inside, carries = masks(first, document_ends(lengths_ref), rows)
     row, column = iota((rows, rows), 0), iota((rows, rows), 1)
     small = rows // PACKED
@@ -280,7 +310,7 @@
     def spread(packed):
         return jnp.concatenate([packed * block for block in blocks], axis=0)
     strict = inside & (row > column)
-    down, across = cumulated(decay_ref)
+    down, across = cumulated(decay)
 
     for kh in range(key_heads):
         at = column_of(kh)
@@ -289,15 +319,8 @@
         ).astype(BF16)
         inner = dot(keys[kh], keys[kh], ((1,), (1,)))
         for h in range(kh * repeat, (kh + 1) * repeat):
-            system = beta_ref[:, h : h + 1] * inner * between(down, across, h, strict)
+            system = beta_all[:, h : h + 1] * inner * between(down, across, h, strict)
             system_ref[h] = system.astype(BF16)
-    for h in range(heads):
-        at = column_of(h)
-        beta = beta_ref[:, h : h + 1]
-        carried = jnp.exp(down[:, h : h + 1]) * carries
-        value = convolve(value_ref[:, at], taps_value[:, at], same)
-        right_ref[h, :, :HEAD] = (beta * value).astype(BF16)
-        right_ref[h, :, HEAD:] = (beta * carried * keys[h // repeat].astype(F32)).astype(BF16)
     for h in range(heads):
         packed = None
         for i in range(PACKED):
@@ -306,10 +329,19 @@
         packed_ref[h] = packed
         inverse_ref[h] = diagonal - packed * mask_ref[0]
     for level in range(1, levels):
+        if fillers:
+            project(*fillers.pop(0))
         for h in range(heads):
             inverse = inverse_ref[h]
             part = dot(packed_ref[h] * mask_ref[level], spread(inverse)).astype(BF16)
             inverse_ref[h] = inverse - dot(inverse, spread(part)).astype(BF16)
+    for h in range(heads):
+        at = column_of(h)
+        beta = beta_all[:, h : h + 1]
+        carried = jnp.exp(down[:, h : h + 1]) * carries
+        value = convolve(value_ref[:, at], taps_value[:, at], same)
+        right_ref[h, :, :HEAD] = (beta * value).astype(BF16)
+        right_ref[h, :, HEAD:] = (beta * carried * keys[h // repeat].astype(F32)).astype(BF16)
     zero = jnp.zeros((small, rows), BF16)
     for h in range(heads):
         inverse = inverse_ref[h]
@@ -357,9 +389,11 @@
         send_ref[...] = states_ref[:, :half]
 
 
-def chunk_scratch(heads, rows):
+def chunk_scratch(heads, rows, key_width, value_width):
     small = rows // PACKED
     return [
+        pltpu.VMEM((TAIL + rows, key_width), BF16),
+        pltpu.VMEM((TAIL + rows, value_width), BF16),
         pltpu.VMEM((heads, rows, rows), BF16),
         pltpu.VMEM((heads, small, rows), BF16),
         pltpu.VMEM((heads, small, rows), BF16),
@@ -387,7 +421,7 @@
         lax.axis_index("seq") * rows, document_ends(lengths_ref), rows
     )
     inside = inside & (iota((rows, rows), 0) >= iota((rows, rows), 1))
-    down, across = cumulated(decay_ref)
+    down, across = cumulated(decay_ref[...])
     for kh in range(key_heads):
         at = column_of(kh)
         query = unit(
@@ -599,36 +633,59 @@
         specs=(ANY,) * len(weights),
         cost=20_000_000,
     )
-    balanced, query, key, value, beta, decay = call(
+    w_beta, w_alpha = w_beta.T, w_alpha.T
+    decay_log, decay_bias = decay_log.reshape(1, heads), decay_bias.reshape(1, heads)
+    w_query, w_key, w_value, w_zgate = [vmem(weight) for weight in fetched]
+    f32 = lambda *shape: out(*shape, dtype=F32)
+    query_sum, key_sum, value_sum, beta_sum, alpha_sum = call(
         project_kernel,
         "project",
         (
-            out(TAIL + rows, width),
+            f32(TAIL + rows, qk),
+            f32(TAIL + rows, qk),
+            f32(TAIL + rows, vw),
+            f32(rows, heads),
+            f32(rows, heads),
+        ),
+        (parts[0], parts[2], w_query, w_key, w_value, w_beta, w_alpha),
+        8,
+        cost=10_000_000,
+    )
+    key_sum, part1, part3 = lax.optimization_barrier((key_sum, parts[1], parts[3]))
+    states = out(2, half, HEAD, HEAD)
+    mine, sent, keys, solved, query, decay = call(
+        chunk_kernel,
+        "chunk",
+        (
+            states,
+            states,
+            out(key_heads, rows, HEAD),
+            out(heads, rows, 2 * HEAD),
             out(TAIL + rows, qk),
-            out(TAIL + rows, qk),
-            out(TAIL + rows, vw),
-            out(rows, heads, dtype=F32),
-            out(rows, heads, dtype=F32),
+            f32(rows, heads),
         ),
         (
-            *parts,
-            *[vmem(weight) for weight in fetched[:3]],
-            w_beta.T,
-            w_alpha.T,
-            decay_log.reshape(1, heads),
-            decay_bias.reshape(1, heads),
+            doc_lengths,
+            part1,
+            part3,
+            query_sum,
+            key_sum,
+            value_sum,
+            beta_sum,
+            alpha_sum,
+            w_query,
+            w_key,
+            w_value,
+            w_beta,
+            w_alpha,
+            decay_log,
+            decay_bias,
+            conv_key,
+            conv_value,
         ),
-        8,
-    )
-    states = out(2, half, HEAD, HEAD)
-    mine, sent, keys, solved = call(
-        chunk_kernel,
-        "chunk",
-        (states, states, out(key_heads, rows, HEAD), out(heads, rows, 2 * HEAD)),
-        (doc_lengths, key, value, conv_key, conv_value, beta, decay),
-        16,
-        scratch=chunk_scratch(heads, rows),
-        inputs=[SMEM] + [VMEM] * 6,
+        20,
+        scratch=chunk_scratch(heads, rows, qk, vw),
+        inputs=[SMEM] + [VMEM] * 16,
     )
     other = swapped(sent, "seq")
     chip = call(chip_kernel, "chip", states, (mine, other), 4)
@@ -646,7 +703,7 @@
         project_gate_kernel,
         "project_gate",
         out(rows, vw),
-        (after(balanced, base), vmem(fetched[3])),
+        (after(parts[0], base), *parts[1:], w_zgate),
         8,
         cost=6_000_000,
     )

time: 101 us -> 96.7 us (0.957)
  waiting for transfers between devices: 38.8 us -> 31.6 us
  starting transfers between devices: 12.1 us -> 15.3 us
    ppermute x9, waiting for transfers between devices: 36.7 us -> 29.5 us  [turned(): lax.ppermute(value, axis, [(at, (at + steps) % count) for at in range(cou...]
    ppermute x9, starting transfers between devices: 9.04 us -> 11.8 us  [turned(): lax.ppermute(value, axis, [(at, (at + steps) % count) for at in range(cou...]
  transfers between devices with their start and end apart: 11 -> 11, of which waited for: 9 -> 10; matrix products, arithmetic and copies ran while one was open for 0% -> 0% of each run, Pallas kernels for 11% -> 13%
where the time goes in v5:
time: 96.7 us; the launch traced here: 96.5 us
  waiting for transfers between devices  31.6 us (33%)
  Pallas kernels  26.1 us (27%)
  blocking collectives  22.4 us (23%)
  starting transfers between devices  15.3 us (16%)
    ppermute x9, waiting for transfers between devices, turned(): lax.ppermute(value, axis, [(at, (at + steps) % count) for at in range(cou...  29.5 us
    pallas_call x12, Pallas kernels, call(): pl.pallas_call(kernel, out_shape=outs, in_specs=[VMEM] * len(ins) if inpu...  26.1 us
    all_to_all x1, blocking collectives, local(): lax.all_to_all(send.reshape(shards, capacity, part + LANES), 'seq', split...  22.4 us
    ppermute x9, starting transfers between devices, turned(): lax.ppermute(value, axis, [(at, (at + steps) % count) for at in range(cou...  11.8 us
    ppermute x2, starting transfers between devices, swapped(): return lax.ppermute(value, axis, [(at, at ^ 1) for at in range(count)])  3.46 us
    ppermute x2, waiting for transfers between devices, swapped(): return lax.ppermute(value, axis, [(at, at ^ 1) for at in range(count)])  2.15 us
  transfers between devices with their start and end apart: 11, of which 10 were waited for; matrix products, arithmetic and copies ran while one was open for 0% of the time, Pallas kernels for 13%

profile of v5, /device:TPU:1, one launch (start us, length us, event | category | flops | bytes accessed | tf_op | source)
XLA Modules:
  0.0 96.5 jit_solution(5072158174195612256)
XLA Ops:
  0.0 3.2 %pack.1 = bf16[512,640]{1,0:T(8,128)(2,1)} custom-call(s32[1,256]{1,0:T(1,128)} %bitcast.17, bf16[256,2048]{1,0:T(8,128)(2,1)} %refs_1_.1), custom_call_target="tpu_custom_call" | custom-call | bytes 2000000 | tf_op jit(solution)/shard_map/pack/pallas_call | solution.py:568
  3.2 22.4 %all_to_all.5 = bf16[32,16,640]{2,1,0:T(8,128)(2,1)S(1)} all-to-all(bf16[32,16,640]{2,1,0:T(8,128)(2,1)} %bitcast.16), channel_id=1, replica_groups=mesh['seq'=32,'head'=4] {'seq'}, dimensions={0} | all-to-all | bytes 1310720 | tf_op jit(solution)/shard_map/all_to_all | solution.py:617
  26.1 3.0 %collective-permute-start = (bf16[272,512]{1,0:T(8,128)(2,1)S(1)}, bf16[272,512]{1,0:T(8,128)(2,1)S(1)}, u32[]{:S(2)}, u32[]{:S(2)}) collective-permute-start(bf16[272,512]{1,0:T(8,128)(2,1)S(1)} %place.1.part0_ref), channel_id=1, source_target_pairs={{0,2},{1,3},{2,0},{3,1},{4,6},{5,7},{6,4},{7,5},{8,10},{9,11},{10,... | collective-permute-start | bytes 835592 | tf_op jit(solution)/shard_map/ppermute | solution.py:545
  30.6 4.7 %fetch.1 = (bf16[2048,512]{1,0:T(8,128)(2,1)S(1)}, bf16[2048,512]{1,0:T(8,128)(2,1)S(1)}, bf16[2048,1024]{1,0:T(8,128)(2,1)S(1)}, bf16[2048,1024]{1,0:T(8,128)(2,1)S(1)}) custom-call(bf16[2048,512]{1,0:T(8,128)(2,1)} %refs_0_, bf16[2048,512]{1,0:T(8,128)(2,1)} %refs_1_.2, bf16[2048,1024]{1,0:T(8,128)(2,1)} %refs_2_, bf16[2048,1024]{1,0:T(8,128)(2,1)} %refs_3_), custom_call_target="tpu_custom_call" | custom-call | bytes 20000000 | tf_op jit(solution)/shard_map/fetch/pallas_call | solution.py:568
  35.4 1.6 %project.1 = (f32[272,512]{1,0:T(8,128)S(1)}, f32[272,512]{1,0:T(8,128)S(1)}, f32[272,1024]{1,0:T(8,128)S(1)}, f32[256,8]{1,0:T(8,128)S(1)}, f32[256,8]{1,0:T(8,128)S(1)}) custom-call(bf16[272,512]{1,0:T(8,128)(2,1)S(1)} %place.1.part0_ref, bf16[272,512]{1,0:T(8,128)(2,1)S(1)} %collective-permute-done.part2_ref, ...), custom_call_target="tpu_custom_call" | custom-call | bytes 10000000 | tf_op jit(solution)/shard_map/project/pallas_call | solution.py:568
  37.0 4.7 %collective-permute-done.2.part3_ref = bf16[272,512]{1,0:T(8,128)(2,1)S(1)} collective-permute-done((bf16[272,512]{1,0:T(8,128)(2,1)S(1)}, bf16[272,512]{1,0:T(8,128)(2,1)S(1)}, u32[]{:S(2)}, u32[]{:S(2)}) %collective-permute-start.2) | collective-permute-done | bytes 278560 | tf_op jit(solution)/shard_map/ppermute | solution.py:545
  42.3 7.4 %chunk.1 = (bf16[2,4,128,128]{3,2,1,0:T(8,128)(2,1)S(1)}, bf16[2,4,128,128]{3,2,1,0:T(8,128)(2,1)S(1)}, bf16[4,256,128]{2,1,0:T(8,128)(2,1)S(1)}, bf16[8,256,256...) custom-call(s32[8]{0:T(128)S(1)} %copy-done.5, ...), custom_call_target="tpu_custom_call" | custom-call | bytes 2000000 | tf_op jit(solution)/shard_map/chunk/pallas_call | solution.py:568
  49.7 0.9 collective-permute-start.3
  50.6 1.2 %collective-permute-done.3.other_ref = bf16[2,4,128,128]{3,2,1,0:T(8,128)(2,1)S(1)} collective-permute-done((bf16[2,4,128,128]{3,2,1,0:T(8,128)(2,1)S(1)}, bf16[2,4,128,128]{3,2,1,0:T(8,128)(2,1)S(1)}, u32[]{:S(2)}, u32[]{:S(2)}) %collective-permute-start.3) | collective-permute-done | bytes 262176 | tf_op jit(solution)/shard_map/ppermute | solution.py:550
  52.8 2.8 %respond.1 = (f32[256,1024]{1,0:T(8,128)S(1)}, bf16[256,1024]{1,0:T(8,128)(2,1)S(1)}) custom-call(s32[8]{0:T(128)S(1)} %copy-done.5, bf16[272,512]{1,0:T(8,128)(2,1)S(1)} %get-tuple-element.66.query_ref, bf16[4,512]{1,0:T(4,128)(2,1)S(1)} %copy-done.4, f32[256,8]{1,0:T(8,128)S(1)} %get-tuple-element.67.decay_ref, ...), custom_call_target="tpu_custom_call" | custom-call | bytes 16000000 | tf_op jit(solution)/shard_map/respond/pallas_call | solution.py:568
  55.6 1.3 %project_gate.1.zgate_ref = bf16[256,1024]{1,0:T(8,128)(2,1)S(1)} custom-call(bf16[272,512]{1,0:T(8,128)(2,1)S(1)} %place.1.part0_ref, bf16[272,512]{1,0:T(8,128)(2,1)S(1)} %collective-permute-done.1.part1_ref, bf16[272,512]{1,0:T(8,128)(2,1)S(1)} %collective-permute-done.part2_ref, bf16[272,512]{1,0:T(8,128)(2,1)S(1)} %collective-permute-done.2.part3_ref, ...), custom_call_target="tpu_custom_call" | custom-call | bytes 6000000 | tf_op jit(solution)/shard_map/project_gate/pallas_call | solution.py:568
  56.9 6.2 %collective-permute-done.4.before_ref = bf16[2,4,128,128]{3,2,1,0:T(8,128)(2,1)S(1)} collective-permute-done((bf16[2,4,128,128]{3,2,1,0:T(8,128)(2,1)S(1)}, bf16[2,4,128,128]{3,2,1,0:T(8,128)(2,1)S(1)}, u32[]{:S(2)}, u32[]{:S(2)}) %collective-permute-start.4) | collective-permute-done | bytes 262176 | tf_op jit(solution)/shard_map/ppermute | solution.py:545
  63.4 1.2 %collective-permute-start.6 = (bf16[4,128,128]{2,1,0:T(8,128)(2,1)S(1)}, bf16[4,128,128]{2,1,0:T(8,128)(2,1)S(1)}, u32[]{:S(2)}, u32[]{:S(2)}) collective-permute-start(bf16[4,128,128]{2,1,0:T(8,128)(2,1)S(1)} %get-tuple-element.80), channel_id=1, source_target_pairs={{0,24},{4,28},{8,32},{12,36},{16,40},{20,44},{24,48},{28,52},{32,5... | collective-permute-start | bytes 393224 | tf_op jit(solution)/shard_map/ppermute | solution.py:545
  64.6 2.2 %gate.1 = (f32[256,1024]{1,0:T(8,128)S(1)}, bf16[1024,2048]{1,0:T(8,128)(2,1)S(1)}) custom-call(bf16[256,1024]{1,0:T(8,128)(2,1)S(1)} %project_gate.1.zgate_ref, f32[1,128]{1,0:T(1,128)S(1)} %bitcast.15, bf16[1024,2048]{1,0:T(8,128)(2,1)} %w_out.1), custom_call_target="tpu_custom_call" | custom-call | bytes 10000000 | tf_op jit(solution)/shard_map/gate/pallas_call | solution.py:568
  66.9 2.8 %collective-permute-done.6.far_ref = bf16[4,128,128]{2,1,0:T(8,128)(2,1)S(1)} collective-permute-done((bf16[4,128,128]{2,1,0:T(8,128)(2,1)S(1)}, bf16[4,128,128]{2,1,0:T(8,128)(2,1)S(1)}, u32[]{:S(2)}, u32[]{:S(2)}) %collective-permute-start.6) | collective-permute-done | bytes 131104 | tf_op jit(solution)/shard_map/ppermute | solution.py:545
  69.7 5.0 %collective-permute-done.5.near_ref = bf16[2,4,128,128]{3,2,1,0:T(8,128)(2,1)S(1)} collective-permute-done((bf16[2,4,128,128]{3,2,1,0:T(8,128)(2,1)S(1)}, bf16[2,4,128,128]{3,2,1,0:T(8,128)(2,1)S(1)}, u32[]{:S(2)}, u32[]{:S(2)}) %collective-permute-start.5) | collective-permute-done | bytes 262176 | tf_op jit(solution)/shard_map/ppermute | solution.py:545
  75.0 2.5 %collective-permute-start.7 = (bf16[4,128,128]{2,1,0:T(8,128)(2,1)S(1)}, bf16[4,128,128]{2,1,0:T(8,128)(2,1)S(1)}, u32[]{:S(2)}, u32[]{:S(2)}) collective-permute-start(bf16[4,128,128]{2,1,0:T(8,128)(2,1)S(1)} %get-tuple-element.84), channel_id=1, source_target_pairs={{0,4},{4,0},{8,12},{12,8},{16,20},{20,16},{24,28},{28,24},{32,36},... | collective-permute-start | bytes 393224 | tf_op jit(solution)/shard_map/ppermute | solution.py:550
  77.5 1.0 %collective-permute-done.7.other_ref = bf16[4,128,128]{2,1,0:T(8,128)(2,1)S(1)} collective-permute-done((bf16[4,128,128]{2,1,0:T(8,128)(2,1)S(1)}, bf16[4,128,128]{2,1,0:T(8,128)(2,1)S(1)}, u32[]{:S(2)}, u32[]{:S(2)}) %collective-permute-start.7) | collective-permute-done | bytes 131104 | tf_op jit(solution)/shard_map/ppermute | solution.py:550
  78.5 1.6 %finish.1 = (bf16[256,512]{1,0:T(8,128)(2,1)S(1)}, bf16[256,512]{1,0:T(8,128)(2,1)S(1)}, bf16[256,512]{1,0:T(8,128)(2,1)S(1)}, bf16[256,512]{1,0:T(8,128)(2,1)S(1)}) custom-call(f32[256,1024]{1,0:T(8,128)S(1)} %get-tuple-element.73.base_ref, bf16[256,1024]{1,0:T(8,128)(2,1)S(1)} %get-tuple-element.74.response_ref, ...), custom_call_target="tpu_custom_call" | custom-call | bytes 2000000 | tf_op jit(solution)/shard_map/finish/pallas_call | solution.py:568
  80.2 2.6 %collective-permute-start.8 = (bf16[256,512]{1,0:T(8,128)(2,1)S(1)}, bf16[256,512]{1,0:T(8,128)(2,1)S(1)}, u32[]{:S(2)}, u32[]{:S(2)}) collective-permute-start(bf16[256,512]{1,0:T(8,128)(2,1)S(1)} %get-tuple-element.88), channel_id=1, source_target_pairs={{0,2},{1,3},{2,0},{3,1},{4,6},{5,7},{6,4},{7,5},{8,10},{9,11},{10,... | collective-permute-start | bytes 786440 | tf_op jit(solution)/shard_map/ppermute | solution.py:545
  83.2 2.3 %collective-permute-start.10 = (bf16[256,512]{1,0:T(8,128)(2,1)S(1)}, bf16[256,512]{1,0:T(8,128)(2,1)S(1)}, u32[]{:S(2)}, u32[]{:S(2)}) collective-permute-start(bf16[256,512]{1,0:T(8,128)(2,1)S(1)} %get-tuple-element.90), channel_id=1, source_target_pairs={{0,3},{1,0},{2,1},{3,2},{4,7},{5,4},{6,5},{7,6},{8,11},{9,8},{10,9... | collective-permute-start | bytes 786440 | tf_op jit(solution)/shard_map/ppermute | solution.py:545
  85.5 3.9 %collective-permute-done.8 = bf16[256,512]{1,0:T(8,128)(2,1)S(1)} collective-permute-done((bf16[256,512]{1,0:T(8,128)(2,1)S(1)}, bf16[256,512]{1,0:T(8,128)(2,1)S(1)}, u32[]{:S(2)}, u32[]{:S(2)}) %collective-permute-start.8) | collective-permute-done | bytes 262176 | tf_op jit(solution)/shard_map/ppermute | solution.py:545
  89.3 6.3 %collective-permute-done.9 = bf16[256,512]{1,0:T(8,128)(2,1)S(1)} collective-permute-done((bf16[256,512]{1,0:T(8,128)(2,1)S(1)}, bf16[256,512]{1,0:T(8,128)(2,1)S(1)}, u32[]{:S(2)}, u32[]{:S(2)}) %collective-permute-start.9) | collective-permute-done | bytes 262176 | tf_op jit(solution)/shard_map/ppermute | solution.py:545
  95.6 0.8 add_convert_fusion
  (30 shorter events, 4.7 us)
Async XLA Ops:
  26.1 9.3 %copy-start = (bf16[2048,8]{0,1:T(8,128)(2,1)S(1)}, bf16[2048,8]{0,1:T(8,128)(2,1)}, u32[]{:S(2)}) copy-start(bf16[2048,8]{0,1:T(8,128)(2,1)} %param.23) | copy-start | bytes 98308
  26.1 9.3 %copy-start.1 = (bf16[2048,8]{0,1:T(8,128)(2,1)S(1)}, bf16[2048,8]{0,1:T(8,128)(2,1)}, u32[]{:S(2)}) copy-start(bf16[2048,8]{0,1:T(8,128)(2,1)} %param.24) | copy-start | bytes 98308
  26.1 9.3 %collective-permute-start = (bf16[272,512]{1,0:T(8,128)(2,1)S(1)}, bf16[272,512]{1,0:T(8,128)(2,1)S(1)}, u32[]{:S(2)}, u32[]{:S(2)}) collective-permute-start(bf16[272,512]{1,0:T(8,128)(2,1)S(1)} %place.1.part0_ref), channel_id=1, source_target_pairs={{0,2},{1,3},{2,0},{3,1},{4,6},{5,7},{6,4},{7,5},{8,10},{9,11},{10,... | collective-permute-start | bytes 835592 | tf_op jit(solution)/shard_map/ppermute | solution.py:545
  29.1 12.6 %collective-permute-start.2 = (bf16[272,512]{1,0:T(8,128)(2,1)S(1)}, bf16[272,512]{1,0:T(8,128)(2,1)S(1)}, u32[]{:S(2)}, u32[]{:S(2)}) collective-permute-start(bf16[272,512]{1,0:T(8,128)(2,1)S(1)} %place.1.part0_ref), channel_id=1, source_target_pairs={{0,3},{1,0},{2,1},{3,2},{4,7},{5,4},{6,5},{7,6},{8,11},{9,8},{10,9... | collective-permute-start | bytes 835592 | tf_op jit(solution)/shard_map/ppermute | solution.py:545
  29.9 12.4 %collective-permute-start.1 = (bf16[272,512]{1,0:T(8,128)(2,1)S(1)}, bf16[272,512]{1,0:T(8,128)(2,1)S(1)}, u32[]{:S(2)}, u32[]{:S(2)}) collective-permute-start(bf16[272,512]{1,0:T(8,128)(2,1)S(1)} %place.1.part0_ref), channel_id=1, source_target_pairs={{0,1},{1,2},{2,3},{3,0},{4,5},{5,6},{6,7},{7,4},{8,9},{9,10},{10,1... | collective-permute-start | bytes 835592 | tf_op jit(solution)/shard_map/ppermute | solution.py:545
  35.4 6.9 %copy-start.2 = (bf16[4,1024]{1,0:T(4,128)(2,1)S(1)}, bf16[4,1024]{1,0:T(4,128)(2,1)}, u32[]{:S(2)}) copy-start(bf16[4,1024]{1,0:T(4,128)(2,1)} %taps_value.1) | copy-start | bytes 24580
  35.4 6.9 %copy-start.3 = (bf16[4,512]{1,0:T(4,128)(2,1)S(1)}, bf16[4,512]{1,0:T(4,128)(2,1)}, u32[]{:S(2)}) copy-start(bf16[4,512]{1,0:T(4,128)(2,1)} %taps_key.1) | copy-start | bytes 12292
  35.4 6.9 %copy-start.5 = (s32[8]{0:T(128)S(1)}, s32[8]{0:T(128)}, u32[]{:S(2)}) copy-start(s32[8]{0:T(128)} %lengths_ref.3) | copy-start | bytes 100
  35.4 6.9 %copy-start.6 = (f32[8]{0:T(128)S(1)}, f32[8]{0:T(128)}, u32[]{:S(2)}) copy-start(f32[8]{0:T(128)} %param.28) | copy-start | bytes 100
  35.4 6.9 %copy-start.7 = (f32[8]{0:T(128)S(1)}, f32[8]{0:T(128)}, u32[]{:S(2)}) copy-start(f32[8]{0:T(128)} %param.29) | copy-start | bytes 100
  42.3 10.5 %copy-start.4 = (bf16[4,512]{1,0:T(4,128)(2,1)S(1)}, bf16[4,512]{1,0:T(4,128)(2,1)}, u32[]{:S(2)}) copy-start(bf16[4,512]{1,0:T(4,128)(2,1)} %taps_query.1) | copy-start | bytes 12292
  49.7 2.1 %collective-permute-start.3 = (bf16[2,4,128,128]{3,2,1,0:T(8,128)(2,1)S(1)}, bf16[2,4,128,128]{3,2,1,0:T(8,128)(2,1)S(1)}, u32[]{:S(2)}, u32[]{:S(2)}) collective-permute-start(bf16[2,4,128,128]{3,2,1,0:T(8,128)(2,1)S(1)} %get-tuple-element.65), channel_id=1, source_target_pairs={{0,4},{4,0},{8,12},{12,8},{16,20},{20,16},{24,28},{28,24},{32,36},... | collective-permute-start | bytes 786440 | tf_op jit(solution)/shard_map/ppermute | solution.py:550
  52.0 12.6 %copy-start.8 = (f32[128]{0:T(128)S(1)}, f32[128]{0:T(128)}, u32[]{:S(2)}) copy-start(f32[128]{0:T(128)} %param.30) | copy-start | bytes 1540
  52.0 11.1 %collective-permute-start.4 = (bf16[2,4,128,128]{3,2,1,0:T(8,128)(2,1)S(1)}, bf16[2,4,128,128]{3,2,1,0:T(8,128)(2,1)S(1)}, u32[]{:S(2)}, u32[]{:S(2)}) collective-permute-start(bf16[2,4,128,128]{3,2,1,0:T(8,128)(2,1)S(1)} %chip.1.chip_ref), channel_id=1, source_target_pairs={{0,8},{4,12},{8,16},{12,20},{16,24},{20,28},{24,32},{28,36},{32,40... | collective-permute-start | bytes 786440 | tf_op jit(solution)/shard_map/ppermute | solution.py:545
  63.3 11.4 %collective-permute-start.5 = (bf16[2,4,128,128]{3,2,1,0:T(8,128)(2,1)S(1)}, bf16[2,4,128,128]{3,2,1,0:T(8,128)(2,1)S(1)}, u32[]{:S(2)}, u32[]{:S(2)}) collective-permute-start(bf16[2,4,128,128]{3,2,1,0:T(8,128)(2,1)S(1)} %get-tuple-element.77), channel_id=1, source_target_pairs={{0,8},{4,12},{8,16},{12,20},{16,24},{20,28},{24,32},{28,36},{32,40... | collective-permute-start | bytes 786440 | tf_op jit(solution)/shard_map/ppermute | solution.py:545
  63.4 6.3 %collective-permute-start.6 = (bf16[4,128,128]{2,1,0:T(8,128)(2,1)S(1)}, bf16[4,128,128]{2,1,0:T(8,128)(2,1)S(1)}, u32[]{:S(2)}, u32[]{:S(2)}) collective-permute-start(bf16[4,128,128]{2,1,0:T(8,128)(2,1)S(1)} %get-tuple-element.80), channel_id=1, source_target_pairs={{0,24},{4,28},{8,32},{12,36},{16,40},{20,44},{24,48},{28,52},{32,5... | collective-permute-start | bytes 393224 | tf_op jit(solution)/shard_map/ppermute | solution.py:545
  75.0 3.5 %collective-permute-start.7 = (bf16[4,128,128]{2,1,0:T(8,128)(2,1)S(1)}, bf16[4,128,128]{2,1,0:T(8,128)(2,1)S(1)}, u32[]{:S(2)}, u32[]{:S(2)}) collective-permute-start(bf16[4,128,128]{2,1,0:T(8,128)(2,1)S(1)} %get-tuple-element.84), channel_id=1, source_target_pairs={{0,4},{4,0},{8,12},{12,8},{16,20},{20,16},{24,28},{28,24},{32,36},... | collective-permute-start | bytes 393224 | tf_op jit(solution)/shard_map/ppermute | solution.py:550
  80.2 9.2 %collective-permute-start.8 = (bf16[256,512]{1,0:T(8,128)(2,1)S(1)}, bf16[256,512]{1,0:T(8,128)(2,1)S(1)}, u32[]{:S(2)}, u32[]{:S(2)}) collective-permute-start(bf16[256,512]{1,0:T(8,128)(2,1)S(1)} %get-tuple-element.88), channel_id=1, source_target_pairs={{0,2},{1,3},{2,0},{3,1},{4,6},{5,7},{6,4},{7,5},{8,10},{9,11},{10,... | collective-permute-start | bytes 786440 | tf_op jit(solution)/shard_map/ppermute | solution.py:545
  82.8 12.8 %collective-permute-start.9 = (bf16[256,512]{1,0:T(8,128)(2,1)S(1)}, bf16[256,512]{1,0:T(8,128)(2,1)S(1)}, u32[]{:S(2)}, u32[]{:S(2)}) collective-permute-start(bf16[256,512]{1,0:T(8,128)(2,1)S(1)} %get-tuple-element.89), channel_id=1, source_target_pairs={{0,1},{1,2},{2,3},{3,0},{4,5},{5,6},{6,7},{7,4},{8,9},{9,10},{10,1... | collective-permute-start | bytes 786440 | tf_op jit(solution)/shard_map/ppermute | solution.py:545
  83.2 12.4 %collective-permute-start.10 = (bf16[256,512]{1,0:T(8,128)(2,1)S(1)}, bf16[256,512]{1,0:T(8,128)(2,1)S(1)}, u32[]{:S(2)}, u32[]{:S(2)}) collective-permute-start(bf16[256,512]{1,0:T(8,128)(2,1)S(1)} %get-tuple-element.90), channel_id=1, source_target_pairs={{0,3},{1,0},{2,1},{3,2},{4,7},{5,4},{6,5},{7,6},{8,11},{9,8},{10,9... | collective-permute-start | bytes 786440 | tf_op jit(solution)/shard_map/ppermute | solution.py:545

commit v6 on v5

--- a/solution.py
+++ b/solution.py
@@ -17,16 +17,15 @@
 ANY = pl.BlockSpec(memory_space=pl.ANY)
 F32 = jnp.float32
 BF16 = jnp.bfloat16
-HIGHEST = lax.Precision.HIGHEST
 
 
 def iota(shape, axis):
     return lax.broadcasted_iota(jnp.int32, shape, axis)
 
 
-def dot(left, right, contract=((1,), (0,)), precision=None):
+def dot(left, right, contract=((1,), (0,))):
     return lax.dot_general(
-        left, right, (contract, ((), ())), precision=precision, preferred_element_type=F32
+        left, right, (contract, ((), ())), preferred_element_type=F32
     )
 
 
@@ -34,7 +33,7 @@
     return pltpu.CompilerParams(vmem_limit_bytes=mib << 20)
 
 
-def pack_kernel(shards, order_ref, tokens_ref, send_ref, part_ref, sem):
+def pack_kernel(shards, order_ref, tokens_ref, send_ref, part_ref, filled_ref, sem, sems):
     rows, width = part_ref.shape
     slots = send_ref.shape[0]
     capacity = slots // shards
@@ -63,10 +62,17 @@
     halo = jnp.where(halo >= 0, later + halo * pieces, -pieces)
     halos = [chosen(halo + piece) for piece in range(pieces)]
     copy.wait()
-    send_ref[:, :width] = dot(hit, part_ref[...]).astype(BF16)
     for piece in range(pieces):
         extra = extra + dot(halos[piece], part_ref[:, piece * LANES : (piece + 1) * LANES])
-    send_ref[:, width:] = extra.astype(BF16)
+    filled_ref[:, width:] = extra.astype(BF16)
+    block = slots // FETCHES
+    copies = in_parts(filled_ref, send_ref, sems, 0)
+    for i, copy in enumerate(copies):
+        at = slice(i * block, (i + 1) * block)
+        filled_ref[at, :width] = dot(hit[at], part_ref[...]).astype(BF16)
+        copy.start()
+    for copy in copies:
+        copy.wait()
 
 
 def place_kernel(shards, got_ref, part_ref):
@@ -206,16 +212,23 @@
     same = [
         (segments(position - lag, ends) == segment).astype(F32) for lag in range(1, KERNEL)
     ]
-    inside = segment == segments(first + iota((1, rows), 1), ends)
+    segment_row = segments(first + iota((1, rows), 1), ends)
+    inside = segment == segment_row
     before = segments(jnp.full((1, 1), first - 1, jnp.int32), ends)
     carries = (segment == before).astype(F32)
-    return segment, same, inside, carries
+    return segment_row, same, inside, carries
 
 
 def cumulated(decay):
     rows, heads = decay.shape
-    lower = (iota((rows, rows), 0) >= iota((rows, rows), 1)).astype(F32)
-    down = dot(lower, decay, precision=HIGHEST)
+    lower = (iota((rows, rows), 0) >= iota((rows, rows), 1)).astype(F32).astype(BF16)
+    high = decay.astype(BF16)
+    rest = decay - high.astype(F32)
+    middle = rest.astype(BF16)
+    low = (rest - middle.astype(F32)).astype(BF16)
+    thirds = [part.astype(F32) for part in (high, middle, low)]
+    sums = dot(lower, jnp.concatenate(thirds, axis=1).astype(BF16))
+    down = sums[:, :heads] + (sums[:, heads : 2 * heads] + sums[:, 2 * heads :])
     padded = jnp.concatenate([down, jnp.zeros((rows, LANES - heads), F32)], axis=1)
     return down, padded.T
 
@@ -266,6 +279,8 @@
     mask_ref,
     states_ref,
     right_ref,
+    part_ref,
+    last_ref,
 ):
     rows, heads = beta_sum.shape
     width = part1_ref.shape[1]
@@ -289,7 +304,7 @@
     first, core = lax.axis_index("seq") * rows, my_core()
     key_heads = key_ref.shape[1] // HEAD
     repeat = heads // key_heads
-    segment, same, inside, carries = masks(first, document_ends(lengths_ref), rows)
+    segment_row, same, inside, carries = masks(first, document_ends(lengths_ref), rows)
     row, column = iota((rows, rows), 0), iota((rows, rows), 1)
     small = rows // PACKED
     levels = small.bit_length() - 1
@@ -314,9 +329,9 @@
 
     for kh in range(key_heads):
         at = column_of(kh)
-        keys[kh] = unit(
-            convolve(key_ref[:, at], taps_key[:, at], same), 1.0
-        ).astype(BF16)
+        key = unit(convolve(key_ref[:, at], taps_key[:, at], same), 1.0)
+        keys[kh] = key.astype(BF16)
+    for kh in range(key_heads):
         inner = dot(keys[kh], keys[kh], ((1,), (1,)))
         for h in range(kh * repeat, (kh + 1) * repeat):
             system = beta_all[:, h : h + 1] * inner * between(down, across, h, strict)
@@ -328,21 +343,38 @@
             packed = term if packed is None else packed + term
         packed_ref[h] = packed
         inverse_ref[h] = diagonal - packed * mask_ref[0]
+
+    def fill_right(some):
+        for h in some:
+            at = column_of(h)
+            beta = beta_all[:, h : h + 1]
+            carried = jnp.exp(down[:, h : h + 1]) * carries
+            value = convolve(value_ref[:, at], taps_value[:, at], same)
+            right_ref[h, :, :HEAD] = (beta * value).astype(BF16)
+            right_ref[h, :, HEAD:] = (beta * carried * keys[h // repeat].astype(F32)).astype(BF16)
+
+    def fill_last():
+        for kh in range(key_heads):
+            key = keys[kh].astype(F32).T
+            for h in range(kh * repeat, (kh + 1) * repeat):
+                gain = across[h : h + 1, :]
+                last = jnp.where(segment_row == segment_row[:, rows - 1 :], 1.0, 0.0)
+                last = jnp.exp(gain[:, rows - 1 :] - gain) * last
+                last_ref[h] = (key * last).astype(BF16)
+
+    work = {}
+    for level, filler in enumerate(fillers):
+        work.setdefault(min(level + 1, levels - 1), []).append(lambda filler=filler: project(*filler))
     for level in range(1, levels):
-        if fillers:
-            project(*fillers.pop(0))
+        for step in work.get(level, []):
+            step()
         for h in range(heads):
             inverse = inverse_ref[h]
             part = dot(packed_ref[h] * mask_ref[level], spread(inverse)).astype(BF16)
             inverse_ref[h] = inverse - dot(inverse, spread(part)).astype(BF16)
-    for h in range(heads):
-        at = column_of(h)
-        beta = beta_all[:, h : h + 1]
-        carried = jnp.exp(down[:, h : h + 1]) * carries
-        value = convolve(value_ref[:, at], taps_value[:, at], same)
-        right_ref[h, :, :HEAD] = (beta * value).astype(BF16)
-        right_ref[h, :, HEAD:] = (beta * carried * keys[h // repeat].astype(F32)).astype(BF16)
     zero = jnp.zeros((small, rows), BF16)
+    fill_right(range(heads))
+    fill_last()
     for h in range(heads):
         inverse = inverse_ref[h]
         spread_inverse = spread(inverse)
@@ -358,7 +390,6 @@
 
     square = (iota((HEAD, HEAD), 0) == iota((HEAD, HEAD), 1)).astype(F32)
     half, middle = heads // 2, rows // 2
-    last_same = (segment == segment[rows - 1 : rows, :]).astype(F32)
     for h in range(heads):
         solved_ref[h, :middle] = dot(
             whole_ref[h, :middle, :middle], right_ref[h, :middle]
@@ -367,14 +398,14 @@
         rest = right_ref[h, middle:].astype(F32) - dot(
             system_ref[h, middle:, :middle], solved_ref[h, :middle]
         )
-        solved_ref[h, middle:] = dot(whole_ref[h, middle:, middle:], rest.astype(BF16)).astype(
-            BF16
-        )
+        right_ref[h, middle:] = rest.astype(BF16)
     for h in range(heads):
-        gain = down[:, h : h + 1]
-        last = jnp.exp(gain[rows - 1 : rows, :] - gain) * last_same
-        ended = dot((last * keys[h // repeat].astype(F32)).astype(BF16), solved_ref[h], ((0,), (0,)))
-        carried = (jnp.exp(gain) * carries)[rows - 1 : rows, :]
+        solved_ref[h, middle:] = dot(
+            whole_ref[h, middle:, middle:], right_ref[h, middle:]
+        ).astype(BF16)
+    for h in range(heads):
+        ended = dot(last_ref[h], solved_ref[h])
+        carried = (jnp.exp(down[:, h : h + 1]) * carries)[rows - 1 : rows, :]
         states_ref[0, h] = (carried * square - ended[:, HEAD:]).astype(BF16)
         states_ref[1, h] = ended[:, :HEAD].astype(BF16)
 
@@ -401,6 +432,8 @@
         pltpu.VMEM((small.bit_length() - 1, small, rows), BF16),
         pltpu.VMEM((2, heads, HEAD, HEAD), BF16),
         pltpu.VMEM((heads, rows, 2 * HEAD), BF16),
+        pltpu.VMEM((heads, small, rows), BF16),
+        pltpu.VMEM((heads, HEAD, rows), BF16),
     ]
 
 
@@ -417,7 +450,7 @@
     rows, heads = decay_ref.shape
     key_heads = query_ref.shape[1] // HEAD
     repeat = heads // key_heads
-    segment, same, inside, carries = masks(
+    _, same, inside, carries = masks(
         lax.axis_index("seq") * rows, document_ends(lengths_ref), rows
     )
     inside = inside & (iota((rows, rows), 0) >= iota((rows, rows), 1))
@@ -611,8 +644,14 @@
         pltpu.HBM((slots, part + LANES), BF16),
         (hbm(order.reshape(1, rows)), hbm(tokens)),
         8,
-        scratch=[pltpu.VMEM((rows, part), BF16), pltpu.SemaphoreType.DMA],
+        scratch=[
+            pltpu.VMEM((rows, part), BF16),
+            pltpu.VMEM((slots, part + LANES), BF16),
+            pltpu.SemaphoreType.DMA,
+            pltpu.SemaphoreType.DMA((FETCHES,)),
+        ],
         inputs=[VMEM, ANY],
+        specs=(ANY,),
     )
     got = lax.all_to_all(
         send.reshape(shards, capacity, part + LANES), "seq", split_axis=0, concat_axis=0, tiled=True
@@ -735,7 +774,7 @@
         scratch=[pltpu.VMEM((rows, vw), BF16), pltpu.VMEM((heads, HEAD, HEAD), BF16)],
     )
     mixed = terms[0].astype(F32)
-    for steps in (2, 1, 3):
+    for steps in (1, 3, 2):
         mixed = mixed + turned(terms[steps], "head", steps).astype(F32)
     return mixed.astype(BF16)
 

time: 96.7 us -> 96.5 us (level)
  starting transfers between devices: 15.3 us -> 14.1 us
    ppermute x9, starting transfers between devices: 11.8 us -> 10.6 us  [turned(): lax.ppermute(value, axis, [(at, (at + steps) % count) for at in range(cou...]
where the time goes in v6:
time: 96.5 us; the launch traced here: 96.3 us
  waiting for transfers between devices  32.5 us (34%)
  Pallas kernels  26.3 us (27%)
  blocking collectives  22.4 us (23%)
  starting transfers between devices  14.1 us (15%)
    ppermute x9, waiting for transfers between devices, turned(): lax.ppermute(value, axis, [(at, (at + steps) % count) for at in range(cou...  30.3 us
    pallas_call x12, Pallas kernels, call(): pl.pallas_call(kernel, out_shape=outs, in_specs=[VMEM] * len(ins) if inpu...  26.3 us
    all_to_all x1, blocking collectives, local(): lax.all_to_all(send.reshape(shards, capacity, part + LANES), 'seq', split...  22.4 us
    ppermute x9, starting transfers between devices, turned(): lax.ppermute(value, axis, [(at, (at + steps) % count) for at in range(cou...  10.6 us
    ppermute x2, starting transfers between devices, swapped(): return lax.ppermute(value, axis, [(at, at ^ 1) for at in range(count)])  3.46 us
    ppermute x2, waiting for transfers between devices, swapped(): return lax.ppermute(value, axis, [(at, at ^ 1) for at in range(count)])  2.15 us
  transfers between devices with their start and end apart: 11, of which 10 were waited for; matrix products, arithmetic and copies ran while one was open for 0% of the time, Pallas kernels for 13%

profile of v6, /device:TPU:1, one launch (start us, length us, event | category | flops | bytes accessed | tf_op | source)
XLA Modules:
  0.0 96.3 jit_solution(13349144731561431881)
XLA Ops:
  0.0 3.2 %pack.1 = bf16[512,640]{1,0:T(8,128)(2,1)} custom-call(s32[1,256]{1,0:T(1,128)} %bitcast.17, bf16[256,2048]{1,0:T(8,128)(2,1)} %refs_1_.1), custom_call_target="tpu_custom_call" | custom-call | bytes 2000000 | tf_op jit(solution)/shard_map/pack/pallas_call | solution.py:601
  3.2 22.4 %all_to_all.5 = bf16[32,16,640]{2,1,0:T(8,128)(2,1)S(1)} all-to-all(bf16[32,16,640]{2,1,0:T(8,128)(2,1)} %bitcast.16), channel_id=1, replica_groups=mesh['seq'=32,'head'=4] {'seq'}, dimensions={0} | all-to-all | bytes 1310720 | tf_op jit(solution)/shard_map/all_to_all | solution.py:656
  26.2 3.0 %collective-permute-start = (bf16[272,512]{1,0:T(8,128)(2,1)S(1)}, bf16[272,512]{1,0:T(8,128)(2,1)S(1)}, u32[]{:S(2)}, u32[]{:S(2)}) collective-permute-start(bf16[272,512]{1,0:T(8,128)(2,1)S(1)} %place.1.part0_ref), channel_id=1, source_target_pairs={{0,2},{1,3},{2,0},{3,1},{4,6},{5,7},{6,4},{7,5},{8,10},{9,11},{10,... | collective-permute-start | bytes 835592 | tf_op jit(solution)/shard_map/ppermute | solution.py:578
  30.6 4.7 %fetch.1 = (bf16[2048,512]{1,0:T(8,128)(2,1)S(1)}, bf16[2048,512]{1,0:T(8,128)(2,1)S(1)}, bf16[2048,1024]{1,0:T(8,128)(2,1)S(1)}, bf16[2048,1024]{1,0:T(8,128)(2,1)S(1)}) custom-call(bf16[2048,512]{1,0:T(8,128)(2,1)} %refs_0_, bf16[2048,512]{1,0:T(8,128)(2,1)} %refs_1_.2, bf16[2048,1024]{1,0:T(8,128)(2,1)} %refs_2_, bf16[2048,1024]{1,0:T(8,128)(2,1)} %refs_3_), custom_call_target="tpu_custom_call" | custom-call | bytes 20000000 | tf_op jit(solution)/shard_map/fetch/pallas_call | solution.py:601
  35.5 1.6 %project.1 = (f32[272,512]{1,0:T(8,128)S(1)}, f32[272,512]{1,0:T(8,128)S(1)}, f32[272,1024]{1,0:T(8,128)S(1)}, f32[256,8]{1,0:T(8,128)S(1)}, f32[256,8]{1,0:T(8,128)S(1)}) custom-call(bf16[272,512]{1,0:T(8,128)(2,1)S(1)} %place.1.part0_ref, bf16[272,512]{1,0:T(8,128)(2,1)S(1)} %collective-permute-done.part2_ref, ...), custom_call_target="tpu_custom_call" | custom-call | bytes 10000000 | tf_op jit(solution)/shard_map/project/pallas_call | solution.py:601
  37.1 4.7 %collective-permute-done.2.part3_ref = bf16[272,512]{1,0:T(8,128)(2,1)S(1)} collective-permute-done((bf16[272,512]{1,0:T(8,128)(2,1)S(1)}, bf16[272,512]{1,0:T(8,128)(2,1)S(1)}, u32[]{:S(2)}, u32[]{:S(2)}) %collective-permute-start.2) | collective-permute-done | bytes 278560 | tf_op jit(solution)/shard_map/ppermute | solution.py:578
  42.3 7.3 %chunk.1 = (bf16[2,4,128,128]{3,2,1,0:T(8,128)(2,1)S(1)}, bf16[2,4,128,128]{3,2,1,0:T(8,128)(2,1)S(1)}, bf16[4,256,128]{2,1,0:T(8,128)(2,1)S(1)}, bf16[8,256,256...) custom-call(s32[8]{0:T(128)S(1)} %copy-done.5, ...), custom_call_target="tpu_custom_call" | custom-call | bytes 2000000 | tf_op jit(solution)/shard_map/chunk/pallas_call | solution.py:601
  49.6 0.9 collective-permute-start.3
  50.6 1.2 %collective-permute-done.3.other_ref = bf16[2,4,128,128]{3,2,1,0:T(8,128)(2,1)S(1)} collective-permute-done((bf16[2,4,128,128]{3,2,1,0:T(8,128)(2,1)S(1)}, bf16[2,4,128,128]{3,2,1,0:T(8,128)(2,1)S(1)}, u32[]{:S(2)}, u32[]{:S(2)}) %collective-permute-start.3) | collective-permute-done | bytes 262176 | tf_op jit(solution)/shard_map/ppermute | solution.py:583
  52.8 3.0 %respond.1 = (f32[256,1024]{1,0:T(8,128)S(1)}, bf16[256,1024]{1,0:T(8,128)(2,1)S(1)}) custom-call(s32[8]{0:T(128)S(1)} %copy-done.5, bf16[272,512]{1,0:T(8,128)(2,1)S(1)} %get-tuple-element.66.query_ref, bf16[4,512]{1,0:T(4,128)(2,1)S(1)} %copy-done.4, f32[256,8]{1,0:T(8,128)S(1)} %get-tuple-element.67.decay_ref, ...), custom_call_target="tpu_custom_call" | custom-call | bytes 16000000 | tf_op jit(solution)/shard_map/respond/pallas_call | solution.py:601
  55.8 1.3 %project_gate.1.zgate_ref = bf16[256,1024]{1,0:T(8,128)(2,1)S(1)} custom-call(bf16[272,512]{1,0:T(8,128)(2,1)S(1)} %place.1.part0_ref, bf16[272,512]{1,0:T(8,128)(2,1)S(1)} %collective-permute-done.1.part1_ref, bf16[272,512]{1,0:T(8,128)(2,1)S(1)} %collective-permute-done.part2_ref, bf16[272,512]{1,0:T(8,128)(2,1)S(1)} %collective-permute-done.2.part3_ref, ...), custom_call_target="tpu_custom_call" | custom-call | bytes 6000000 | tf_op jit(solution)/shard_map/project_gate/pallas_call | solution.py:601
  57.1 6.0 %collective-permute-done.4.before_ref = bf16[2,4,128,128]{3,2,1,0:T(8,128)(2,1)S(1)} collective-permute-done((bf16[2,4,128,128]{3,2,1,0:T(8,128)(2,1)S(1)}, bf16[2,4,128,128]{3,2,1,0:T(8,128)(2,1)S(1)}, u32[]{:S(2)}, u32[]{:S(2)}) %collective-permute-start.4) | collective-permute-done | bytes 262176 | tf_op jit(solution)/shard_map/ppermute | solution.py:578
  63.4 1.2 %collective-permute-start.6 = (bf16[4,128,128]{2,1,0:T(8,128)(2,1)S(1)}, bf16[4,128,128]{2,1,0:T(8,128)(2,1)S(1)}, u32[]{:S(2)}, u32[]{:S(2)}) collective-permute-start(bf16[4,128,128]{2,1,0:T(8,128)(2,1)S(1)} %get-tuple-element.80), channel_id=1, source_target_pairs={{0,24},{4,28},{8,32},{12,36},{16,40},{20,44},{24,48},{28,52},{32,5... | collective-permute-start | bytes 393224 | tf_op jit(solution)/shard_map/ppermute | solution.py:578
  64.6 2.2 %gate.1 = (f32[256,1024]{1,0:T(8,128)S(1)}, bf16[1024,2048]{1,0:T(8,128)(2,1)S(1)}) custom-call(bf16[256,1024]{1,0:T(8,128)(2,1)S(1)} %project_gate.1.zgate_ref, f32[1,128]{1,0:T(1,128)S(1)} %bitcast.15, bf16[1024,2048]{1,0:T(8,128)(2,1)} %w_out.1), custom_call_target="tpu_custom_call" | custom-call | bytes 10000000 | tf_op jit(solution)/shard_map/gate/pallas_call | solution.py:601
  66.8 2.8 %collective-permute-done.6.far_ref = bf16[4,128,128]{2,1,0:T(8,128)(2,1)S(1)} collective-permute-done((bf16[4,128,128]{2,1,0:T(8,128)(2,1)S(1)}, bf16[4,128,128]{2,1,0:T(8,128)(2,1)S(1)}, u32[]{:S(2)}, u32[]{:S(2)}) %collective-permute-start.6) | collective-permute-done | bytes 131104 | tf_op jit(solution)/shard_map/ppermute | solution.py:578
  69.6 5.0 %collective-permute-done.5.near_ref = bf16[2,4,128,128]{3,2,1,0:T(8,128)(2,1)S(1)} collective-permute-done((bf16[2,4,128,128]{3,2,1,0:T(8,128)(2,1)S(1)}, bf16[2,4,128,128]{3,2,1,0:T(8,128)(2,1)S(1)}, u32[]{:S(2)}, u32[]{:S(2)}) %collective-permute-start.5) | collective-permute-done | bytes 262176 | tf_op jit(solution)/shard_map/ppermute | solution.py:578
  75.0 2.5 %collective-permute-start.7 = (bf16[4,128,128]{2,1,0:T(8,128)(2,1)S(1)}, bf16[4,128,128]{2,1,0:T(8,128)(2,1)S(1)}, u32[]{:S(2)}, u32[]{:S(2)}) collective-permute-start(bf16[4,128,128]{2,1,0:T(8,128)(2,1)S(1)} %get-tuple-element.84), channel_id=1, source_target_pairs={{0,4},{4,0},{8,12},{12,8},{16,20},{20,16},{24,28},{28,24},{32,36},... | collective-permute-start | bytes 393224 | tf_op jit(solution)/shard_map/ppermute | solution.py:583
  77.5 1.0 %collective-permute-done.7.other_ref = bf16[4,128,128]{2,1,0:T(8,128)(2,1)S(1)} collective-permute-done((bf16[4,128,128]{2,1,0:T(8,128)(2,1)S(1)}, bf16[4,128,128]{2,1,0:T(8,128)(2,1)S(1)}, u32[]{:S(2)}, u32[]{:S(2)}) %collective-permute-start.7) | collective-permute-done | bytes 131104 | tf_op jit(solution)/shard_map/ppermute | solution.py:583
  78.5 1.6 %finish.1 = (bf16[256,512]{1,0:T(8,128)(2,1)S(1)}, bf16[256,512]{1,0:T(8,128)(2,1)S(1)}, bf16[256,512]{1,0:T(8,128)(2,1)S(1)}, bf16[256,512]{1,0:T(8,128)(2,1)S(1)}) custom-call(f32[256,1024]{1,0:T(8,128)S(1)} %get-tuple-element.73.base_ref, bf16[256,1024]{1,0:T(8,128)(2,1)S(1)} %get-tuple-element.74.response_ref, ...), custom_call_target="tpu_custom_call" | custom-call | bytes 2000000 | tf_op jit(solution)/shard_map/finish/pallas_call | solution.py:601
  80.1 1.1 %collective-permute-start.8 = (bf16[256,512]{1,0:T(8,128)(2,1)S(1)}, bf16[256,512]{1,0:T(8,128)(2,1)S(1)}, u32[]{:S(2)}, u32[]{:S(2)}) collective-permute-start(bf16[256,512]{1,0:T(8,128)(2,1)S(1)} %get-tuple-element.88), channel_id=1, source_target_pairs={{0,1},{1,2},{2,3},{3,0},{4,5},{5,6},{6,7},{7,4},{8,9},{9,10},{10,1... | collective-permute-start | bytes 786440 | tf_op jit(solution)/shard_map/ppermute | solution.py:578
  81.3 1.6 %collective-permute-start.9 = (bf16[256,512]{1,0:T(8,128)(2,1)S(1)}, bf16[256,512]{1,0:T(8,128)(2,1)S(1)}, u32[]{:S(2)}, u32[]{:S(2)}) collective-permute-start(bf16[256,512]{1,0:T(8,128)(2,1)S(1)} %get-tuple-element.89), channel_id=1, source_target_pairs={{0,3},{1,0},{2,1},{3,2},{4,7},{5,4},{6,5},{7,6},{8,11},{9,8},{10,9... | collective-permute-start | bytes 786440 | tf_op jit(solution)/shard_map/ppermute | solution.py:578
  82.9 1.3 %collective-permute-start.10 = (bf16[256,512]{1,0:T(8,128)(2,1)S(1)}, bf16[256,512]{1,0:T(8,128)(2,1)S(1)}, u32[]{:S(2)}, u32[]{:S(2)}) collective-permute-start(bf16[256,512]{1,0:T(8,128)(2,1)S(1)} %get-tuple-element.90), channel_id=1, source_target_pairs={{0,2},{1,3},{2,0},{3,1},{4,6},{5,7},{6,4},{7,5},{8,10},{9,11},{10,... | collective-permute-start | bytes 786440 | tf_op jit(solution)/shard_map/ppermute | solution.py:578
  84.2 4.8 %collective-permute-done.8 = bf16[256,512]{1,0:T(8,128)(2,1)S(1)} collective-permute-done((bf16[256,512]{1,0:T(8,128)(2,1)S(1)}, bf16[256,512]{1,0:T(8,128)(2,1)S(1)}, u32[]{:S(2)}, u32[]{:S(2)}) %collective-permute-start.8) | collective-permute-done | bytes 262176 | tf_op jit(solution)/shard_map/ppermute | solution.py:578
  89.0 6.5 %collective-permute-done.10 = bf16[256,512]{1,0:T(8,128)(2,1)S(1)} collective-permute-done((bf16[256,512]{1,0:T(8,128)(2,1)S(1)}, bf16[256,512]{1,0:T(8,128)(2,1)S(1)}, u32[]{:S(2)}, u32[]{:S(2)}) %collective-permute-start.10) | collective-permute-done | bytes 262176 | tf_op jit(solution)/shard_map/ppermute | solution.py:578
  (30 shorter events, 5.2 us)
Async XLA Ops:
  26.1 9.3 %copy-start = (bf16[2048,8]{0,1:T(8,128)(2,1)S(1)}, bf16[2048,8]{0,1:T(8,128)(2,1)}, u32[]{:S(2)}) copy-start(bf16[2048,8]{0,1:T(8,128)(2,1)} %param.23) | copy-start | bytes 98308
  26.1 9.3 %copy-start.1 = (bf16[2048,8]{0,1:T(8,128)(2,1)S(1)}, bf16[2048,8]{0,1:T(8,128)(2,1)}, u32[]{:S(2)}) copy-start(bf16[2048,8]{0,1:T(8,128)(2,1)} %param.24) | copy-start | bytes 98308
  26.2 9.3 %collective-permute-start = (bf16[272,512]{1,0:T(8,128)(2,1)S(1)}, bf16[272,512]{1,0:T(8,128)(2,1)S(1)}, u32[]{:S(2)}, u32[]{:S(2)}) collective-permute-start(bf16[272,512]{1,0:T(8,128)(2,1)S(1)} %place.1.part0_ref), channel_id=1, source_target_pairs={{0,2},{1,3},{2,0},{3,1},{4,6},{5,7},{6,4},{7,5},{8,10},{9,11},{10,... | collective-permute-start | bytes 835592 | tf_op jit(solution)/shard_map/ppermute | solution.py:578
  29.1 12.6 %collective-permute-start.2 = (bf16[272,512]{1,0:T(8,128)(2,1)S(1)}, bf16[272,512]{1,0:T(8,128)(2,1)S(1)}, u32[]{:S(2)}, u32[]{:S(2)}) collective-permute-start(bf16[272,512]{1,0:T(8,128)(2,1)S(1)} %place.1.part0_ref), channel_id=1, source_target_pairs={{0,3},{1,0},{2,1},{3,2},{4,7},{5,4},{6,5},{7,6},{8,11},{9,8},{10,9... | collective-permute-start | bytes 835592 | tf_op jit(solution)/shard_map/ppermute | solution.py:578
  29.9 12.4 %collective-permute-start.1 = (bf16[272,512]{1,0:T(8,128)(2,1)S(1)}, bf16[272,512]{1,0:T(8,128)(2,1)S(1)}, u32[]{:S(2)}, u32[]{:S(2)}) collective-permute-start(bf16[272,512]{1,0:T(8,128)(2,1)S(1)} %place.1.part0_ref), channel_id=1, source_target_pairs={{0,1},{1,2},{2,3},{3,0},{4,5},{5,6},{6,7},{7,4},{8,9},{9,10},{10,1... | collective-permute-start | bytes 835592 | tf_op jit(solution)/shard_map/ppermute | solution.py:578
  35.4 6.8 %copy-start.2 = (bf16[4,1024]{1,0:T(4,128)(2,1)S(1)}, bf16[4,1024]{1,0:T(4,128)(2,1)}, u32[]{:S(2)}) copy-start(bf16[4,1024]{1,0:T(4,128)(2,1)} %taps_value.1) | copy-start | bytes 24580
  35.4 6.8 %copy-start.3 = (bf16[4,512]{1,0:T(4,128)(2,1)S(1)}, bf16[4,512]{1,0:T(4,128)(2,1)}, u32[]{:S(2)}) copy-start(bf16[4,512]{1,0:T(4,128)(2,1)} %taps_key.1) | copy-start | bytes 12292
  35.5 6.8 %copy-start.5 = (s32[8]{0:T(128)S(1)}, s32[8]{0:T(128)}, u32[]{:S(2)}) copy-start(s32[8]{0:T(128)} %lengths_ref.3) | copy-start | bytes 100
  35.5 6.8 %copy-start.6 = (f32[8]{0:T(128)S(1)}, f32[8]{0:T(128)}, u32[]{:S(2)}) copy-start(f32[8]{0:T(128)} %param.28) | copy-start | bytes 100
  35.5 6.8 %copy-start.7 = (f32[8]{0:T(128)S(1)}, f32[8]{0:T(128)}, u32[]{:S(2)}) copy-start(f32[8]{0:T(128)} %param.29) | copy-start | bytes 100
  42.3 10.5 %copy-start.4 = (bf16[4,512]{1,0:T(4,128)(2,1)S(1)}, bf16[4,512]{1,0:T(4,128)(2,1)}, u32[]{:S(2)}) copy-start(bf16[4,512]{1,0:T(4,128)(2,1)} %taps_query.1) | copy-start | bytes 12292
  49.6 2.1 %collective-permute-start.3 = (bf16[2,4,128,128]{3,2,1,0:T(8,128)(2,1)S(1)}, bf16[2,4,128,128]{3,2,1,0:T(8,128)(2,1)S(1)}, u32[]{:S(2)}, u32[]{:S(2)}) collective-permute-start(bf16[2,4,128,128]{3,2,1,0:T(8,128)(2,1)S(1)} %get-tuple-element.65), channel_id=1, source_target_pairs={{0,4},{4,0},{8,12},{12,8},{16,20},{20,16},{24,28},{28,24},{32,36},... | collective-permute-start | bytes 786440 | tf_op jit(solution)/shard_map/ppermute | solution.py:583
  52.0 12.6 %copy-start.8 = (f32[128]{0:T(128)S(1)}, f32[128]{0:T(128)}, u32[]{:S(2)}) copy-start(f32[128]{0:T(128)} %param.30) | copy-start | bytes 1540
  52.0 11.1 %collective-permute-start.4 = (bf16[2,4,128,128]{3,2,1,0:T(8,128)(2,1)S(1)}, bf16[2,4,128,128]{3,2,1,0:T(8,128)(2,1)S(1)}, u32[]{:S(2)}, u32[]{:S(2)}) collective-permute-start(bf16[2,4,128,128]{3,2,1,0:T(8,128)(2,1)S(1)} %chip.1.chip_ref), channel_id=1, source_target_pairs={{0,8},{4,12},{8,16},{12,20},{16,24},{20,28},{24,32},{28,36},{32,40... | collective-permute-start | bytes 786440 | tf_op jit(solution)/shard_map/ppermute | solution.py:578
  63.3 11.4 %collective-permute-start.5 = (bf16[2,4,128,128]{3,2,1,0:T(8,128)(2,1)S(1)}, bf16[2,4,128,128]{3,2,1,0:T(8,128)(2,1)S(1)}, u32[]{:S(2)}, u32[]{:S(2)}) collective-permute-start(bf16[2,4,128,128]{3,2,1,0:T(8,128)(2,1)S(1)} %get-tuple-element.77), channel_id=1, source_target_pairs={{0,8},{4,12},{8,16},{12,20},{16,24},{20,28},{24,32},{28,36},{32,40... | collective-permute-start | bytes 786440 | tf_op jit(solution)/shard_map/ppermute | solution.py:578
  63.4 6.3 %collective-permute-start.6 = (bf16[4,128,128]{2,1,0:T(8,128)(2,1)S(1)}, bf16[4,128,128]{2,1,0:T(8,128)(2,1)S(1)}, u32[]{:S(2)}, u32[]{:S(2)}) collective-permute-start(bf16[4,128,128]{2,1,0:T(8,128)(2,1)S(1)} %get-tuple-element.80), channel_id=1, source_target_pairs={{0,24},{4,28},{8,32},{12,36},{16,40},{20,44},{24,48},{28,52},{32,5... | collective-permute-start | bytes 393224 | tf_op jit(solution)/shard_map/ppermute | solution.py:578
  75.0 3.5 %collective-permute-start.7 = (bf16[4,128,128]{2,1,0:T(8,128)(2,1)S(1)}, bf16[4,128,128]{2,1,0:T(8,128)(2,1)S(1)}, u32[]{:S(2)}, u32[]{:S(2)}) collective-permute-start(bf16[4,128,128]{2,1,0:T(8,128)(2,1)S(1)} %get-tuple-element.84), channel_id=1, source_target_pairs={{0,4},{4,0},{8,12},{12,8},{16,20},{20,16},{24,28},{28,24},{32,36},... | collective-permute-start | bytes 393224 | tf_op jit(solution)/shard_map/ppermute | solution.py:583
  80.1 8.8 %collective-permute-start.8 = (bf16[256,512]{1,0:T(8,128)(2,1)S(1)}, bf16[256,512]{1,0:T(8,128)(2,1)S(1)}, u32[]{:S(2)}, u32[]{:S(2)}) collective-permute-start(bf16[256,512]{1,0:T(8,128)(2,1)S(1)} %get-tuple-element.88), channel_id=1, source_target_pairs={{0,1},{1,2},{2,3},{3,0},{4,5},{5,6},{6,7},{7,4},{8,9},{9,10},{10,1... | collective-permute-start | bytes 786440 | tf_op jit(solution)/shard_map/ppermute | solution.py:578
  81.3 7.7 %collective-permute-start.9 = (bf16[256,512]{1,0:T(8,128)(2,1)S(1)}, bf16[256,512]{1,0:T(8,128)(2,1)S(1)}, u32[]{:S(2)}, u32[]{:S(2)}) collective-permute-start(bf16[256,512]{1,0:T(8,128)(2,1)S(1)} %get-tuple-element.89), channel_id=1, source_target_pairs={{0,3},{1,0},{2,1},{3,2},{4,7},{5,4},{6,5},{7,6},{8,11},{9,8},{10,9... | collective-permute-start | bytes 786440 | tf_op jit(solution)/shard_map/ppermute | solution.py:578
  82.9 12.5 %collective-permute-start.10 = (bf16[256,512]{1,0:T(8,128)(2,1)S(1)}, bf16[256,512]{1,0:T(8,128)(2,1)S(1)}, u32[]{:S(2)}, u32[]{:S(2)}) collective-permute-start(bf16[256,512]{1,0:T(8,128)(2,1)S(1)} %get-tuple-element.90), channel_id=1, source_target_pairs={{0,2},{1,3},{2,0},{3,1},{4,6},{5,7},{6,4},{7,5},{8,10},{9,11},{10,... | collective-permute-start | bytes 786440 | tf_op jit(solution)/shard_map/ppermute | solution.py:578
